TPU v7x, 32 devices: a whole 2x2x4 slice. The times are simulated.
32 devices in a mesh: rows: 4 (over y, core), tok: 8 (over z, x).
Axes of the slice: x: 2, y: 2, z: 4, core: 2. Of those that a mesh axis runs over, the one named last changes fastest.
Arguments:
- tokens_in: bfloat16 [28, 512, 64], P('rows', 'tok'), may hold values from -6 to 6
- segments: int32 [28, 512], P('rows', 'tok'), may hold values from 0 to 3, as said below
- landmark_index: int32 [28, 2, 128], P('rows'), may hold values from 0 to 1023
- ln1_gain: bfloat16 [64], replicated, may hold values from 0.5 to 1.5
- ln1_bias: bfloat16 [64], replicated, may hold values from -3 to 3
- w_query: bfloat16 [64, 64], replicated, may hold values from -0.375 to 0.375
- b_query: bfloat16 [64], replicated, may hold values from -1.5 to 1.5
- w_key: bfloat16 [64, 64], replicated, may hold values from -0.375 to 0.375
- b_key: bfloat16 [64], replicated, may hold values from -1.5 to 1.5
- w_value: bfloat16 [64, 64], replicated, may hold values from -0.75 to 0.75
- b_value: bfloat16 [64], replicated, may hold values from -3 to 3
- w_out: bfloat16 [64, 64], replicated, may hold values from -1.5 to 1.5
- b_out: bfloat16 [64], replicated, may hold values from -3 to 3
- ln2_gain: bfloat16 [64], replicated, may hold values from 0.5 to 1.5
- ln2_bias: bfloat16 [64], replicated, may hold values from -3 to 3
- w_up: bfloat16 [64, 128], replicated, may hold values from -0.75 to 0.75
- b_up: bfloat16 [128], replicated, may hold values from -3 to 3
- w_down: bfloat16 [128, 64], replicated, may hold values from -0.5 to 0.5
- b_down: bfloat16 [64], replicated, may hold values from -3 to 3
- grad_out: bfloat16 [28, 512, 64], P('rows', 'tok'), may hold values from -6 to 6
Outputs:
- layer_out: bfloat16 [28, 512, 64], P('rows', 'tok')
- grad_input: float32 [28, 512, 64], P('rows', 'tok')
- grad_ln1_gain: float32 [64], replicated
- grad_ln1_bias: float32 [64], replicated
- grad_w_query: float32 [64, 64], replicated
- grad_b_query: float32 [64], replicated
- grad_w_key: float32 [64, 64], replicated
- grad_b_key: float32 [64], replicated
- grad_w_value: float32 [64, 64], replicated
- grad_b_value: float32 [64], replicated
- grad_w_out: float32 [64, 64], replicated
- grad_b_out: float32 [64], replicated
- grad_ln2_gain: float32 [64], replicated
- grad_ln2_bias: float32 [64], replicated
- grad_w_up: float32 [64, 128], replicated
- grad_b_up: float32 [128], replicated
- grad_w_down: float32 [128, 64], replicated
- grad_b_down: float32 [64], replicated
Inputs may be any that keep to these rules, and one draw needn't show every extreme that they name: Ids never fall along a row and no segment is empty. In one row of each aligned block of 7 rows the ids are 0, 1, 2, segment 1 beginning within the first 64 tokens and ending within the last 64; every other row holds segments 0 to 3, boundary k (k = 1, 2, 3) lying within 64 tokens of k * 128.
All inputs are finite; a program needn't handle non-finite values.
Results may differ from a plain program's by a relative error of at most 0.013.
Values may be sent and summed in bfloat16 or wider, within the bound.
No kernel may reach another device: no remote copies, remote signals or barrier semaphores. Data moves between devices by JAX's collectives and lax.ppermute only.
A program may use at most 64 MiB of HBM per device.

v0:
```python
from functools import partial

import jax
import jax.numpy as jnp
from jax import lax
from jax.sharding import PartitionSpec as P

NS_STEPS = 6


highest_precision = lax.Precision.HIGHEST
eps = 1e-05
ridge = 0.1


def norm_layer(values, gain_vec, shift_vec):
    centre = values - jnp.mean(values, axis=-1, keepdims=True)
    spread = jnp.mean(centre * centre, axis=-1, keepdims=True)
    return centre * lax.rsqrt(spread + eps) * gain_vec + shift_vec


def kernel_rows(points, landmarks, sharpness):
    inner_part = jnp.einsum("...td,...md->...tm", points, landmarks, precision=highest_precision)
    point_half = 0.5 * jnp.sum(points * points, axis=-1)
    mark_half = 0.5 * jnp.sum(landmarks * landmarks, axis=-1)
    return jnp.exp(sharpness * (inner_part - point_half[..., :, None] - mark_half[..., None, :]))


def pseudo_inverse(landmarks, same_mark, sharpness):
    mark_count = landmarks.shape[-2]
    kernel = kernel_rows(landmarks, landmarks, sharpness) * same_mark + ridge * jnp.eye(
        mark_count, dtype=jnp.float32
    )
    widest = jnp.max(jnp.sum(kernel, axis=-1), axis=-1)
    approx = kernel / (widest * widest)[..., None, None]
    for repeat_idx in range(NS_STEPS):
        middle = jnp.einsum("...ij,...jk->...ik", approx, kernel, precision=highest_precision)
        approx = 2.0 * approx - jnp.einsum(
            "...ij,...jk->...ik", middle, approx, precision=highest_precision
        )
    return approx


def kernel_pair(query_f, key_f, landmarks, same_tok, sharpness):
    return (
        kernel_rows(query_f, landmarks, sharpness) * same_tok,
        kernel_rows(key_f, landmarks, sharpness) * same_tok,
    )


def as_matrix(array):
    return array.reshape(-1, array.shape[-1])


def shards(
    tokens_in,
    segments,
    landmark_index,
    ln1_gain,
    ln1_bias,
    w_query,
    b_query,
    w_key,
    b_key,
    w_value,
    b_value,
    w_out,
    b_out,
    ln2_gain,
    ln2_bias,
    w_up,
    b_up,
    w_down,
    b_down,
    grad_out,
):
    rows_here, tok_here, model_width = tokens_in.shape
    head_count = landmark_index.shape[1]
    head_size = model_width // head_count
    sharpness = head_size ** (-0.5)
    length_total = tok_here * lax.axis_size("tok")
    out_scale = length_total ** (-0.5)
    positions = lax.axis_index("tok") * tok_here + jnp.arange(tok_here, dtype=jnp.int32)
    token_of = landmark_index % length_total
    from_query = (landmark_index < length_total).astype(jnp.float32)
    pick_all = (token_of[..., None] == positions).astype(jnp.float32)
    pick_query_f = pick_all * from_query[..., None]
    pick_key_f = pick_all * (1.0 - from_query)[..., None]
    pick_query = pick_query_f.astype(jnp.bfloat16)
    pick_key = pick_key_f.astype(jnp.bfloat16)
    seg_float = segments.astype(jnp.float32)
    mark_seg_part = jnp.einsum(
        "rhmt,rt->rhm", pick_all, seg_float, precision=highest_precision
    ).astype(jnp.bfloat16)
    gain1 = ln1_gain.astype(jnp.float32)
    bias1 = ln1_bias.astype(jnp.float32)
    gain2 = ln2_gain.astype(jnp.float32)
    bias2 = ln2_bias.astype(jnp.float32)

    def split_heads(array):
        return array.reshape(rows_here, tok_here, head_count, head_size).transpose(0, 2, 1, 3)

    def join_heads(array):
        return array.transpose(0, 2, 1, 3).reshape(rows_here, tok_here, model_width)

    x_float = tokens_in.astype(jnp.float32)
    normed_f, norm_pull = jax.vjp(norm_layer, x_float, gain1, bias1)
    normed = normed_f.astype(jnp.bfloat16)

    def project(weight, shift_vec):
        made = jnp.dot(normed, weight, preferred_element_type=jnp.float32) + shift_vec.astype(
            jnp.float32
        )
        return split_heads(made.astype(jnp.bfloat16))

    query = project(w_query, b_query)
    key_vec = project(w_key, b_key)
    value_rows = project(w_value, b_value)

    def attention_section(again):
        own_marks = (
            jnp.einsum("rhmt,rhtd->rhmd", pick_query, query, preferred_element_type=jnp.float32)
            + jnp.einsum("rhmt,rhtd->rhmd", pick_key, key_vec, preferred_element_type=jnp.float32)
        ).astype(jnp.bfloat16)
        if again:
            landmarks, mark_seg = (
                lax.psum(own_marks, "tok").astype(jnp.float32),
                lax.psum(mark_seg_part, "tok").astype(jnp.float32),
            )
        else:
            landmarks, mark_seg = (
                lax.psum(own_marks, "tok").astype(jnp.float32),
                lax.psum(mark_seg_part, "tok").astype(jnp.float32),
            )
        same_tok = (seg_float[:, None, :, None] == mark_seg[:, :, None, :]).astype(jnp.float32)
        same_mark = (mark_seg[:, :, :, None] == mark_seg[:, :, None, :]).astype(jnp.float32)
        pair_fn = partial(kernel_pair, same_tok=same_tok, sharpness=sharpness)
        (near_q_f, near_k_f), kernel_pull = jax.vjp(
            pair_fn, query.astype(jnp.float32), key_vec.astype(jnp.float32), landmarks
        )
        nearby_key_kernel = near_k_f.astype(jnp.bfloat16)
        partial_sum = jnp.einsum(
            "rhtm,rhtd->rhmd", nearby_key_kernel, value_rows, preferred_element_type=jnp.float32
        )
        if again:
            summed_output = lax.psum(partial_sum, "tok")
        else:
            summed_output = lax.psum(partial_sum, "tok")
        inverse_fn = partial(pseudo_inverse, same_mark=same_mark, sharpness=sharpness)
        inverse_matrix, inverse_pull = jax.vjp(inverse_fn, landmarks)
        mixed_value = jnp.einsum(
            "rhmn,rhnd->rhmd", inverse_matrix, summed_output, precision=highest_precision
        ).astype(jnp.bfloat16)
        return (
            near_q_f.astype(jnp.bfloat16),
            nearby_key_kernel,
            summed_output,
            inverse_matrix,
            mixed_value,
            kernel_pull,
            inverse_pull,
        )

    (
        nearby_query_kernel,
        nearby_key_kernel,
        summed_output,
        inverse_matrix,
        mixed_value,
        kernel_pull,
        inverse_pull,
    ) = attention_section(False)
    attended_h = (
        jnp.einsum(
            "rhtm,rhmd->rhtd", nearby_query_kernel, mixed_value, preferred_element_type=jnp.float32
        )
        * out_scale
    )
    attention_result = join_heads(attended_h.astype(jnp.bfloat16))
    hidden = (
        x_float
        + jnp.dot(attention_result, w_out, preferred_element_type=jnp.float32)
        + b_out.astype(jnp.float32)
    )
    normed2_f, norm2_pull = jax.vjp(norm_layer, hidden, gain2, bias2)
    normed2 = normed2_f.astype(jnp.bfloat16)
    inner_pre = jnp.dot(normed2, w_up, preferred_element_type=jnp.float32) + b_up.astype(
        jnp.float32
    )
    gelu_val, gelu_pull = jax.vjp(jax.nn.gelu, inner_pre)
    activated = gelu_val.astype(jnp.bfloat16)
    result = (
        hidden
        + jnp.dot(activated, w_down, preferred_element_type=jnp.float32)
        + b_down.astype(jnp.float32)
    )
    grad_w_down = jnp.dot(
        as_matrix(activated).T, as_matrix(grad_out), preferred_element_type=jnp.float32
    )
    grad_b_down = jnp.sum(grad_out.astype(jnp.float32), axis=(0, 1))
    d_act = jnp.dot(grad_out, w_down.T, preferred_element_type=jnp.float32)
    d_inner = gelu_pull(d_act)[0].astype(jnp.bfloat16)
    grad_w_up = jnp.dot(
        as_matrix(normed2).T, as_matrix(d_inner), preferred_element_type=jnp.float32
    )
    grad_b_up = jnp.sum(d_inner.astype(jnp.float32), axis=(0, 1))
    d_norm2 = jnp.dot(d_inner, w_up.T, preferred_element_type=jnp.float32)
    d_hidden_norm, grad_gain2, grad_bias2 = norm2_pull(d_norm2)
    d_hidden = grad_out.astype(jnp.float32) + d_hidden_norm
    d_branch = d_hidden.astype(jnp.bfloat16)
    grad_w_out = jnp.dot(
        as_matrix(attention_result).T, as_matrix(d_branch), preferred_element_type=jnp.float32
    )
    grad_b_out = jnp.sum(d_branch.astype(jnp.float32), axis=(0, 1))
    d_att = split_heads(
        jnp.dot(d_branch, w_out.T, preferred_element_type=jnp.float32).astype(jnp.bfloat16)
    )
    (
        nearby_query_kernel,
        nearby_key_kernel,
        summed_output,
        inverse_matrix,
        mixed_value,
        kernel_pull,
        inverse_pull,
    ) = attention_section(True)
    d_mixed_part = (
        jnp.einsum(
            "rhtm,rhtd->rhmd", nearby_query_kernel, d_att, preferred_element_type=jnp.float32
        )
        * out_scale
    )
    d_mixed = lax.psum(d_mixed_part.astype(jnp.bfloat16), "tok")
    d_near_q = (
        jnp.einsum("rhtd,rhmd->rhtm", d_att, mixed_value, preferred_element_type=jnp.float32)
        * out_scale
    ).astype(jnp.bfloat16)
    d_mixed_f = d_mixed.astype(jnp.float32)
    d_inverse = jnp.einsum("rhmd,rhnd->rhmn", d_mixed_f, summed_output, precision=highest_precision)
    d_summed = jnp.einsum(
        "rhnm,rhnd->rhmd", inverse_matrix, d_mixed_f, precision=highest_precision
    ).astype(jnp.bfloat16)
    d_near_k = jnp.einsum(
        "rhtd,rhmd->rhtm", value_rows, d_summed, preferred_element_type=jnp.float32
    ).astype(jnp.bfloat16)
    d_value = jnp.einsum(
        "rhtm,rhmd->rhtd", nearby_key_kernel, d_summed, preferred_element_type=jnp.float32
    ).astype(jnp.bfloat16)
    d_query_k, d_key_k, d_marks_part = kernel_pull(
        (d_near_q.astype(jnp.float32), d_near_k.astype(jnp.float32))
    )
    d_marks_here = inverse_pull(d_inverse)[0]
    d_marks = lax.psum(d_marks_part.astype(jnp.bfloat16), "tok").astype(jnp.float32) + d_marks_here
    d_query = (
        d_query_k
        + jnp.einsum("rhmt,rhmd->rhtd", pick_query_f, d_marks, precision=highest_precision)
    ).astype(jnp.bfloat16)
    d_key = (
        d_key_k + jnp.einsum("rhmt,rhmd->rhtd", pick_key_f, d_marks, precision=highest_precision)
    ).astype(jnp.bfloat16)
    d_query_flat = join_heads(d_query)
    d_key_flat = join_heads(d_key)
    d_value_flat = join_heads(d_value)
    normed_mat = as_matrix(normed).T
    grad_w_query = jnp.dot(normed_mat, as_matrix(d_query_flat), preferred_element_type=jnp.float32)
    grad_w_key = jnp.dot(normed_mat, as_matrix(d_key_flat), preferred_element_type=jnp.float32)
    grad_w_value = jnp.dot(normed_mat, as_matrix(d_value_flat), preferred_element_type=jnp.float32)
    grad_b_query = jnp.sum(d_query_flat.astype(jnp.float32), axis=(0, 1))
    grad_b_key = jnp.sum(d_key_flat.astype(jnp.float32), axis=(0, 1))
    grad_b_value = jnp.sum(d_value_flat.astype(jnp.float32), axis=(0, 1))
    d_normed = (
        jnp.dot(d_query_flat, w_query.T, preferred_element_type=jnp.float32)
        + jnp.dot(d_key_flat, w_key.T, preferred_element_type=jnp.float32)
        + jnp.dot(d_value_flat, w_value.T, preferred_element_type=jnp.float32)
    )
    d_x_norm, grad_gain1, grad_bias1 = norm_pull(d_normed)
    grad_input = d_hidden + d_x_norm
    all_sums = lax.psum(
        (
            grad_gain1,
            grad_bias1,
            grad_w_query,
            grad_b_query,
            grad_w_key,
            grad_b_key,
            grad_w_value,
            grad_b_value,
            grad_w_out,
            grad_b_out,
            grad_gain2,
            grad_bias2,
            grad_w_up,
            grad_b_up,
            grad_w_down,
            grad_b_down,
        ),
        ("rows", "tok"),
    )
    return (result.astype(jnp.bfloat16), grad_input) + tuple(all_sums)


def solution(mesh):
    return jax.shard_map(
        shards,
        mesh=mesh,
        in_specs=(
            P("rows", "tok", None),
            P("rows", "tok"),
            P("rows", None, None),
            P(),
            P(),
            P(),
            P(),
            P(),
            P(),
            P(),
            P(),
            P(),
            P(),
            P(),
            P(),
            P(),
            P(),
            P(),
            P(),
            P("rows", "tok", None),
        ),
        out_specs=(
            P("rows", "tok", None),
            P("rows", "tok", None),
            P(),
            P(),
            P(),
            P(),
            P(),
            P(),
            P(),
            P(),
            P(),
            P(),
            P(),
            P(),
            P(),
            P(),
            P(),
            P(),
        ),
        check_vma=False,
    )
```

profile of v0, /device:TPU:0, one launch (start us, length us, event | category | flops | bytes accessed | tf_op | source)
XLA Modules:
  0.0 559.1 jit_solution(8397584559008552173)
XLA Ops:
  17.8 23.1 %psum.156 = bf16[7,2,128]{2,1,0:T(2,128)(2,1)S(1)} all-reduce(bf16[7,2,128]{2,1,0:T(2,128)(2,1)S(1)} %convert_element_type.197), channel_id=1, replica_groups=mesh['rows'=4,'tok'=8] {'tok'}, use_global_device_ids=true, to_apply=%region_0.1 | all-reduce | flops 1792 | bytes 7168 | tf_op jit(solution)/shard_map/psum | solution.py:133
  46.6 41.1 %all-reduce.7.cloned.1.call-done = bf16[7,2,128,32]{2,3,1,0:T(8,128)(2,1)} async-done(((bf16[7,2,128,32]{2,3,1,0:T(8,128)(2,1)}), bf16[7,2,128,32]{2,3,1,0:T(8,128)(2,1)}) %all-reduce.7.cloned.1.call-update) | async-done | bytes 114704 | tf_op jit(solution)/shard_map/psum | solution.py:132
  91.7 2.1 fusion.143
  93.8 2.1 convolution_subtract_fusion.5
  96.0 2.0 fusion.160
  98.1 2.0 convolution_subtract_fusion.4
  100.1 2.0 fusion.158
  102.2 2.0 convolution_subtract_fusion.3
  104.2 2.2 fusion.156
  106.4 2.0 convolution_subtract_fusion.2
  108.5 2.0 fusion.154
  110.6 2.1 convolution_subtract_fusion.1
  112.6 2.0 fusion.152
  114.7 3.0 convolution_subtract_fusion
  120.1 42.2 %all-reduce.9.cloned.1.call-done = f32[7,2,128,32]{2,3,1,0:T(8,128)} async-done(((f32[7,2,128,32]{2,3,1,0:T(8,128)}), f32[7,2,128,32]{2,3,1,0:T(8,128)}) %all-reduce.9.cloned.1.call-update) | async-done | bytes 229392 | tf_op jit(solution)/shard_map/psum | solution.py:148
  162.3 2.2 convolution_convert_fusion.1
  170.7 1.8 copy.177
  172.5 1.7 multiply_reduce_fusion.1
  179.7 2.0 fusion.41
  181.7 2.8 fusion.167
  185.3 1.7 reshape_reshape.15
  186.9 1.7 reshape.215
  191.5 2.2 fusion.28
  194.6 62.5 %all-reduce.11.cloned.1.call-done = bf16[7,2,128,32]{2,3,1,0:T(8,128)(2,1)} async-done(((bf16[7,2,128,32]{2,3,1,0:T(8,128)(2,1)}), bf16[7,2,128,32]{2,3,1,0:T(8,128)(2,1)}) %all-reduce.11.cloned.1.call-update) | async-done | bytes 114704 | tf_op jit(solution)/shard_map/psum | solution.py:233
  257.2 2.0 convolution_convert_fusion.2
  260.7 1.7 fusion.166
  263.9 2.0 fusion.59
  265.9 2.4 copy.183
  268.4 4.1 fusion.175
  274.2 2.0 convolution_add_fusion.15
  277.4 1.7 fusion.56
  279.1 2.2 convolution_add_fusion.12
  282.4 1.7 fusion.53
  284.0 2.0 convolution_add_fusion.9
  289.8 2.0 convolution_add_fusion.6
  293.0 1.9 fusion.47
  294.9 2.0 convolution_add_fusion.3
  296.9 2.0 convolution_add_fusion.1
  299.0 2.9 fusion.44
  304.5 1.7 reshape_reshape.14
  309.0 3.4 convolution_add_fusion.14
  312.5 1.7 convolution_add_fusion.11
  314.2 1.7 convolution_add_fusion.8
  316.0 1.7 convolution_add_fusion.5
  317.7 2.3 multiply_reduce_fusion
  320.8 2.5 fusion.165
  326.4 51.4 %all-reduce.13.cloned.1.call-done = bf16[7,2,128,32]{2,3,1,0:T(8,128)(2,1)} async-done(((bf16[7,2,128,32]{2,3,1,0:T(8,128)(2,1)}), bf16[7,2,128,32]{2,3,1,0:T(8,128)(2,1)}) %all-reduce.13.cloned.1.call-update) | async-done | bytes 114704 | tf_op jit(solution)/shard_map/psum | solution.py:253
  391.8 149.7 %all-reduce.15.cloned.1.call-done = (f32[64]{0:T(128)}, f32[64]{0:T(128)}, f32[64,64]{1,0:T(8,128)}, f32[64]{0:T(128)}, f32[64,64]{1,0:T(8,128)}, /*index=5*/f32...) async-done(((f32[64]{0:T(128)}, f32[64]{0:T(128)}, ...) | async-done | bytes 133904 | tf_op jit(solution)/shard_map/psum | solution.py:278
  (424 shorter events, 83.7 us)
Async XLA Ops:
  7.2 161.3 %copy-start = (bf16[128,64]{0,1:T(8,128)(2,1)S(1)}, bf16[128,64]{0,1:T(8,128)(2,1)}, u32[]{:S(2)}) copy-start(bf16[128,64]{0,1:T(8,128)(2,1)} %param.37) | copy-start | bytes 49156
  7.2 80.5 %all-reduce.7.cloned.1.call-start = ((), (), s32[]{:S(2)}) async-start(), calls=%async_computation | async-start | bytes 229376 | tf_op jit(solution)/shard_map/psum | solution.py:132
  8.1 8.5 %copy-start.78 = (s32[7,2,128]{2,1,0:T(2,128)}, s32[7,2,128]{2,1,0:T(2,128)S(1)}, u32[]{:S(2)}) copy-start(s32[7,2,128]{2,1,0:T(2,128)S(1)} %and_select_fusion) | copy-start | bytes 21508
  8.1 6.7 %copy-start.97 = (f32[7,2,128]{2,1,0:T(2,128)}, f32[7,2,128]{2,1,0:T(2,128)S(1)}, u32[]{:S(2)}) copy-start(f32[7,2,128]{2,1,0:T(2,128)S(1)} %broadcast_subtract_fusion) | copy-start | bytes 21508
  8.1 6.4 %copy-start.95 = (f32[7,2,128]{2,1,0:T(2,128)}, f32[7,2,128]{2,1,0:T(2,128)S(1)}, u32[]{:S(2)}) copy-start(f32[7,2,128]{2,1,0:T(2,128)S(1)} %compare_convert_fusion) | copy-start | bytes 21508
  8.8 7.8 %copy-start.120 = (s32[64]{0:T(128)}, s32[64]{0:T(128)S(1)}, u32[]{:S(2)}) copy-start(s32[64]{0:T(128)S(1)} %iota_add_fusion) | copy-start | bytes 772
  9.4 2.5 copy-start.112
  14.1 74.6 %copy-start.39 = (bf16[7,64,64]{1,2,0:T(8,128)(2,1)}, bf16[7,64,64]{1,2,0:T(8,128)(2,1)S(1)}, u32[]{:S(2)}) copy-start(bf16[7,64,64]{1,2,0:T(8,128)(2,1)S(1)} %copy.144) | copy-start | bytes 172036
  15.7 146.6 %all-reduce.9.cloned.1.call-start = ((), (), s32[]{:S(2)}) async-start(), calls=%async_computation.1 | async-start | bytes 458752 | tf_op jit(solution)/shard_map/psum | solution.py:148
  44.8 44.2 %copy-start.48 = (bf16[7,64,64]{1,2,0:T(8,128)(2,1)}, bf16[7,64,64]{1,2,0:T(8,128)(2,1)S(1)}, u32[]{:S(2)}) copy-start(bf16[7,64,64]{1,2,0:T(8,128)(2,1)S(1)} %copy.170) | copy-start | bytes 172036
  90.0 167.1 %all-reduce.11.cloned.1.call-start = ((), (), s32[]{:S(2)}) async-start(), calls=%async_computation.2 | async-start | bytes 229376 | tf_op jit(solution)/shard_map/psum | solution.py:233
  91.7 2.1 copy-start.115
  93.8 2.1 copy-start.58
  96.0 2.1 copy-start.7
  106.4 2.1 copy-start.23
  108.5 2.1 copy-start.1
  110.6 2.1 copy-start.25
  112.6 2.1 copy-start.3
  114.7 3.0 copy-start.10
  114.7 3.0 copy-start.42
  114.7 3.0 copy-start.81
  114.7 3.0 copy-start.99
  162.3 2.2 copy-start.31
  181.7 2.8 copy-start.54
  188.6 189.2 %all-reduce.13.cloned.1.call-start = ((), (), s32[]{:S(2)}) async-start(), calls=%async_computation.3 | async-start | bytes 229376 | tf_op jit(solution)/shard_map/psum | solution.py:253
  189.1 2.4 copy-start.29
  191.5 2.3 copy-start.63
  191.5 2.3 copy-start.111
  191.5 2.3 copy-start.119
  268.4 4.1 copy-start.6
  268.4 4.1 copy-start.11
  268.4 4.1 copy-start.37
  279.1 2.2 copy-start.12
  279.1 2.2 copy-start.24
  298.9 4.2 copy-start.105
  298.9 4.8 copy-start.55
  298.9 7.3 %copy-start.102 = (f32[7,2,128]{2,1,0:T(2,128)S(1)}, f32[7,2,128]{2,1,0:T(2,128)}, u32[]{:S(2)}) copy-start(f32[7,2,128]{2,1,0:T(2,128)} %get-tuple-element.60) | copy-start | bytes 21508
  298.9 7.3 %copy-start.103 = (f32[7,2,128]{2,1,0:T(2,128)S(1)}, f32[7,2,128]{2,1,0:T(2,128)}, u32[]{:S(2)}) copy-start(f32[7,2,128]{2,1,0:T(2,128)} %get-tuple-element.59) | copy-start | bytes 21508
  308.7 232.8 %all-reduce.15.cloned.1.call-start = ((), (), s32[]{:S(2)}) async-start(), calls=%async_computation.4 | async-start | bytes 403456 | tf_op jit(solution)/shard_map/psum | solution.py:278
  309.0 3.5 copy-start.14
  317.7 2.4 copy-start.106
  317.7 2.4 copy-start.108
  320.8 2.6 copy-start.35
  326.4 52.9 %copy-start.79 = (s32[7,2,128]{2,1,0:T(2,128)S(1)}, s32[7,2,128]{2,1,0:T(2,128)}, u32[]{:S(2)}) copy-start(s32[7,2,128]{2,1,0:T(2,128)} %copy-done.78) | copy-start | bytes 21508
  326.4 52.9 %copy-start.98 = (f32[7,2,128]{2,1,0:T(2,128)S(1)}, f32[7,2,128]{2,1,0:T(2,128)}, u32[]{:S(2)}) copy-start(f32[7,2,128]{2,1,0:T(2,128)} %copy-done.97) | copy-start | bytes 21508
  326.4 52.9 %copy-start.121 = (s32[64]{0:T(128)S(1)}, s32[64]{0:T(128)}, u32[]{:S(2)}) copy-start(s32[64]{0:T(128)} %copy-done.120) | copy-start | bytes 772
  541.5 2.3 copy-start.94
  547.3 2.5 copy-start.90
  (101 other events, 111.3 us)
Sparse Core Ops, SparseCore 0:
  15.8 71.8 all-reduce.6
  92.0 70.2 all-reduce.8
  188.8 68.3 all-reduce.10
  308.8 68.9 all-reduce.12
  389.2 152.2 all-reduce.14
where the time goes:
time: 563 us; the launch traced here: 559 us
  waiting for transfers between devices  347 us (62%)
  matrix products  112 us (20%)
  local copies, waits for them, and re-layouts  47.9 us (9%)
  blocking collectives  23.1 us (4%)
  between operations  15.8 us (3%)
  other arithmetic  12.6 us (2%)
    psum x1, waiting for transfers between devices, shards(): lax.psum((grad_gain1, grad_bias1, grad_w_query, grad_b_query, grad_w_key,...  150 us
    psum x1, waiting for transfers between devices, shards(): d_mixed = lax.psum(d_mixed_part.astype(jnp.bfloat16), 'tok')  62.5 us
    psum x1, waiting for transfers between devices, shards(): lax.psum(d_marks_part.astype(jnp.bfloat16), 'tok').astype(jnp.float32)  51.4 us
    psum x1, waiting for transfers between devices, attention_section(): summed_output = lax.psum(partial_sum, 'tok')  42.2 us
    psum x1, waiting for transfers between devices, attention_section(): lax.psum(own_marks, 'tok').astype(jnp.float32)  41.1 us
    dot_general x18, matrix products, pseudo_inverse(): jnp.einsum('...ij,...jk->...ik', approx, kernel, precision=highest_precis...  40.3 us
    dot_general x18, matrix products, pseudo_inverse(): jnp.einsum('...ij,...jk->...ik', middle, approx, precision=highest_precis...  32.8 us
    unnamed x308, local copies, waits for them, and re-layouts  31.2 us
  transfers between devices with their start and end apart: 5, of which 5 were waited for; matrix products, arithmetic and copies ran while one was open for 10% of the time, Pallas kernels for 0%

commit v1 on v0

v1 whole, which is shorter than its diff:
```python
from functools import partial

import jax
import jax.numpy as jnp
from jax import lax
from jax.experimental import pallas as pl
from jax.experimental.pallas import tpu as pltpu
from jax.sharding import PartitionSpec as P


NS_STEPS = 6
EPS = 1e-05
RIDGE = 0.1
FAR = 640.0
SEG_ROWS = 16
GRAD_ROWS = 272

f32 = jnp.float32
bf16 = jnp.bfloat16


def mm(a, b):
    return lax.dot_general(a, b, (((1,), (0,)), ((), ())), preferred_element_type=f32)


def mm_nt(a, b):
    return lax.dot_general(a, b, (((1,), (1,)), ((), ())), preferred_element_type=f32)


def mm_tn(a, b):
    return lax.dot_general(a, b, (((0,), (0,)), ((), ())), preferred_element_type=f32)


def split(a):
    hi = a.astype(bf16)
    return hi, (a - hi.astype(f32)).astype(bf16)


def wide_right(b):
    hi, lo = split(b)
    return jnp.concatenate(
        [jnp.concatenate([hi, lo], 1), jnp.concatenate([hi, jnp.zeros_like(hi)], 1)], 0
    )


def mm_wide(a, wide):
    n = wide.shape[1] // 2
    both = mm(jnp.concatenate(split(a), 1), wide)
    return both[:, :n] + both[:, n:]


def row_sum(a):
    return jnp.sum(a, axis=1, keepdims=True)


def col_sum(a):
    return jnp.sum(a, axis=0, keepdims=True)


def norm_stats(values):
    centre = values - row_sum(values) * (1.0 / values.shape[1])
    spread = row_sum(centre * centre) * (1.0 / values.shape[1])
    scale = lax.rsqrt(spread + EPS)
    return centre * scale, scale


def norm_back(d_norm, xhat, scale, gain):
    scaled = d_norm * gain
    n = 1.0 / scaled.shape[1]
    return scale * (scaled - row_sum(scaled) * n - xhat * (row_sum(scaled * xhat) * n))


def iota(shape, dim):
    return lax.broadcasted_iota(jnp.int32, shape, dim)


def row_work(xg, onehot_t, idx, par):
    (gain1, bias1, wq, bq, wk, bk, wv, bv, wo, bo, gain2, bias2, wup, bup, wdown, bdown) = par
    tokens = xg.shape[0]
    width = wq.shape[0]
    heads, marks = idx.shape
    size = width // heads
    sharp = size**-0.5
    out_scale = tokens**-0.5
    hm = heads * marks
    lane = iota((tokens, 128), 1)
    low = lane < width

    def vec(v):
        return v.astype(f32)

    x = xg[:, :width].astype(f32)
    g16 = xg[:, width:]
    g = g16.astype(f32)
    xhat1, scale1 = norm_stats(x)
    normed = (xhat1 * vec(gain1) + vec(bias1)).astype(bf16)

    q2 = (mm(normed, jnp.concatenate([wq, wq], 1)) + vec(jnp.concatenate([bq, bq], 1))).astype(bf16)
    k2 = (mm(normed, jnp.concatenate([wk, wk], 1)) + vec(jnp.concatenate([bk, bk], 1))).astype(bf16)
    v = (mm(normed, wv) + vec(bv)).astype(bf16)
    q_t = q2.astype(f32).T[:width].astype(bf16)
    k_t = k2.astype(f32).T[:width].astype(bf16)
    v_t = v.astype(f32).T.astype(bf16)
    qk_t = jnp.concatenate([q_t, k_t], 1)

    place = (iota((SEG_ROWS, 128), 1) == iota((SEG_ROWS, 128), 0) + width).astype(f32).astype(bf16)
    seg_lanes = mm_tn(onehot_t, place)
    feat = jnp.where((lane >= width + 4) & (lane < width + 8), 1.0, seg_lanes)

    def features(p2):
        p = p2.astype(f32)
        sq = p * p
        hi = sq.astype(bf16).astype(f32)
        return jnp.concatenate(
            [jnp.where(low, p, hi).astype(bf16), jnp.where(low, sq - hi, feat).astype(bf16)], 1
        )

    feats = jnp.concatenate([features(q2), features(k2)], 0)

    idx_row = jnp.concatenate([idx[h : h + 1] for h in range(heads)], 1)
    pick_t = (iota((2 * tokens, hm), 0) == idx_row).astype(f32).astype(bf16)
    seg2 = jnp.concatenate([onehot_t, onehot_t], 1)
    picked = mm(jnp.concatenate([qk_t, seg2], 0), pick_t)
    own = ((iota((width, hm), 0) // size) == (iota((width, hm), 1) // marks)).astype(f32)
    mark_t = picked[:width] * own
    mark_seg = picked[width : width + 8]
    sq = mark_t * mark_t
    half = -0.5 * col_sum(sq)
    half_hi = half.astype(bf16).astype(f32)
    half_mid = (half - half_hi).astype(bf16).astype(f32)
    half_lo = half - half_hi - half_mid
    row8 = iota((8, hm), 0)
    extra = jnp.where(row8 < 4, mark_seg * FAR, 0.0)
    extra = jnp.where(row8 == 4, half_hi, extra)
    extra = jnp.where(row8 == 5, half_mid, extra)
    extra = jnp.where(row8 == 6, half_lo, extra)
    extra = jnp.where(row8 == 7, -FAR, extra)
    pad = jnp.zeros((width - 8, hm), f32)
    right = jnp.concatenate([mark_t, -0.5 * own, -0.5 * own, extra, pad], 0).astype(bf16)
    near = jnp.exp(sharp * mm(feats, right)).astype(bf16)
    near_q, near_k = near[:tokens], near[tokens:]

    sq_hi = sq.astype(bf16).astype(f32)
    left = jnp.concatenate(
        [mark_t, sq_hi, sq - sq_hi, jnp.where(row8 < 4, mark_seg, 1.0), pad], 0
    ).astype(bf16)
    mark16 = mark_t.astype(bf16)

    eye = (iota((marks, marks), 0) == iota((marks, marks), 1)).astype(f32)
    heads_now = []
    for h in range(heads):
        at = slice(h * marks, (h + 1) * marks)
        kernel = jnp.exp(sharp * mm_tn(left[:, at], right[:, at]))
        gram = kernel + RIDGE * eye
        sums = col_sum(gram)
        widest = jnp.max(sums, axis=1, keepdims=True)
        inv2 = 1.0 / (widest * widest)
        approx = gram * inv2
        rest = eye - mm_wide(approx, wide_right(gram))
        steps = []
        for step in range(NS_STEPS):
            steps.append((approx, rest))
            wide = wide_right(rest)
            if step < NS_STEPS - 1:
                both = mm_wide(jnp.concatenate([rest, approx], 0), wide)
                rest, approx = both[:marks], approx + both[marks:]
            else:
                approx = approx + mm_wide(approx, wide)
        heads_now.append((kernel, gram, sums, widest, inv2, steps, approx))

    summed_t = mm(v_t, near_k) * own
    mixed_t = jnp.concatenate(
        [
            mm_wide(summed_t[:, h * marks : (h + 1) * marks], wide_right(heads_now[h][6]))
            for h in range(heads)
        ],
        1,
    ).astype(bf16)
    att = (mm_nt(near_q, mixed_t) * out_scale).astype(bf16)
    hidden = x + mm(att, wo) + vec(bo)
    xhat2, scale2 = norm_stats(hidden)
    normed2 = (xhat2 * vec(gain2) + vec(bias2)).astype(bf16)
    inner = mm(normed2, wup) + vec(bup)
    c = (2.0 / jnp.pi) ** 0.5
    inner2 = inner * inner
    th = jnp.tanh(c * inner * (1.0 + 0.044715 * inner2))
    act = (0.5 * inner * (1.0 + th)).astype(bf16)
    layer_out = hidden + mm(act, wdown) + vec(bdown)

    d_act = mm_nt(g16, wdown)
    slope = 0.5 * (1.0 + th) + 0.5 * inner * (1.0 - th * th) * (
        c * (1.0 + (3.0 * 0.044715) * inner2)
    )
    d_inner = (d_act * slope).astype(bf16)
    g_wdown_t = mm_tn(g16, act)
    g_bdown = col_sum(g)
    g_wup = mm_tn(normed2, d_inner)
    g_bup = col_sum(d_inner.astype(f32))
    d_norm2 = mm_nt(d_inner, wup)
    g_gain2 = col_sum(d_norm2 * xhat2)
    g_bias2 = col_sum(d_norm2)
    d_hidden = g + norm_back(d_norm2, xhat2, scale2, vec(gain2))
    d_branch = d_hidden.astype(bf16)
    g_wo = mm_tn(att, d_branch)
    g_bo = col_sum(d_branch.astype(f32))
    d_att = mm_nt(d_branch, wo).astype(bf16)
    d_att_t = mm_nt(wo, d_branch).astype(bf16)
    d_mixed_t = (mm(d_att_t, near_q) * (own * out_scale)).astype(bf16)
    pull_q = ((mm(d_att, mixed_t) * out_scale) * near_q.astype(f32)).astype(bf16)
    d_summed = []
    gram_parts = []
    for h in range(heads):
        kernel, gram, sums, widest, inv2, steps, approx = heads_now[h]
        at = slice(h * marks, (h + 1) * marks)
        rows = slice(h * size, (h + 1) * size)
        hi, lo = split(approx)
        both = mm(d_mixed_t[:, at], jnp.concatenate([hi, lo], 1))
        d_summed.append((both[:, :marks] + both[:, marks:]).astype(bf16))
        dm = d_mixed_t[rows, at]
        s_hi, s_lo = split(summed_t[rows, at])
        d_now = 0.5 * mm_tn(
            jnp.concatenate([dm, dm, s_hi, s_lo], 0), jnp.concatenate([s_hi, s_lo, dm, dm], 0)
        )
        d_gram = jnp.zeros((marks, marks), f32)
        for step in reversed(range(NS_STEPS)):
            before, rest = steps[step]
            both = mm_wide(jnp.concatenate([rest, before], 0), wide_right(d_now))
            d_gram = d_gram - mm_wide(both[marks:], wide_right(before))
            turned = both[:marks]
            d_now = turned + turned.T
        d_gram = d_gram + inv2 * d_now
        d_widest = -2.0 * jnp.sum(row_sum(d_now * gram), axis=0, keepdims=True) * (inv2 / widest)
        top = (sums == widest).astype(f32)
        top = top * (d_widest / row_sum(top))
        d_gram = d_gram + top
        weighted = d_gram * kernel
        weighted = (0.5 * (weighted + weighted.T)).astype(bf16)
        lhs = jnp.concatenate([mark16[:, at], jnp.ones((16, marks), bf16)], 0)
        gram_parts.append(2.0 * mm(lhs, weighted))
    gram_part = jnp.concatenate(gram_parts, 1)
    d_summed_t = jnp.concatenate(d_summed, 1)
    pull_k = (mm(v, d_summed_t) * near_k.astype(f32)).astype(bf16)
    dv = mm_nt(near_k, d_summed_t).astype(bf16)
    pulls = jnp.concatenate([pull_q, pull_k], 0)
    tok_part = mm(jnp.concatenate([qk_t, jnp.ones((16, 2 * tokens), bf16)], 0), pulls)
    both_part = tok_part + gram_part
    d_mark_t = (both_part[:width] - mark_t * both_part[width : width + 1]) * own
    onto = jnp.concatenate([mark16, d_mark_t.astype(bf16)], 1)
    moved = mm_nt(jnp.concatenate([pulls, pick_t], 1), onto)
    weight = mm_nt(pulls, own.astype(bf16))
    dq = (sharp * (moved[:tokens] - weight[:tokens] * q2[:, :width].astype(f32))).astype(bf16)
    dk = (sharp * (moved[tokens:] - weight[tokens:] * k2[:, :width].astype(f32))).astype(bf16)
    d_normed = mm_nt(dq, wq) + mm_nt(dk, wk) + mm_nt(dv, wv)
    g_wq = mm_tn(normed, dq)
    g_wk = mm_tn(normed, dk)
    g_wv = mm_tn(normed, dv)
    g_bq = col_sum(dq.astype(f32))
    g_bk = col_sum(dk.astype(f32))
    g_bv = col_sum(dv.astype(f32))
    g_gain1 = col_sum(d_normed * xhat1)
    g_bias1 = col_sum(d_normed)
    grad_in = d_hidden + norm_back(d_normed, xhat1, scale1, vec(gain1))

    def pair(a, b):
        return jnp.concatenate([a, b], 1)

    vecs = [
        g_bup,
        pair(g_bdown, g_bq),
        pair(g_bk, g_bv),
        pair(g_bo, g_gain1),
        pair(g_bias1, g_gain2),
        pair(g_bias2, jnp.zeros_like(g_bias2)),
        jnp.zeros((GRAD_ROWS - 262, 128), f32),
    ]
    grads = jnp.concatenate([g_wup, g_wdown_t, pair(g_wq, g_wk), pair(g_wv, g_wo)] + vecs, 0)
    return pair(layer_out, grad_in).astype(bf16), grads


def read_params(refs):
    return tuple(r[...] if len(r.shape) == 2 else r[...].reshape(1, -1) for r in refs)


def main_kernel(tok_block, blk_ref, idx_ref, *refs):
    params, (out_ref, keep_ref, send_ref) = refs[:16], refs[16:]
    blocks = blk_ref.shape[0]
    tokens = blocks * tok_block
    row = jnp.minimum(lax.axis_index("tok"), idx_ref.shape[0] - 1)
    xg = blk_ref[:, :tok_block, :].reshape(tokens, 128)
    ids = blk_ref[:, tok_block:, :].astype(f32)
    half = iota((SEG_ROWS, 128), 1) < tok_block
    onehot_t = jnp.concatenate(
        [jnp.where(half, ids[2 * j], ids[2 * j + 1]) for j in range(blocks // 2)], 1
    ).astype(bf16)
    out, grads = row_work(xg, onehot_t, idx_ref[row], read_params(params))
    out_ref[...] = out.reshape(blocks, tok_block, 128)
    first = lax.rem(lax.axis_index("rows"), 2) == 0
    h = GRAD_ROWS // 2
    keep_ref[...] = jnp.where(first, grads[:h], grads[h:])
    send_ref[...] = jnp.where(first, grads[h:], grads[:h])


def pack_kernel(x_ref, g_ref, s_ref, out_ref):
    rows, tok, width = x_ref.shape
    out_ref[...] = jnp.zeros(out_ref.shape, out_ref.dtype)
    out_ref[:rows, :tok, :width] = x_ref[...]
    out_ref[:rows, :tok, width:] = g_ref[...]
    seg = s_ref[...]
    for r in range(rows):
        ids = jnp.broadcast_to(seg[r : r + 1], (SEG_ROWS, tok))
        onehot = (ids == iota((SEG_ROWS, tok), 0)).astype(f32).astype(bf16)
        out_ref[r, tok:, :width] = onehot
        out_ref[r, tok:, width:] = onehot


def sum_kernel(got_ref, out_ref, grad_ref, sum_ref):
    rows, tok, width = out_ref.shape
    out_ref[...] = got_ref[:rows, :tok, :width]
    grad_ref[...] = got_ref[:rows, :tok, width:].astype(f32)
    total = got_ref[0, tok:, :].astype(f32)
    for j in range(1, got_ref.shape[0]):
        total = total + got_ref[j, tok:, :].astype(f32)
    sum_ref[...] = total


def unpack_kernel(mine_ref, other_ref, *outs):
    first = lax.rem(lax.axis_index("rows"), 2) == 0
    mine, other = mine_ref[...], other_ref[...]
    a = jnp.where(first, mine, other)
    b = jnp.where(first, other, mine)
    whole = jnp.concatenate([a, b], 0)
    (gain1, bias1, wq, bq, wk, bk, wv, bv, wo, bo, gain2, bias2, wup, bup, wdown, bdown) = outs
    wup[...] = whole[0:64]
    wdown[...] = whole[64:128].T
    wq[...] = whole[128:192, :64]
    wk[...] = whole[128:192, 64:]
    wv[...] = whole[192:256, :64]
    wo[...] = whole[192:256, 64:]
    bup[...] = whole[256]
    bdown[...] = whole[257, :64]
    bq[...] = whole[257, 64:]
    bk[...] = whole[258, :64]
    bv[...] = whole[258, 64:]
    bo[...] = whole[259, :64]
    gain1[...] = whole[259, 64:]
    bias1[...] = whole[260, :64]
    gain2[...] = whole[260, 64:]
    bias2[...] = whole[261, :64]


def call(kernel, outs, *args):
    vmem = pl.BlockSpec(memory_space=pltpu.VMEM)
    return pl.pallas_call(
        kernel,
        out_shape=outs,
        in_specs=[vmem] * len(args),
        out_specs=jax.tree.map(lambda _: vmem, outs),
        compiler_params=pltpu.CompilerParams(vmem_limit_bytes=56 * 1024 * 1024),
    )(*args)


def shards(tokens_in, segments, landmark_index, *rest):
    params, grad_out = rest[:16], rest[16]
    rows, tok, width = tokens_in.shape
    n_tok = lax.axis_size("tok")
    n_rows = lax.axis_size("rows")
    sds = jax.ShapeDtypeStruct
    sent = call(
        pack_kernel, sds((n_tok, tok + SEG_ROWS, 128), bf16), tokens_in, grad_out, segments
    )
    got = lax.all_to_all(sent, "tok", 0, 0, tiled=True)
    h = GRAD_ROWS // 2
    out, keep, send = call(
        partial(main_kernel, tok),
        (sds((n_tok, tok, 128), bf16), sds((h, 128), f32), sds((h, 128), f32)),
        got,
        landmark_index,
        *params,
    )
    total = keep + lax.ppermute(send, "rows", [(i, i ^ 1) for i in range(n_rows)])
    step = 2
    while step < n_rows:
        total = total + lax.ppermute(total, "rows", [(i, i ^ step) for i in range(n_rows)])
        step *= 2
    back = jnp.concatenate([out, jnp.broadcast_to(total.astype(bf16), (n_tok, h, 128))], 1)
    got = lax.all_to_all(back, "tok", 0, 0, tiled=True)
    layer_out, grad_input, mine = call(
        sum_kernel,
        (sds((rows, tok, width), bf16), sds((rows, tok, width), f32), sds((h, 128), f32)),
        got,
    )
    other = lax.ppermute(mine, "rows", [(i, i ^ 1) for i in range(n_rows)])
    sums = call(unpack_kernel, tuple(sds(p.shape, f32) for p in params), mine, other)
    return (layer_out, grad_input) + tuple(sums)


def solution(mesh):
    split3 = P("rows", "tok", None)
    return jax.shard_map(
        shards,
        mesh=mesh,
        in_specs=(split3, P("rows", "tok"), P("rows", None, None)) + (P(),) * 16 + (split3,),
        out_specs=(split3, split3) + (P(),) * 16,
        check_vma=False,
    )
```

time: 563 us -> 60.1 us (0.11)
  waiting for transfers between devices: 347 us -> 12.6 us
  matrix products: 112 us -> 0 us
  local copies, waits for them, and re-layouts: 47.9 us -> 4.45 us
  Pallas kernels: 0 us -> 17.1 us
  between operations: 15.8 us -> 0.7 us
  other arithmetic: 12.6 us -> 0.94 us
  blocking collectives: 23.1 us -> 14.9 us
  starting transfers between devices: 1.03 us -> 8.97 us
    psum x5 -> x0, waiting for transfers between devices: 347 us -> none  [the longest x1 150 us: shards(): lax.psum((grad_gain1, grad_bias1, grad_w_query, grad_b_query, grad_w_key,...]
    dot_general x77 -> x0, matrix products: 112 us -> none  [the longest x18 40.3 us: pseudo_inverse(): jnp.einsum('...ij,...jk->...ik', approx, kernel, precision=highest_precis...]
    unnamed x308 -> x10, local copies, waits for them, and re-layouts: 31.2 us -> 4.41 us
    psum x1 -> x0, blocking collectives: 23.1 us -> none  [attention_section(): lax.psum(mark_seg_part, 'tok').astype(jnp.float32)]
    pallas_call x0 -> x4, Pallas kernels: none -> 17.1 us  [call(): pl.pallas_call(kernel, out_shape=outs, in_specs=[vmem] * len(args), out_s...]
    all_to_all x0 -> x1, blocking collectives: none -> 14.9 us  [shards(): got = lax.all_to_all(back, 'tok', 0, 0, tiled=True)]
    all_to_all x0 -> x1, starting transfers between devices: none -> 7.38 us  [shards(): got = lax.all_to_all(sent, 'tok', 0, 0, tiled=True)]
    all_to_all x0 -> x1, waiting for transfers between devices: none -> 6.83 us  [shards(): got = lax.all_to_all(sent, 'tok', 0, 0, tiled=True)]
  transfers between devices with their start and end apart: 5 -> 4, of which waited for: 5 -> 4; matrix products, arithmetic and copies ran while one was open for 10% -> 1% of each run, Pallas kernels for 0% -> 0%
where the time goes in v1:
time: 60.1 us; the launch traced here: 59.6 us
  Pallas kernels  17.1 us (28%)
  blocking collectives  14.9 us (25%)
  waiting for transfers between devices  12.6 us (21%)
  starting transfers between devices  8.97 us (15%)
  local copies, waits for them, and re-layouts  4.45 us (7%)
  other arithmetic  0.94 us (2%)
  between operations  0.7 us (1%)
    pallas_call x4, Pallas kernels, call(): pl.pallas_call(kernel, out_shape=outs, in_specs=[vmem] * len(args), out_s...  17.1 us
    all_to_all x1, blocking collectives, shards(): got = lax.all_to_all(back, 'tok', 0, 0, tiled=True)  14.9 us
    all_to_all x1, starting transfers between devices, shards(): got = lax.all_to_all(sent, 'tok', 0, 0, tiled=True)  7.38 us
    all_to_all x1, waiting for transfers between devices, shards(): got = lax.all_to_all(sent, 'tok', 0, 0, tiled=True)  6.83 us
    unnamed x10, local copies, waits for them, and re-layouts  4.41 us
    ppermute x1, waiting for transfers between devices, shards(): lax.ppermute(total, 'rows', [(i, i ^ step) for i in range(n_rows)])  2.79 us
    ppermute x1, starting transfers between devices, shards(): lax.ppermute(total, 'rows', [(i, i ^ step) for i in range(n_rows)])  1.58 us
    ppermute x1, waiting for transfers between devices, shards(): other = lax.ppermute(mine, 'rows', [(i, i ^ 1) for i in range(n_rows)])  1.47 us
  transfers between devices with their start and end apart: 4, of which 4 were waited for; matrix products, arithmetic and copies ran while one was open for 1% of the time, Pallas kernels for 0%

profile of v1, /device:TPU:0, one launch (start us, length us, event | category | flops | bytes accessed | tf_op | source)
XLA Modules:
  0.0 59.6 jit_solution(10373896584374256518)
XLA Ops:
  0.7 1.8 %shard_map.331 = bf16[8,80,128]{2,1,0:T(8,128)(2,1)} custom-call(bf16[7,64,64]{2,1,0:T(8,128)(2,1)} %x_ref.1, bf16[7,64,64]{2,1,0:T(8,128)(2,1)} %g_ref.1, s32[7,64]{1,0:T(8,128)} %s_ref.1), custom_call_target="tpu_custom_call" | custom-call | tf_op jit(solution)/shard_map/pallas_call | solution.py:353
  2.4 0.0 copy-start.3
  2.4 7.4 %all-to-all-start = ((bf16[8,80,128]{2,1,0:T(8,128)(2,1)}), bf16[8,80,128]{2,1,0:T(8,128)(2,1)S(1)}, u32[]{:S(2)}, u32[]{:S(2)}) async-start(bf16[8,80,128]{2,1,0:T(8,128)(2,1)} %shard_map.331), calls=%async_computation | async-start | bytes 327680 | tf_op jit(solution)/shard_map/all_to_all | solution.py:371
  9.8 0.0 copy-done.3
  9.8 0.7 %copy.38.refs_14_ = bf16[128,64]{1,0:T(8,128)(2,1)} copy(bf16[128,64]{0,1:T(8,128)(2,1)S(1)} %copy-done.3) | data formatting | bytes 32768 | tf_op args[17]
  10.5 6.8 %all-to-all-done.blk_ref = bf16[8,80,128]{2,1,0:T(8,128)(2,1)S(1)} async-done(((bf16[8,80,128]{2,1,0:T(8,128)(2,1)}), bf16[8,80,128]{2,1,0:T(8,128)(2,1)S(1)}, u32[]{:S(2)}, u32[]{:S(2)}) %all-to-all-start) | async-done | bytes 163872 | tf_op jit(solution)/shard_map/all_to_all | solution.py:371
  17.4 0.0 copy-start
  17.4 0.7 %copy-done = bf16[8,80,128]{2,1,0:T(8,128)(2,1)} copy-done((bf16[8,80,128]{2,1,0:T(8,128)(2,1)}, bf16[8,80,128]{2,1,0:T(8,128)(2,1)S(1)}, u32[]{:S(2)}) %copy-start) | copy-done | bytes 163864
  18.0 11.8 %shard_map.332 = (bf16[8,64,128]{2,1,0:T(8,128)(2,1)}, f32[136,128]{1,0:T(8,128)}, f32[136,128]{1,0:T(8,128)}) custom-call(bf16[8,80,128]{2,1,0:T(8,128)(2,1)} %copy-done, s32[7,2,128]{2,1,0:T(2,128)} %idx_ref.1, bf16[64]{0:T(256)(128)(2,1)} %refs_0_.1, bf16[64]{0:T(256)(128)(2,1)} %refs_1_.1, bf16[64,64]{1,0:T(8,128)(2,1)} %refs_2_.1, ...), custom_call_target="tpu_custom_call" | custom-call | tf_op jit(solution)/shard_map/pallas_call | solution.py:353
  29.8 0.0 collective-permute-start
  29.8 1.5 %collective-permute-done = f32[136,128]{1,0:T(8,128)S(1)} collective-permute-done((f32[136,128]{1,0:T(8,128)}, f32[136,128]{1,0:T(8,128)S(1)}, u32[]{:S(2)}, u32[]{:S(2)}) %collective-permute-start) | collective-permute-done | bytes 69664 | tf_op jit(solution)/shard_map/ppermute | solution.py:380
  31.3 0.9 %add.6 = f32[136,128]{1,0:T(8,128)S(1)} add(f32[136,128]{1,0:T(8,128)} %get-tuple-element.41, f32[136,128]{1,0:T(8,128)S(1)} %collective-permute-done) | non-fusion elementwise | flops 17408 | bytes 208896 | tf_op jit(solution)/shard_map/add | solution.py:380
  32.2 1.6 %collective-permute-start.1 = (f32[136,128]{1,0:T(8,128)S(1)}, f32[136,128]{1,0:T(8,128)S(1)}, u32[]{:S(2)}, u32[]{:S(2)}) collective-permute-start(f32[136,128]{1,0:T(8,128)S(1)} %add.6), channel_id=1, source_target_pairs={{0,16},{8,24},{16,0},{24,8},{1,17},{9,25},{17,1},{25,9},{2,18},{10... | collective-permute-start | bytes 208904 | tf_op jit(solution)/shard_map/ppermute | solution.py:383
  33.8 2.8 %collective-permute-done.1 = f32[136,128]{1,0:T(8,128)S(1)} collective-permute-done((f32[136,128]{1,0:T(8,128)S(1)}, f32[136,128]{1,0:T(8,128)S(1)}, u32[]{:S(2)}, u32[]{:S(2)}) %collective-permute-start.1) | collective-permute-done | bytes 69664 | tf_op jit(solution)/shard_map/ppermute | solution.py:383
  36.6 0.0 copy-start.1
  36.7 0.8 %copy-done.1 = bf16[8,64,128]{2,1,0:T(8,128)(2,1)S(1)} copy-done((bf16[8,64,128]{2,1,0:T(8,128)(2,1)S(1)}, bf16[8,64,128]{2,1,0:T(8,128)(2,1)}, u32[]{:S(2)}) %copy-start.1) | copy-done | bytes 131096
  37.5 14.9 %all_to_all.10.got_ref = bf16[8,200,128]{2,1,0:T(8,128)(2,1)} all-to-all(bf16[8,200,128]{2,1,0:T(8,128)(2,1)S(1)} %pad_maximum_fusion), channel_id=1, replica_groups=mesh['rows'=4,'tok'=8] {'tok'}, dimensions={0} | all-to-all | bytes 819200 | tf_op jit(solution)/shard_map/all_to_all | solution.py:386
  52.4 1.8 %shard_map.333 = (bf16[7,64,64]{2,1,0:T(8,128)(2,1)}, f32[7,64,64]{2,1,0:T(8,128)}, f32[136,128]{1,0:T(8,128)}) custom-call(bf16[8,200,128]{2,1,0:T(8,128)(2,1)} %all_to_all.10.got_ref), custom_call_target="tpu_custom_call" | custom-call | tf_op jit(solution)/shard_map/pallas_call | solution.py:353
  54.3 0.0 collective-permute-start.2
  54.3 1.5 %collective-permute-done.2.other_ref = f32[136,128]{1,0:T(8,128)S(1)} collective-permute-done((f32[136,128]{1,0:T(8,128)}, f32[136,128]{1,0:T(8,128)S(1)}, u32[]{:S(2)}, u32[]{:S(2)}) %collective-permute-start.2) | collective-permute-done | bytes 69664 | tf_op jit(solution)/shard_map/ppermute | solution.py:392
  55.7 0.0 copy-start.2
  55.7 0.6 %copy-done.2 = f32[136,128]{1,0:T(8,128)} copy-done((f32[136,128]{1,0:T(8,128)}, f32[136,128]{1,0:T(8,128)S(1)}, u32[]{:S(2)}) %copy-start.2) | copy-done | bytes 69656
  56.4 1.7 %shard_map.334 = (f32[64]{0:T(128)}, f32[64]{0:T(128)}, f32[64,64]{1,0:T(8,128)}, f32[64]{0:T(128)}, f32[64,64]{1,0:T(8,128)}, /*index=5*/f32[64]{0:T(128)}, f32...) custom-call(f32[136,128]{1,0:T(8,128)} %get-tuple-element.45.mine_re, ...), custom_call_target="tpu_custom_call" | custom-call | tf_op jit(solution)/shard_map/pallas_call | solution.py:353
  58.1 1.5 %copy.39 = f32[128,64]{0,1:T(8,128)} copy(f32[128,64]{1,0:T(8,128)} %get-tuple-element.78) | data formatting | bytes 65536
  (3 shorter events, 0.1 us)
Async XLA Ops:
  2.4 7.4 %copy-start.3 = (bf16[128,64]{0,1:T(8,128)(2,1)S(1)}, bf16[128,64]{0,1:T(8,128)(2,1)}, u32[]{:S(2)}) copy-start(bf16[128,64]{0,1:T(8,128)(2,1)} %param.37) | copy-start | bytes 49156
  2.4 14.9 %all-to-all-start = ((bf16[8,80,128]{2,1,0:T(8,128)(2,1)}), bf16[8,80,128]{2,1,0:T(8,128)(2,1)S(1)}, u32[]{:S(2)}, u32[]{:S(2)}) async-start(bf16[8,80,128]{2,1,0:T(8,128)(2,1)} %shard_map.331), calls=%async_computation | async-start | bytes 327680 | tf_op jit(solution)/shard_map/all_to_all | solution.py:371
  17.4 0.7 %copy-start = (bf16[8,80,128]{2,1,0:T(8,128)(2,1)}, bf16[8,80,128]{2,1,0:T(8,128)(2,1)S(1)}, u32[]{:S(2)}) copy-start(bf16[8,80,128]{2,1,0:T(8,128)(2,1)S(1)} %all-to-all-done.blk_ref) | copy-start | bytes 491524
  29.8 1.5 %collective-permute-start = (f32[136,128]{1,0:T(8,128)}, f32[136,128]{1,0:T(8,128)S(1)}, u32[]{:S(2)}, u32[]{:S(2)}) collective-permute-start(f32[136,128]{1,0:T(8,128)} %get-tuple-element.42), channel_id=1, source_target_pairs={{0,8},{8,0},{16,24},{24,16},{1,9},{9,1},{17,25},{25,17},{2,10},{10... | collective-permute-start | bytes 208904 | tf_op jit(solution)/shard_map/ppermute | solution.py:380
  32.2 4.4 %collective-permute-start.1 = (f32[136,128]{1,0:T(8,128)S(1)}, f32[136,128]{1,0:T(8,128)S(1)}, u32[]{:S(2)}, u32[]{:S(2)}) collective-permute-start(f32[136,128]{1,0:T(8,128)S(1)} %add.6), channel_id=1, source_target_pairs={{0,16},{8,24},{16,0},{24,8},{1,17},{9,25},{17,1},{25,9},{2,18},{10... | collective-permute-start | bytes 208904 | tf_op jit(solution)/shard_map/ppermute | solution.py:383
  36.6 0.9 %copy-start.1 = (bf16[8,64,128]{2,1,0:T(8,128)(2,1)S(1)}, bf16[8,64,128]{2,1,0:T(8,128)(2,1)}, u32[]{:S(2)}) copy-start(bf16[8,64,128]{2,1,0:T(8,128)(2,1)} %get-tuple-element.40) | copy-start | bytes 393220
  54.3 1.5 %collective-permute-start.2 = (f32[136,128]{1,0:T(8,128)}, f32[136,128]{1,0:T(8,128)S(1)}, u32[]{:S(2)}, u32[]{:S(2)}) collective-permute-start(f32[136,128]{1,0:T(8,128)} %get-tuple-element.45.mine_ref), channel_id=1, source_target_pairs={{0,8},{8,0},{16,24},{24,16},{1,9},{9,1},{17,25},{25,17},{2,10},{10... | collective-permute-start | bytes 208904 | tf_op jit(solution)/shard_map/ppermute | solution.py:392
  55.7 0.6 %copy-start.2 = (f32[136,128]{1,0:T(8,128)}, f32[136,128]{1,0:T(8,128)S(1)}, u32[]{:S(2)}) copy-start(f32[136,128]{1,0:T(8,128)S(1)} %collective-permute-done.2.other_ref) | copy-start | bytes 208900

commit v2 on v1

--- a/solution.py
+++ b/solution.py
@@ -57,6 +57,24 @@
     return jnp.sum(a, axis=0, keepdims=True)
 
 
+def total_of(a):
+    return col_sum(row_sum(a))
+
+
+def sym_outer(a, b):
+    a_hi, a_lo = split(a)
+    b_hi, b_lo = split(b)
+    return 0.5 * mm_tn(
+        jnp.concatenate([a_hi, a_hi, a_lo, b_hi, b_lo, b_hi], 0),
+        jnp.concatenate([b_hi, b_lo, b_hi, a_hi, a_hi, a_lo], 0),
+    )
+
+
+def both_sides(a, wide):
+    one = mm_wide(a, wide)
+    return one + one.T
+
+
 def norm_stats(values):
     centre = values - row_sum(values) * (1.0 / values.shape[1])
     spread = row_sum(centre * centre) * (1.0 / values.shape[1])
@@ -75,7 +93,7 @@
 
 
 def row_work(xg, onehot_t, idx, par):
-    (gain1, bias1, wq, bq, wk, bk, wv, bv, wo, bo, gain2, bias2, wup, bup, wdown, bdown) = par
+    (gain1, bias1, wq, bq, wk, bk, wv, bv, wo, bo, gain2, bias2, wup, bup, wdown_t, bdown) = par
     tokens = xg.shape[0]
     width = wq.shape[0]
     heads, marks = idx.shape
@@ -147,35 +165,35 @@
     mark16 = mark_t.astype(bf16)
 
     eye = (iota((marks, marks), 0) == iota((marks, marks), 1)).astype(f32)
-    heads_now = []
-    for h in range(heads):
-        at = slice(h * marks, (h + 1) * marks)
-        kernel = jnp.exp(sharp * mm_tn(left[:, at], right[:, at]))
-        gram = kernel + RIDGE * eye
-        sums = col_sum(gram)
-        widest = jnp.max(sums, axis=1, keepdims=True)
-        inv2 = 1.0 / (widest * widest)
-        approx = gram * inv2
-        rest = eye - mm_wide(approx, wide_right(gram))
-        steps = []
-        for step in range(NS_STEPS):
-            steps.append((approx, rest))
-            wide = wide_right(rest)
-            if step < NS_STEPS - 1:
-                both = mm_wide(jnp.concatenate([rest, approx], 0), wide)
-                rest, approx = both[:marks], approx + both[marks:]
-            else:
-                approx = approx + mm_wide(approx, wide)
-        heads_now.append((kernel, gram, sums, widest, inv2, steps, approx))
-
-    summed_t = mm(v_t, near_k) * own
-    mixed_t = jnp.concatenate(
-        [
-            mm_wide(summed_t[:, h * marks : (h + 1) * marks], wide_right(heads_now[h][6]))
-            for h in range(heads)
-        ],
-        1,
-    ).astype(bf16)
+    hs = range(heads)
+    at = [slice(h * marks, (h + 1) * marks) for h in hs]
+    rows_of = [slice(h * size, (h + 1) * size) for h in hs]
+    kernel = [jnp.exp(sharp * mm_tn(left[:, at[h]], right[:, at[h]])) for h in hs]
+    gram = [kernel[h] + RIDGE * eye for h in hs]
+    sums = [col_sum(gram[h]) for h in hs]
+    widest = [jnp.max(sums[h], axis=1, keepdims=True) for h in hs]
+    inv2 = [1.0 / (widest[h] * widest[h]) for h in hs]
+    gram_wide = [wide_right(gram[h]) for h in hs]
+    summed_t = [mm(v_t[rows_of[h]], near_k[:, at[h]]) for h in hs]
+    rests, wides, grown = [], [], []
+    rest = [eye - mm_wide(gram[h] * inv2[h], gram_wide[h]) for h in hs]
+    now = [mm_wide(summed_t[h], gram_wide[h]) * inv2[h] for h in hs]
+    for step in range(NS_STEPS):
+        wide = [wide_right(rest[h]) for h in hs]
+        rests.append(rest)
+        wides.append(wide)
+        grown.append(now)
+        if step < NS_STEPS - 1:
+            rest = [mm_wide(rest[h], wide[h]) for h in hs]
+        now = [now[h] + mm_wide(now[h], wide[h]) for h in hs]
+
+    def spread_heads(parts):
+        zero = jnp.zeros_like(parts[0])
+        return jnp.concatenate(
+            [jnp.concatenate([parts[h] if g == h else zero for g in hs], 1) for h in hs], 0
+        )
+
+    mixed_t = spread_heads(now).astype(bf16)
     att = (mm_nt(near_q, mixed_t) * out_scale).astype(bf16)
     hidden = x + mm(att, wo) + vec(bo)
     xhat2, scale2 = norm_stats(hidden)
@@ -185,9 +203,9 @@
     inner2 = inner * inner
     th = jnp.tanh(c * inner * (1.0 + 0.044715 * inner2))
     act = (0.5 * inner * (1.0 + th)).astype(bf16)
-    layer_out = hidden + mm(act, wdown) + vec(bdown)
-
-    d_act = mm_nt(g16, wdown)
+    layer_out = hidden + mm_nt(act, wdown_t) + vec(bdown)
+
+    d_act = mm(g16, wdown_t)
     slope = 0.5 * (1.0 + th) + 0.5 * inner * (1.0 - th * th) * (
         c * (1.0 + (3.0 * 0.044715) * inner2)
     )
@@ -207,38 +225,30 @@
     d_att_t = mm_nt(wo, d_branch).astype(bf16)
     d_mixed_t = (mm(d_att_t, near_q) * (own * out_scale)).astype(bf16)
     pull_q = ((mm(d_att, mixed_t) * out_scale) * near_q.astype(f32)).astype(bf16)
-    d_summed = []
+    back = [d_mixed_t[rows_of[h], at[h]].astype(f32) for h in hs]
+    d_rest = None
+    for step in reversed(range(NS_STEPS)):
+        outer = [sym_outer(back[h], grown[step][h]) for h in hs]
+        if d_rest is None:
+            d_rest = outer
+        else:
+            d_rest = [outer[h] + both_sides(d_rest[h], wides[step][h]) for h in hs]
+        back = [back[h] + mm_wide(back[h], wides[step][h]) for h in hs]
+    d_summed_t = spread_heads([mm_wide(back[h], gram_wide[h]) * inv2[h] for h in hs]).astype(bf16)
     gram_parts = []
-    for h in range(heads):
-        kernel, gram, sums, widest, inv2, steps, approx = heads_now[h]
-        at = slice(h * marks, (h + 1) * marks)
-        rows = slice(h * size, (h + 1) * size)
-        hi, lo = split(approx)
-        both = mm(d_mixed_t[:, at], jnp.concatenate([hi, lo], 1))
-        d_summed.append((both[:, :marks] + both[:, marks:]).astype(bf16))
-        dm = d_mixed_t[rows, at]
-        s_hi, s_lo = split(summed_t[rows, at])
-        d_now = 0.5 * mm_tn(
-            jnp.concatenate([dm, dm, s_hi, s_lo], 0), jnp.concatenate([s_hi, s_lo, dm, dm], 0)
+    for h in hs:
+        d_gram = inv2[h] * (
+            sym_outer(back[h], summed_t[h]) - both_sides(d_rest[h], gram_wide[h])
         )
-        d_gram = jnp.zeros((marks, marks), f32)
-        for step in reversed(range(NS_STEPS)):
-            before, rest = steps[step]
-            both = mm_wide(jnp.concatenate([rest, before], 0), wide_right(d_now))
-            d_gram = d_gram - mm_wide(both[marks:], wide_right(before))
-            turned = both[:marks]
-            d_now = turned + turned.T
-        d_gram = d_gram + inv2 * d_now
-        d_widest = -2.0 * jnp.sum(row_sum(d_now * gram), axis=0, keepdims=True) * (inv2 / widest)
-        top = (sums == widest).astype(f32)
-        top = top * (d_widest / row_sum(top))
-        d_gram = d_gram + top
-        weighted = d_gram * kernel
+        d_widest = (2.0 / widest[h]) * (
+            total_of(d_rest[h] * (eye - rests[0][h])) - total_of(back[h] * grown[0][h])
+        )
+        top = (sums[h] == widest[h]).astype(f32)
+        weighted = (d_gram + top * (d_widest / row_sum(top))) * kernel[h]
         weighted = (0.5 * (weighted + weighted.T)).astype(bf16)
-        lhs = jnp.concatenate([mark16[:, at], jnp.ones((16, marks), bf16)], 0)
+        lhs = jnp.concatenate([mark16[:, at[h]], jnp.ones((16, marks), bf16)], 0)
         gram_parts.append(2.0 * mm(lhs, weighted))
     gram_part = jnp.concatenate(gram_parts, 1)
-    d_summed_t = jnp.concatenate(d_summed, 1)
     pull_k = (mm(v, d_summed_t) * near_k.astype(f32)).astype(bf16)
     dv = mm_nt(near_k, d_summed_t).astype(bf16)
     pulls = jnp.concatenate([pull_q, pull_k], 0)
@@ -315,23 +325,27 @@
 
 def sum_kernel(got_ref, out_ref, grad_ref, sum_ref):
     rows, tok, width = out_ref.shape
-    out_ref[...] = got_ref[:rows, :tok, :width]
-    grad_ref[...] = got_ref[:rows, :tok, width:].astype(f32)
     total = got_ref[0, tok:, :].astype(f32)
     for j in range(1, got_ref.shape[0]):
         total = total + got_ref[j, tok:, :].astype(f32)
-    sum_ref[...] = total
-
-
-def unpack_kernel(mine_ref, other_ref, *outs):
+    sum_ref[...] = total.astype(bf16)
+    out_ref[...] = got_ref[:rows, :tok, :width]
+    grad_ref[...] = got_ref[:rows, :tok, width:].astype(f32)
+
+
+def unpack_kernel(n_parts, *refs):
+    parts, outs = refs[:n_parts], refs[n_parts:]
+    halves = [
+        sum([p[...].astype(f32) for p in parts[core + 2 :: 2]], parts[core][...].astype(f32))
+        for core in range(2)
+    ]
     first = lax.rem(lax.axis_index("rows"), 2) == 0
-    mine, other = mine_ref[...], other_ref[...]
-    a = jnp.where(first, mine, other)
-    b = jnp.where(first, other, mine)
+    a = jnp.where(first, halves[0], halves[1])
+    b = jnp.where(first, halves[1], halves[0])
     whole = jnp.concatenate([a, b], 0)
-    (gain1, bias1, wq, bq, wk, bk, wv, bv, wo, bo, gain2, bias2, wup, bup, wdown, bdown) = outs
+    (gain1, bias1, wq, bq, wk, bk, wv, bv, wo, bo, gain2, bias2, wup, bup, wdown_t, bdown) = outs
     wup[...] = whole[0:64]
-    wdown[...] = whole[64:128].T
+    wdown_t[...] = whole[64:128]
     wq[...] = whole[128:192, :64]
     wk[...] = whole[128:192, 64:]
     wv[...] = whole[192:256, :64]
@@ -348,25 +362,25 @@
     bias2[...] = whole[261, :64]
 
 
-def call(kernel, outs, *args):
+def call(kernel, outs, *args, mib=12):
     vmem = pl.BlockSpec(memory_space=pltpu.VMEM)
     return pl.pallas_call(
         kernel,
         out_shape=outs,
         in_specs=[vmem] * len(args),
         out_specs=jax.tree.map(lambda _: vmem, outs),
-        compiler_params=pltpu.CompilerParams(vmem_limit_bytes=56 * 1024 * 1024),
+        compiler_params=pltpu.CompilerParams(vmem_limit_bytes=mib * 1024 * 1024),
     )(*args)
 
 
 def shards(tokens_in, segments, landmark_index, *rest):
-    params, grad_out = rest[:16], rest[16]
+    params, grad_out = rest[:14] + (rest[14].T, rest[15]), rest[16]
     rows, tok, width = tokens_in.shape
     n_tok = lax.axis_size("tok")
     n_rows = lax.axis_size("rows")
     sds = jax.ShapeDtypeStruct
     sent = call(
-        pack_kernel, sds((n_tok, tok + SEG_ROWS, 128), bf16), tokens_in, grad_out, segments
+        pack_kernel, sds((n_tok, tok + SEG_ROWS, 128), bf16), tokens_in, grad_out, segments, mib=56
     )
     got = lax.all_to_all(sent, "tok", 0, 0, tiled=True)
     h = GRAD_ROWS // 2
@@ -376,21 +390,24 @@
         got,
         landmark_index,
         *params,
-    )
-    total = keep + lax.ppermute(send, "rows", [(i, i ^ 1) for i in range(n_rows)])
-    step = 2
-    while step < n_rows:
-        total = total + lax.ppermute(total, "rows", [(i, i ^ step) for i in range(n_rows)])
-        step *= 2
-    back = jnp.concatenate([out, jnp.broadcast_to(total.astype(bf16), (n_tok, h, 128))], 1)
+        mib=12 * max(1, n_tok * tok // 512),
+    )
+    def from_xor(array, m):
+        return lax.ppermute(array, "rows", [(i, i ^ m) for i in range(n_rows)])
+
+    total = (keep + from_xor(send, 1)).astype(bf16)
+    back = jnp.concatenate([out, jnp.broadcast_to(total, (n_tok, h, 128))], 1)
     got = lax.all_to_all(back, "tok", 0, 0, tiled=True)
     layer_out, grad_input, mine = call(
         sum_kernel,
-        (sds((rows, tok, width), bf16), sds((rows, tok, width), f32), sds((h, 128), f32)),
+        (sds((rows, tok, width), bf16), sds((rows, tok, width), f32), sds((h, 128), bf16)),
         got,
     )
-    other = lax.ppermute(mine, "rows", [(i, i ^ 1) for i in range(n_rows)])
-    sums = call(unpack_kernel, tuple(sds(p.shape, f32) for p in params), mine, other)
+    parts = [mine] + [from_xor(mine, m) for m in range(1, n_rows)]
+    sums = call(
+        partial(unpack_kernel, n_rows), tuple(sds(p.shape, f32) for p in params), *parts
+    )
+    sums = sums[:14] + (sums[14].T,) + sums[15:]
     return (layer_out, grad_input) + tuple(sums)
 
 

time: 60.1 us -> 48.4 us (0.81)
  blocking collectives: 14.9 us -> 30.3 us
  waiting for transfers between devices: 12.6 us -> 3.49 us
  starting transfers between devices: 8.97 us -> 1.93 us
  Pallas kernels: 17.1 us -> 10.8 us
  local copies, waits for them, and re-layouts: 4.45 us -> 0.66 us
  other arithmetic: 0.94 us -> 0.04 us
    all_to_all x0 -> x1, blocking collectives: none -> 15 us  [shards(): got = lax.all_to_all(sent, 'tok', 0, 0, tiled=True)]
    all_to_all x1 -> x0, starting transfers between devices: 7.38 us -> none  [shards(): got = lax.all_to_all(sent, 'tok', 0, 0, tiled=True)]
    all_to_all x1 -> x0, waiting for transfers between devices: 6.83 us -> none  [shards(): got = lax.all_to_all(sent, 'tok', 0, 0, tiled=True)]
    pallas_call x4, Pallas kernels: 17.1 us -> 10.8 us  [call(): pl.pallas_call(kernel, out_shape=outs, in_specs=[vmem] * len(args), out_s...]
    unnamed x10 -> x34, local copies, waits for them, and re-layouts: 4.41 us -> 0.63 us
    ppermute x3 -> x4, waiting for transfers between devices: 5.72 us -> 3.49 us  [from_xor(): return lax.ppermute(array, 'rows', [(i, i ^ m) for i in range(n_rows)])]
    add x1 -> x0, other arithmetic: 0.89 us -> none  [shards(): keep + lax.ppermute(send, 'rows', [(i, i ^ 1) for i in range(n_rows)])]
    ppermute x3 -> x4, starting transfers between devices: 1.59 us -> 1.93 us  [from_xor(): return lax.ppermute(array, 'rows', [(i, i ^ m) for i in range(n_rows)])]
  transfers between devices with their start and end apart: 4 -> 4, of which waited for: 4 -> 3; matrix products, arithmetic and copies ran while one was open for 1% -> 0% of each run, Pallas kernels for 0% -> 0%
where the time goes in v2:
time: 48.4 us; the launch traced here: 48.1 us
  blocking collectives  30.3 us (63%)
  Pallas kernels  10.8 us (22%)
  waiting for transfers between devices  3.49 us (7%)
  starting transfers between devices  1.93 us (4%)
  between operations  0.89 us (2%)
  local copies, waits for them, and re-layouts  0.66 us (1%)
    all_to_all x1, blocking collectives, shards(): got = lax.all_to_all(back, 'tok', 0, 0, tiled=True)  15.3 us
    all_to_all x1, blocking collectives, shards(): got = lax.all_to_all(sent, 'tok', 0, 0, tiled=True)  15 us
    pallas_call x4, Pallas kernels, call(): pl.pallas_call(kernel, out_shape=outs, in_specs=[vmem] * len(args), out_s...  10.8 us
    ppermute x4, waiting for transfers between devices, from_xor(): return lax.ppermute(array, 'rows', [(i, i ^ m) for i in range(n_rows)])  3.49 us
    ppermute x4, starting transfers between devices, from_xor(): return lax.ppermute(array, 'rows', [(i, i ^ m) for i in range(n_rows)])  1.93 us
  transfers between devices with their start and end apart: 4, of which 3 were waited for; matrix products, arithmetic and copies ran while one was open for 0% of the time, Pallas kernels for 0%

profile of v2, /device:TPU:0, one launch (start us, length us, event | category | flops | bytes accessed | tf_op | source)
XLA Modules:
  0.0 48.1 jit_solution(4305403206796271681)
XLA Ops:
  0.7 1.8 %shard_map.331 = bf16[8,80,128]{2,1,0:T(8,128)(2,1)} custom-call(bf16[7,64,64]{2,1,0:T(8,128)(2,1)} %x_ref.1, bf16[7,64,64]{2,1,0:T(8,128)(2,1)} %g_ref.1, s32[7,64]{1,0:T(8,128)} %s_ref.1), custom_call_target="tpu_custom_call" | custom-call | tf_op jit(solution)/shard_map/pallas_call | solution.py:367
  2.4 0.0 copy-start
  2.4 0.0 copy-start.1
  2.4 0.0 copy-start.2
  2.4 0.0 copy-start.3
  2.4 0.0 copy-start.4
  2.5 0.0 copy-start.5
  2.5 0.0 copy-start.6
  2.5 0.0 copy-start.10
  2.5 0.0 copy-start.11
  2.5 0.0 copy-start.12
  2.5 0.0 copy-start.13
  2.5 0.0 copy-start.14
  2.5 0.0 copy-start.15
  2.5 0.0 copy-start.16
  2.6 15.0 %all_to_all.10.blk_ref = bf16[8,80,128]{2,1,0:T(8,128)(2,1)S(1)} all-to-all(bf16[8,80,128]{2,1,0:T(8,128)(2,1)} %shard_map.331), channel_id=1, replica_groups=mesh['rows'=4,'tok'=8] {'tok'}, dimensions={0} | all-to-all | bytes 327680 | tf_op jit(solution)/shard_map/all_to_all | solution.py:385
  17.5 0.0 copy-start.7
  17.5 0.0 copy-start.8
  17.5 0.0 copy-start.9
  17.5 0.0 copy-done
  17.5 0.0 copy-done.1
  17.5 0.0 copy-done.2
  17.5 0.0 copy-done.3
  17.6 0.0 copy-done.4
  17.6 0.0 copy-done.5
  17.6 0.0 copy-done.6
  17.6 0.0 copy-done.10
  17.6 0.0 copy-done.11
  17.6 0.0 copy-done.12
  17.6 0.0 copy-done.13
  17.6 0.0 copy-done.14
  17.6 0.0 copy-done.15
  17.6 0.0 copy-done.16
  17.7 0.5 %copy-done.7 = bf16[64]{0:T(256)(128)(2,1)S(1)} copy-done((bf16[64]{0:T(256)(128)(2,1)S(1)}, bf16[64]{0:T(256)(128)(2,1)}, u32[]{:S(2)}) %copy-start.7) | copy-done | bytes 152
  18.2 0.0 copy-done.8
  18.2 0.0 copy-done.9
  18.2 7.5 %shard_map.332 = (bf16[8,64,128]{2,1,0:T(8,128)(2,1)S(1)}, f32[136,128]{1,0:T(8,128)S(1)}, f32[136,128]{1,0:T(8,128)S(1)}) custom-call(bf16[8,80,128]{2,1,0:T(8,128)(2,1)S(1)} %all_to_all.10.blk_ref, s32[7,2,128]{2,1,0:T(2,128)S(1)} %copy-done.6, bf16[64]{0:T(256)(128)(2,1)S(1)} %copy-done.7, bf16[64]{0:T(256)(128)(2,1)S(1)} %copy-done.8, ...), custom_call_target="tpu_custom_call" | custom-call | tf_op jit(solution)/shard_map/pallas_call | solution.py:367
  25.7 0.1 collective-permute-start
  25.8 1.2 %collective-permute-done = f32[136,128]{1,0:T(8,128)S(1)} collective-permute-done((f32[136,128]{1,0:T(8,128)S(1)}, f32[136,128]{1,0:T(8,128)S(1)}, u32[]{:S(2)}, u32[]{:S(2)}) %collective-permute-start) | collective-permute-done | bytes 69664 | tf_op jit(solution)/shard_map/ppermute | solution.py:396
  27.1 15.3 %all_to_all.11.got_ref = bf16[8,200,128]{2,1,0:T(8,128)(2,1)S(1)} all-to-all(bf16[8,200,128]{2,1,0:T(8,128)(2,1)S(1)} %pad_maximum_fusion), channel_id=1, replica_groups=mesh['rows'=4,'tok'=8] {'tok'}, dimensions={0} | all-to-all | bytes 819200 | tf_op jit(solution)/shard_map/all_to_all | solution.py:400
  42.5 0.8 %shard_map.333 = (bf16[7,64,64]{2,1,0:T(8,128)(2,1)}, f32[7,64,64]{2,1,0:T(8,128)}, bf16[136,128]{1,0:T(8,128)(2,1)S(1)}) custom-call(bf16[8,200,128]{2,1,0:T(8,128)(2,1)S(1)} %all_to_all.11.got_ref), custom_call_target="tpu_custom_call" | custom-call | tf_op jit(solution)/shard_map/pallas_call | solution.py:367
  43.3 0.0 collective-permute-start.3
  43.3 1.5 %collective-permute-start.2 = (bf16[136,128]{1,0:T(8,128)(2,1)S(1)}, bf16[136,128]{1,0:T(8,128)(2,1)S(1)}, u32[]{:S(2)}, u32[]{:S(2)}) collective-permute-start(bf16[136,128]{1,0:T(8,128)(2,1)S(1)} %get-tuple-element.45.refs_0_), channel_id=1, source_target_pairs={{0,16},{8,24},{16,0},{24,8},{1,17},{9,25},{17,1},{25,9},{2,18},{10... | collective-permute-start | bytes 104456 | tf_op jit(solution)/shard_map/ppermute | solution.py:396
  44.8 0.3 collective-permute-start.1
  45.1 1.8 %collective-permute-done.3.refs_3_ = bf16[136,128]{1,0:T(8,128)(2,1)S(1)} collective-permute-done((bf16[136,128]{1,0:T(8,128)(2,1)S(1)}, bf16[136,128]{1,0:T(8,128)(2,1)S(1)}, u32[]{:S(2)}, u32[]{:S(2)}) %collective-permute-start.3) | collective-permute-done | bytes 34848 | tf_op jit(solution)/shard_map/ppermute | solution.py:396
  46.9 0.4 collective-permute-done.2.refs_2_
  47.4 0.0 collective-permute-done.1.refs_1_
  47.4 0.7 %shard_map.334 = (f32[64]{0:T(128)}, f32[64]{0:T(128)}, f32[64,64]{1,0:T(8,128)}, f32[64]{0:T(128)}, f32[64,64]{1,0:T(8,128)}, /*index=5*/f32[64]{0:T(128)}, f32...) custom-call(bf16[136,128]{1,0:T(8,128)(2,1)S(1)} %get-tuple-element., ...), custom_call_target="tpu_custom_call" | custom-call | tf_op jit(solution)/shard_map/pallas_call | solution.py:367
  (3 shorter events, 0.1 us)
Async XLA Ops:
  2.4 15.1 %copy-start = (bf16[64,64]{1,0:T(8,128)(2,1)S(1)}, bf16[64,64]{1,0:T(8,128)(2,1)}, u32[]{:S(2)}) copy-start(bf16[64,64]{1,0:T(8,128)(2,1)} %refs_2_.1) | copy-start | bytes 24580
  2.4 15.1 %copy-start.1 = (bf16[64,64]{1,0:T(8,128)(2,1)S(1)}, bf16[64,64]{1,0:T(8,128)(2,1)}, u32[]{:S(2)}) copy-start(bf16[64,64]{1,0:T(8,128)(2,1)} %refs_4_.1) | copy-start | bytes 24580
  2.4 15.1 %copy-start.2 = (bf16[64,64]{1,0:T(8,128)(2,1)S(1)}, bf16[64,64]{1,0:T(8,128)(2,1)}, u32[]{:S(2)}) copy-start(bf16[64,64]{1,0:T(8,128)(2,1)} %refs_6_.1) | copy-start | bytes 24580
  2.4 15.1 %copy-start.3 = (bf16[64,64]{1,0:T(8,128)(2,1)S(1)}, bf16[64,64]{1,0:T(8,128)(2,1)}, u32[]{:S(2)}) copy-start(bf16[64,64]{1,0:T(8,128)(2,1)} %refs_8_.1) | copy-start | bytes 24580
  2.4 15.1 %copy-start.4 = (bf16[64,128]{1,0:T(8,128)(2,1)S(1)}, bf16[64,128]{1,0:T(8,128)(2,1)}, u32[]{:S(2)}) copy-start(bf16[64,128]{1,0:T(8,128)(2,1)} %refs_12_.1) | copy-start | bytes 49156
  2.5 15.1 %copy-start.5 = (bf16[128,64]{0,1:T(8,128)(2,1)S(1)}, bf16[128,64]{0,1:T(8,128)(2,1)}, u32[]{:S(2)}) copy-start(bf16[128,64]{0,1:T(8,128)(2,1)} %param.37) | copy-start | bytes 49156
  2.5 15.1 %copy-start.6 = (s32[7,2,128]{2,1,0:T(2,128)S(1)}, s32[7,2,128]{2,1,0:T(2,128)}, u32[]{:S(2)}) copy-start(s32[7,2,128]{2,1,0:T(2,128)} %idx_ref.1) | copy-start | bytes 21508
  2.5 15.1 %copy-start.10 = (bf16[64]{0:T(256)(128)(2,1)S(1)}, bf16[64]{0:T(256)(128)(2,1)}, u32[]{:S(2)}) copy-start(bf16[64]{0:T(256)(128)(2,1)} %refs_5_.1) | copy-start | bytes 388
  2.5 15.1 %copy-start.11 = (bf16[64]{0:T(256)(128)(2,1)S(1)}, bf16[64]{0:T(256)(128)(2,1)}, u32[]{:S(2)}) copy-start(bf16[64]{0:T(256)(128)(2,1)} %refs_7_.1) | copy-start | bytes 388
  2.5 15.1 %copy-start.12 = (bf16[64]{0:T(256)(128)(2,1)S(1)}, bf16[64]{0:T(256)(128)(2,1)}, u32[]{:S(2)}) copy-start(bf16[64]{0:T(256)(128)(2,1)} %refs_9_.1) | copy-start | bytes 388
  2.5 15.1 %copy-start.13 = (bf16[64]{0:T(256)(128)(2,1)S(1)}, bf16[64]{0:T(256)(128)(2,1)}, u32[]{:S(2)}) copy-start(bf16[64]{0:T(256)(128)(2,1)} %refs_10_.1) | copy-start | bytes 388
  2.5 15.1 %copy-start.14 = (bf16[64]{0:T(256)(128)(2,1)S(1)}, bf16[64]{0:T(256)(128)(2,1)}, u32[]{:S(2)}) copy-start(bf16[64]{0:T(256)(128)(2,1)} %refs_11_.1) | copy-start | bytes 388
  2.5 15.1 %copy-start.15 = (bf16[128]{0:T(256)(128)(2,1)S(1)}, bf16[128]{0:T(256)(128)(2,1)}, u32[]{:S(2)}) copy-start(bf16[128]{0:T(256)(128)(2,1)} %refs_13_.1) | copy-start | bytes 772
  2.5 15.1 %copy-start.16 = (bf16[64]{0:T(256)(128)(2,1)S(1)}, bf16[64]{0:T(256)(128)(2,1)}, u32[]{:S(2)}) copy-start(bf16[64]{0:T(256)(128)(2,1)} %refs_15_.1) | copy-start | bytes 388
  17.5 0.7 %copy-start.7 = (bf16[64]{0:T(256)(128)(2,1)S(1)}, bf16[64]{0:T(256)(128)(2,1)}, u32[]{:S(2)}) copy-start(bf16[64]{0:T(256)(128)(2,1)} %refs_0_.1) | copy-start | bytes 388
  17.5 0.7 %copy-start.8 = (bf16[64]{0:T(256)(128)(2,1)S(1)}, bf16[64]{0:T(256)(128)(2,1)}, u32[]{:S(2)}) copy-start(bf16[64]{0:T(256)(128)(2,1)} %refs_1_.1) | copy-start | bytes 388
  17.5 0.7 %copy-start.9 = (bf16[64]{0:T(256)(128)(2,1)S(1)}, bf16[64]{0:T(256)(128)(2,1)}, u32[]{:S(2)}) copy-start(bf16[64]{0:T(256)(128)(2,1)} %refs_3_.1) | copy-start | bytes 388
  25.7 1.3 %collective-permute-start = (f32[136,128]{1,0:T(8,128)S(1)}, f32[136,128]{1,0:T(8,128)S(1)}, u32[]{:S(2)}, u32[]{:S(2)}) collective-permute-start(f32[136,128]{1,0:T(8,128)S(1)} %get-tuple-element.42), channel_id=1, source_target_pairs={{0,8},{8,0},{16,24},{24,16},{1,9},{9,1},{17,25},{25,17},{2,10},{10... | collective-permute-start | bytes 208904 | tf_op jit(solution)/shard_map/ppermute | solution.py:396
  43.3 3.7 %collective-permute-start.3 = (bf16[136,128]{1,0:T(8,128)(2,1)S(1)}, bf16[136,128]{1,0:T(8,128)(2,1)S(1)}, u32[]{:S(2)}, u32[]{:S(2)}) collective-permute-start(bf16[136,128]{1,0:T(8,128)(2,1)S(1)} %get-tuple-element.45.refs_0_), channel_id=1, source_target_pairs={{0,24},{8,16},{16,8},{24,0},{1,25},{9,17},{17,9},{25,1},{2,26},{10... | collective-permute-start | bytes 104456 | tf_op jit(solution)/shard_map/ppermute | solution.py:396
  43.3 4.1 %collective-permute-start.2 = (bf16[136,128]{1,0:T(8,128)(2,1)S(1)}, bf16[136,128]{1,0:T(8,128)(2,1)S(1)}, u32[]{:S(2)}, u32[]{:S(2)}) collective-permute-start(bf16[136,128]{1,0:T(8,128)(2,1)S(1)} %get-tuple-element.45.refs_0_), channel_id=1, source_target_pairs={{0,16},{8,24},{16,0},{24,8},{1,17},{9,25},{17,1},{25,9},{2,18},{10... | collective-permute-start | bytes 104456 | tf_op jit(solution)/shard_map/ppermute | solution.py:396
  44.8 2.6 %collective-permute-start.1 = (bf16[136,128]{1,0:T(8,128)(2,1)S(1)}, bf16[136,128]{1,0:T(8,128)(2,1)S(1)}, u32[]{:S(2)}, u32[]{:S(2)}) collective-permute-start(bf16[136,128]{1,0:T(8,128)(2,1)S(1)} %get-tuple-element.45.refs_0_), channel_id=1, source_target_pairs={{0,8},{8,0},{16,24},{24,16},{1,9},{9,1},{17,25},{25,17},{2,10},{10... | collective-permute-start | bytes 104456 | tf_op jit(solution)/shard_map/ppermute | solution.py:396

commit v3 on v2

--- a/solution.py
+++ b/solution.py
@@ -61,18 +61,20 @@
     return col_sum(row_sum(a))
 
 
-def sym_outer(a, b):
-    a_hi, a_lo = split(a)
-    b_hi, b_lo = split(b)
-    return 0.5 * mm_tn(
-        jnp.concatenate([a_hi, a_hi, a_lo, b_hi, b_lo, b_hi], 0),
-        jnp.concatenate([b_hi, b_lo, b_hi, a_hi, a_hi, a_lo], 0),
-    )
-
-
-def both_sides(a, wide):
-    one = mm_wide(a, wide)
-    return one + one.T
+def both_parts(product, a, b):
+    n = b.shape[1]
+    both = product(a, jnp.concatenate(split(b), 1))
+    return both[:, :n] + both[:, n:]
+
+
+def pair(a, b):
+    return jnp.concatenate([a, b], 1)
+
+
+def wide_mm(a_pair, wide):
+    n = wide.shape[1] // 2
+    both = mm(a_pair, wide)
+    return both[:, :n] + both[:, n:]
 
 
 def norm_stats(values):
@@ -133,7 +135,7 @@
             [jnp.where(low, p, hi).astype(bf16), jnp.where(low, sq - hi, feat).astype(bf16)], 1
         )
 
-    feats = jnp.concatenate([features(q2), features(k2)], 0)
+    feats_q, feats_k = features(q2), features(k2)
 
     idx_row = jnp.concatenate([idx[h : h + 1] for h in range(heads)], 1)
     pick_t = (iota((2 * tokens, hm), 0) == idx_row).astype(f32).astype(bf16)
@@ -155,9 +157,6 @@
     extra = jnp.where(row8 == 7, -FAR, extra)
     pad = jnp.zeros((width - 8, hm), f32)
     right = jnp.concatenate([mark_t, -0.5 * own, -0.5 * own, extra, pad], 0).astype(bf16)
-    near = jnp.exp(sharp * mm(feats, right)).astype(bf16)
-    near_q, near_k = near[:tokens], near[tokens:]
-
     sq_hi = sq.astype(bf16).astype(f32)
     left = jnp.concatenate(
         [mark_t, sq_hi, sq - sq_hi, jnp.where(row8 < 4, mark_seg, 1.0), pad], 0
@@ -174,10 +173,20 @@
     widest = [jnp.max(sums[h], axis=1, keepdims=True) for h in hs]
     inv2 = [1.0 / (widest[h] * widest[h]) for h in hs]
     gram_wide = [wide_right(gram[h]) for h in hs]
+
+    def near_of(points):
+        return jnp.exp(sharp * mm(points, right)).astype(bf16)
+
+    chunk = tokens // 4
+    near_q_parts = []
+    rest_pair, grown_pair = [], []
+    wo_of = [wo[rows_of[h]] for h in hs]
+    rest = [eye - mm_wide(gram[h] * inv2[h], gram_wide[h]) for h in hs]
+    near_k = near_of(feats_k)
     summed_t = [mm(v_t[rows_of[h]], near_k[:, at[h]]) for h in hs]
+    sent_t = [both_parts(mm_tn, wo_of[h], summed_t[h]) for h in hs]
+    now = [mm_wide(sent_t[h], gram_wide[h]) * inv2[h] for h in hs]
     rests, wides, grown = [], [], []
-    rest = [eye - mm_wide(gram[h] * inv2[h], gram_wide[h]) for h in hs]
-    now = [mm_wide(summed_t[h], gram_wide[h]) * inv2[h] for h in hs]
     for step in range(NS_STEPS):
         wide = [wide_right(rest[h]) for h in hs]
         rests.append(rest)
@@ -186,16 +195,14 @@
         if step < NS_STEPS - 1:
             rest = [mm_wide(rest[h], wide[h]) for h in hs]
         now = [now[h] + mm_wide(now[h], wide[h]) for h in hs]
-
-    def spread_heads(parts):
-        zero = jnp.zeros_like(parts[0])
-        return jnp.concatenate(
-            [jnp.concatenate([parts[h] if g == h else zero for g in hs], 1) for h in hs], 0
-        )
-
-    mixed_t = spread_heads(now).astype(bf16)
-    att = (mm_nt(near_q, mixed_t) * out_scale).astype(bf16)
-    hidden = x + mm(att, wo) + vec(bo)
+        if len(near_q_parts) < 4:
+            lo = len(near_q_parts) * chunk
+            near_q_parts.append(near_of(feats_q[lo : lo + chunk]))
+        rest_pair.append([pair(*split(rests[step][h])) for h in hs])
+        grown_pair.append([grown[step][h].T.astype(bf16) for h in hs])
+    near_q = jnp.concatenate(near_q_parts, 0)
+    mixed_t = jnp.concatenate(now, 1).astype(bf16)
+    hidden = x + (mm_nt(near_q, mixed_t) * out_scale + vec(bo))
     xhat2, scale2 = norm_stats(hidden)
     normed2 = (xhat2 * vec(gain2) + vec(bias2)).astype(bf16)
     inner = mm(normed2, wup) + vec(bup)
@@ -205,6 +212,24 @@
     act = (0.5 * inner * (1.0 + th)).astype(bf16)
     layer_out = hidden + mm_nt(act, wdown_t) + vec(bdown)
 
+    gram_pair = [pair(*split(gram[h])) for h in hs]
+    sent_pair = [pair(*split(sent_t[h].T)) for h in hs]
+    kernel_inv = [kernel[h] * inv2[h] for h in hs]
+    widest_a = [(2.0 / widest[h]) * (eye - rests[0][h]) for h in hs]
+    widest_b = [(2.0 / widest[h]) * grown[0][h] for h in hs]
+    mark_ones = [
+        jnp.concatenate([mark16[:, at[h]], jnp.ones((16, marks), bf16)], 0) for h in hs
+    ]
+    top_part = []
+    for h in hs:
+        top = (sums[h] == widest[h]).astype(f32)
+        top = top * (1.0 / row_sum(top))
+        seen = kernel[h].astype(bf16)
+        along = jnp.broadcast_to(top, (16, marks)).astype(bf16)
+        top_part.append(
+            top * mm(mark_ones[h], seen)
+            + mm_nt(mark_ones[h], along)[:, :1] * mm(along, seen)[:1]
+        )
     d_act = mm(g16, wdown_t)
     slope = 0.5 * (1.0 + th) + 0.5 * inner * (1.0 - th * th) * (
         c * (1.0 + (3.0 * 0.044715) * inner2)
@@ -219,47 +244,73 @@
     g_bias2 = col_sum(d_norm2)
     d_hidden = g + norm_back(d_norm2, xhat2, scale2, vec(gain2))
     d_branch = d_hidden.astype(bf16)
-    g_wo = mm_tn(att, d_branch)
     g_bo = col_sum(d_branch.astype(f32))
-    d_att = mm_nt(d_branch, wo).astype(bf16)
-    d_att_t = mm_nt(wo, d_branch).astype(bf16)
-    d_mixed_t = (mm(d_att_t, near_q) * (own * out_scale)).astype(bf16)
-    pull_q = ((mm(d_att, mixed_t) * out_scale) * near_q.astype(f32)).astype(bf16)
-    back = [d_mixed_t[rows_of[h], at[h]].astype(f32) for h in hs]
+    d_sent_t = mm_tn(d_branch, near_q) * out_scale
+    back = [d_sent_t[:, at[h]] for h in hs]
+
+    def pulled(rows):
+        pull = ((mm(d_branch[rows], mixed_t) * out_scale) * near_q[rows].astype(f32)).astype(bf16)
+        return pull, stays(pull, q2[rows])
+
+    def stays(pull, p2):
+        both = mm(pull, both_m)
+        return sharp * (both[:, :width] - both[:, width:] * p2[:, :width].astype(f32))
+
+    both_m = jnp.concatenate([mark_t, own], 0).T.astype(bf16)
+    q_parts = []
     d_rest = None
     for step in reversed(range(NS_STEPS)):
-        outer = [sym_outer(back[h], grown[step][h]) for h in hs]
+        outer = [mm(grown_pair[step][h], back[h].astype(bf16)) for h in hs]
+        back = [back[h] + mm_wide(back[h], wides[step][h]) for h in hs]
         if d_rest is None:
             d_rest = outer
         else:
-            d_rest = [outer[h] + both_sides(d_rest[h], wides[step][h]) for h in hs]
-        back = [back[h] + mm_wide(back[h], wides[step][h]) for h in hs]
-    d_summed_t = spread_heads([mm_wide(back[h], gram_wide[h]) * inv2[h] for h in hs]).astype(bf16)
+            d_rest = [
+                mm_wide(d_rest[h], wides[step][h])
+                + wide_mm(rest_pair[step][h], wide_right(d_rest[h]))
+                + outer[h]
+                for h in hs
+            ]
+        if len(q_parts) < 4:
+            lo = len(q_parts) * chunk
+            q_parts.append(pulled(slice(lo, lo + chunk)))
+    pull_q = jnp.concatenate([p for p, _ in q_parts], 0)
+    stay_q = [s for _, s in q_parts]
+    left_now = [mm_wide(jnp.concatenate([back[h], d_rest[h]], 0), gram_wide[h]) for h in hs]
+    d_start = [left_now[h][:width] * inv2[h] for h in hs]
+    d_summed = [both_parts(mm, wo_of[h], d_start[h]).astype(bf16) for h in hs]
+    none = jnp.zeros((size, marks), bf16)
+    d_summed_t = jnp.concatenate(
+        [jnp.concatenate([d_summed[h] if g == h else none for g in hs], 1) for h in hs], 0
+    )
+    d_gram = [
+        wide_mm(
+            pair(sent_pair[h], -gram_pair[h]),
+            jnp.concatenate([wide_right(back[h]), wide_right(d_rest[h])], 0),
+        )
+        - left_now[h][width:]
+        for h in hs
+    ]
+    pull_k = (mm(v, d_summed_t) * near_k.astype(f32)).astype(bf16)
     gram_parts = []
     for h in hs:
-        d_gram = inv2[h] * (
-            sym_outer(back[h], summed_t[h]) - both_sides(d_rest[h], gram_wide[h])
-        )
-        d_widest = (2.0 / widest[h]) * (
-            total_of(d_rest[h] * (eye - rests[0][h])) - total_of(back[h] * grown[0][h])
-        )
-        top = (sums[h] == widest[h]).astype(f32)
-        weighted = (d_gram + top * (d_widest / row_sum(top))) * kernel[h]
-        weighted = (0.5 * (weighted + weighted.T)).astype(bf16)
-        lhs = jnp.concatenate([mark16[:, at[h]], jnp.ones((16, marks), bf16)], 0)
-        gram_parts.append(2.0 * mm(lhs, weighted))
+        d_widest = total_of(d_rest[h] * widest_a[h]) - total_of(back[h] * widest_b[h])
+        weighted = ((d_gram[h] + d_gram[h].T) * kernel_inv[h]).astype(bf16)
+        gram_parts.append(mm(mark_ones[h], weighted) + d_widest * top_part[h])
     gram_part = jnp.concatenate(gram_parts, 1)
-    pull_k = (mm(v, d_summed_t) * near_k.astype(f32)).astype(bf16)
-    dv = mm_nt(near_k, d_summed_t).astype(bf16)
     pulls = jnp.concatenate([pull_q, pull_k], 0)
     tok_part = mm(jnp.concatenate([qk_t, jnp.ones((16, 2 * tokens), bf16)], 0), pulls)
     both_part = tok_part + gram_part
     d_mark_t = (both_part[:width] - mark_t * both_part[width : width + 1]) * own
-    onto = jnp.concatenate([mark16, d_mark_t.astype(bf16)], 1)
-    moved = mm_nt(jnp.concatenate([pulls, pick_t], 1), onto)
-    weight = mm_nt(pulls, own.astype(bf16))
-    dq = (sharp * (moved[:tokens] - weight[:tokens] * q2[:, :width].astype(f32))).astype(bf16)
-    dk = (sharp * (moved[tokens:] - weight[tokens:] * k2[:, :width].astype(f32))).astype(bf16)
+    stay_k = [stays(pull_k[lo : lo + chunk], k2[lo : lo + chunk]) for lo in range(0, tokens, chunk)]
+    stay = jnp.concatenate(stay_q + stay_k, 0)
+    g_wo = jnp.concatenate(
+        [mm_nt(summed_t[h].astype(bf16), d_start[h].astype(bf16)) for h in hs], 0
+    )
+    dv = mm_nt(near_k, d_summed_t).astype(bf16)
+    moved = mm_nt(pick_t, d_mark_t.astype(bf16))
+    dq = (stay[:tokens] + sharp * moved[:tokens]).astype(bf16)
+    dk = (stay[tokens:] + sharp * moved[tokens:]).astype(bf16)
     d_normed = mm_nt(dq, wq) + mm_nt(dk, wk) + mm_nt(dv, wv)
     g_wq = mm_tn(normed, dq)
     g_wk = mm_tn(normed, dk)
@@ -270,9 +321,6 @@
     g_gain1 = col_sum(d_normed * xhat1)
     g_bias1 = col_sum(d_normed)
     grad_in = d_hidden + norm_back(d_normed, xhat1, scale1, vec(gain1))
-
-    def pair(a, b):
-        return jnp.concatenate([a, b], 1)
 
     vecs = [
         g_bup,
@@ -287,12 +335,22 @@
     return pair(layer_out, grad_in).astype(bf16), grads
 
 
-def read_params(refs):
-    return tuple(r[...] if len(r.shape) == 2 else r[...].reshape(1, -1) for r in refs)
-
-
-def main_kernel(tok_block, blk_ref, idx_ref, *refs):
-    params, (out_ref, keep_ref, send_ref) = refs[:16], refs[16:]
+MATRICES = (2, 4, 6, 8, 12, 14)
+VECTORS = (0, 1, 3, 5, 7, 9, 10, 11, 13, 15)
+
+
+def read_params(mats, vec_ref):
+    par = [None] * 16
+    for i, ref in zip(MATRICES, mats):
+        par[i] = ref[...]
+    for row, i in enumerate(VECTORS):
+        wide = par[12].shape[1] if i == 13 else par[2].shape[0]
+        par[i] = vec_ref[row : row + 1, :wide]
+    return tuple(par)
+
+
+def main_kernel(tok_block, blk_ref, idx_ref, vec_ref, *refs):
+    mats, (out_ref, keep_ref, send_ref) = refs[:6], refs[6:]
     blocks = blk_ref.shape[0]
     tokens = blocks * tok_block
     row = jnp.minimum(lax.axis_index("tok"), idx_ref.shape[0] - 1)
@@ -302,7 +360,7 @@
     onehot_t = jnp.concatenate(
         [jnp.where(half, ids[2 * j], ids[2 * j + 1]) for j in range(blocks // 2)], 1
     ).astype(bf16)
-    out, grads = row_work(xg, onehot_t, idx_ref[row], read_params(params))
+    out, grads = row_work(xg, onehot_t, idx_ref[row], read_params(mats, vec_ref))
     out_ref[...] = out.reshape(blocks, tok_block, 128)
     first = lax.rem(lax.axis_index("rows"), 2) == 0
     h = GRAD_ROWS // 2
@@ -310,8 +368,11 @@
     send_ref[...] = jnp.where(first, grads[h:], grads[:h])
 
 
-def pack_kernel(x_ref, g_ref, s_ref, out_ref):
+def pack_kernel(x_ref, g_ref, s_ref, *refs):
+    vecs, (out_ref, vec_ref) = refs[:-2], refs[-2:]
     rows, tok, width = x_ref.shape
+    for i, ref in enumerate(vecs):
+        vec_ref[i : i + 1, : ref.shape[0]] = ref[...].astype(f32).reshape(1, -1)
     out_ref[...] = jnp.zeros(out_ref.shape, out_ref.dtype)
     out_ref[:rows, :tok, :width] = x_ref[...]
     out_ref[:rows, :tok, width:] = g_ref[...]
@@ -379,8 +440,14 @@
     n_tok = lax.axis_size("tok")
     n_rows = lax.axis_size("rows")
     sds = jax.ShapeDtypeStruct
-    sent = call(
-        pack_kernel, sds((n_tok, tok + SEG_ROWS, 128), bf16), tokens_in, grad_out, segments, mib=56
+    sent, vecs = call(
+        pack_kernel,
+        (sds((n_tok, tok + SEG_ROWS, 128), bf16), sds((16, 128), f32)),
+        tokens_in,
+        grad_out,
+        segments,
+        *[params[i] for i in VECTORS],
+        mib=56,
     )
     got = lax.all_to_all(sent, "tok", 0, 0, tiled=True)
     h = GRAD_ROWS // 2
@@ -389,7 +456,8 @@
         (sds((n_tok, tok, 128), bf16), sds((h, 128), f32), sds((h, 128), f32)),
         got,
         landmark_index,
-        *params,
+        vecs,
+        *[params[i] for i in MATRICES],
         mib=12 * max(1, n_tok * tok // 512),
     )
     def from_xor(array, m):

time: 48.4 us -> 47.3 us (0.977)
  local copies, waits for them, and re-layouts: 0.66 us -> 0.08 us
  Pallas kernels: 10.8 us -> 10.3 us
    unnamed x34 -> x16, local copies, waits for them, and re-layouts: 0.63 us -> 0.05 us
    pallas_call x4, Pallas kernels: 10.8 us -> 10.3 us  [call(): pl.pallas_call(kernel, out_shape=outs, in_specs=[vmem] * len(args), out_s...]
where the time goes in v3:
time: 47.3 us; the launch traced here: 46.9 us
  blocking collectives  30.3 us (64%)
  Pallas kernels  10.3 us (22%)
  waiting for transfers between devices  3.49 us (7%)
  starting transfers between devices  1.93 us (4%)
  between operations  0.8 us (2%)
    all_to_all x1, blocking collectives, shards(): got = lax.all_to_all(back, 'tok', 0, 0, tiled=True)  15.3 us
    all_to_all x1, blocking collectives, shards(): got = lax.all_to_all(sent, 'tok', 0, 0, tiled=True)  15 us
    pallas_call x4, Pallas kernels, call(): pl.pallas_call(kernel, out_shape=outs, in_specs=[vmem] * len(args), out_s...  10.3 us
    ppermute x4, waiting for transfers between devices, from_xor(): return lax.ppermute(array, 'rows', [(i, i ^ m) for i in range(n_rows)])  3.49 us
    ppermute x4, starting transfers between devices, from_xor(): return lax.ppermute(array, 'rows', [(i, i ^ m) for i in range(n_rows)])  1.93 us
  transfers between devices with their start and end apart: 4, of which 3 were waited for; matrix products, arithmetic and copies ran while one was open for 0% of the time, Pallas kernels for 0%

profile of v3, /device:TPU:0, one launch (start us, length us, event | category | flops | bytes accessed | tf_op | source)
XLA Modules:
  0.0 46.9 jit_solution(12661698884498816779)
XLA Ops:
  0.7 1.9 %shard_map.331 = (bf16[8,80,128]{2,1,0:T(8,128)(2,1)}, f32[16,128]{1,0:T(8,128)}) custom-call(bf16[7,64,64]{2,1,0:T(8,128)(2,1)} %x_ref.1, bf16[7,64,64]{2,1,0:T(8,128)(2,1)} %g_ref.1, s32[7,64]{1,0:T(8,128)} %s_ref.1, bf16[64]{0:T(256)(128)(2,1)} %refs_0_.2, bf16[64]{0:T(256)(128)(2,1)} %refs_1_.2, bf16[64]{0:T(256)(128)(2,1)} %refs_2_.2, ...), custom_call_target="tpu_custom_call" | custom-call | tf_op jit(solution)/shard_map/pallas_call | solution.py:428
  2.5 0.0 copy-start
  2.5 0.0 copy-start.1
  2.5 0.0 copy-start.2
  2.5 0.0 copy-start.3
  2.6 0.0 copy-start.4
  2.6 0.0 copy-start.5
  2.6 0.0 copy-start.6
  2.6 0.0 copy-start.7
  2.6 15.0 %all_to_all.10.blk_ref = bf16[8,80,128]{2,1,0:T(8,128)(2,1)S(1)} all-to-all(bf16[8,80,128]{2,1,0:T(8,128)(2,1)} %get-tuple-element.42), channel_id=1, replica_groups=mesh['rows'=4,'tok'=8] {'tok'}, dimensions={0} | all-to-all | bytes 327680 | tf_op jit(solution)/shard_map/all_to_all | solution.py:452
  17.6 0.0 copy-done
  17.6 0.0 copy-done.1
  17.6 0.0 copy-done.2
  17.6 0.0 copy-done.3
  17.6 0.0 copy-done.4
  17.6 0.0 copy-done.5
  17.6 0.0 copy-done.6
  17.6 0.0 copy-done.7
  17.6 6.9 %shard_map.332 = (bf16[8,64,128]{2,1,0:T(8,128)(2,1)S(1)}, f32[136,128]{1,0:T(8,128)S(1)}, f32[136,128]{1,0:T(8,128)S(1)}) custom-call(bf16[8,80,128]{2,1,0:T(8,128)(2,1)S(1)} %all_to_all.10.blk_ref, s32[7,2,128]{2,1,0:T(2,128)S(1)} %copy-done.7, f32[16,128]{1,0:T(8,128)S(1)} %copy-done.6, bf16[64,64]{1,0:T(8,128)(2,1)S(1)} %copy-done, ...), custom_call_target="tpu_custom_call" | custom-call | tf_op jit(solution)/shard_map/pallas_call | solution.py:428
  24.5 0.1 collective-permute-start
  24.6 1.2 %collective-permute-done = f32[136,128]{1,0:T(8,128)S(1)} collective-permute-done((f32[136,128]{1,0:T(8,128)S(1)}, f32[136,128]{1,0:T(8,128)S(1)}, u32[]{:S(2)}, u32[]{:S(2)}) %collective-permute-start) | collective-permute-done | bytes 69664 | tf_op jit(solution)/shard_map/ppermute | solution.py:464
  25.9 15.3 %all_to_all.11.got_ref = bf16[8,200,128]{2,1,0:T(8,128)(2,1)S(1)} all-to-all(bf16[8,200,128]{2,1,0:T(8,128)(2,1)S(1)} %pad_maximum_fusion), channel_id=1, replica_groups=mesh['rows'=4,'tok'=8] {'tok'}, dimensions={0} | all-to-all | bytes 819200 | tf_op jit(solution)/shard_map/all_to_all | solution.py:468
  41.3 0.8 %shard_map.333 = (bf16[7,64,64]{2,1,0:T(8,128)(2,1)}, f32[7,64,64]{2,1,0:T(8,128)}, bf16[136,128]{1,0:T(8,128)(2,1)S(1)}) custom-call(bf16[8,200,128]{2,1,0:T(8,128)(2,1)S(1)} %all_to_all.11.got_ref), custom_call_target="tpu_custom_call" | custom-call | tf_op jit(solution)/shard_map/pallas_call | solution.py:428
  42.1 0.0 collective-permute-start.3
  42.1 1.5 %collective-permute-start.2 = (bf16[136,128]{1,0:T(8,128)(2,1)S(1)}, bf16[136,128]{1,0:T(8,128)(2,1)S(1)}, u32[]{:S(2)}, u32[]{:S(2)}) collective-permute-start(bf16[136,128]{1,0:T(8,128)(2,1)S(1)} %get-tuple-element.49.refs_0_), channel_id=1, source_target_pairs={{0,16},{8,24},{16,0},{24,8},{1,17},{9,25},{17,1},{25,9},{2,18},{10... | collective-permute-start | bytes 104456 | tf_op jit(solution)/shard_map/ppermute | solution.py:464
  43.6 0.3 collective-permute-start.1
  43.9 1.8 %collective-permute-done.3.refs_3_ = bf16[136,128]{1,0:T(8,128)(2,1)S(1)} collective-permute-done((bf16[136,128]{1,0:T(8,128)(2,1)S(1)}, bf16[136,128]{1,0:T(8,128)(2,1)S(1)}, u32[]{:S(2)}, u32[]{:S(2)}) %collective-permute-start.3) | collective-permute-done | bytes 34848 | tf_op jit(solution)/shard_map/ppermute | solution.py:464
  45.7 0.4 collective-permute-done.2.refs_2_
  46.2 0.0 collective-permute-done.1.refs_1_
  46.2 0.7 %shard_map.334 = (f32[64]{0:T(128)}, f32[64]{0:T(128)}, f32[64,64]{1,0:T(8,128)}, f32[64]{0:T(128)}, f32[64,64]{1,0:T(8,128)}, /*index=5*/f32[64]{0:T(128)}, f32...) custom-call(bf16[136,128]{1,0:T(8,128)(2,1)S(1)} %get-tuple-element., ...), custom_call_target="tpu_custom_call" | custom-call | tf_op jit(solution)/shard_map/pallas_call | solution.py:428
  (3 shorter events, 0.1 us)
Async XLA Ops:
  2.5 15.0 %copy-start = (bf16[64,64]{1,0:T(8,128)(2,1)S(1)}, bf16[64,64]{1,0:T(8,128)(2,1)}, u32[]{:S(2)}) copy-start(bf16[64,64]{1,0:T(8,128)(2,1)} %refs_0_.3) | copy-start | bytes 24580
  2.5 15.0 %copy-start.1 = (bf16[64,64]{1,0:T(8,128)(2,1)S(1)}, bf16[64,64]{1,0:T(8,128)(2,1)}, u32[]{:S(2)}) copy-start(bf16[64,64]{1,0:T(8,128)(2,1)} %refs_1_.3) | copy-start | bytes 24580
  2.5 15.0 %copy-start.2 = (bf16[64,64]{1,0:T(8,128)(2,1)S(1)}, bf16[64,64]{1,0:T(8,128)(2,1)}, u32[]{:S(2)}) copy-start(bf16[64,64]{1,0:T(8,128)(2,1)} %refs_2_.3) | copy-start | bytes 24580
  2.5 15.0 %copy-start.3 = (bf16[64,64]{1,0:T(8,128)(2,1)S(1)}, bf16[64,64]{1,0:T(8,128)(2,1)}, u32[]{:S(2)}) copy-start(bf16[64,64]{1,0:T(8,128)(2,1)} %refs_3_.3) | copy-start | bytes 24580
  2.6 15.0 %copy-start.4 = (bf16[64,128]{1,0:T(8,128)(2,1)S(1)}, bf16[64,128]{1,0:T(8,128)(2,1)}, u32[]{:S(2)}) copy-start(bf16[64,128]{1,0:T(8,128)(2,1)} %refs_4_.3) | copy-start | bytes 49156
  2.6 15.0 %copy-start.5 = (bf16[128,64]{0,1:T(8,128)(2,1)S(1)}, bf16[128,64]{0,1:T(8,128)(2,1)}, u32[]{:S(2)}) copy-start(bf16[128,64]{0,1:T(8,128)(2,1)} %param.37) | copy-start | bytes 49156
  2.6 15.0 %copy-start.6 = (f32[16,128]{1,0:T(8,128)S(1)}, f32[16,128]{1,0:T(8,128)}, u32[]{:S(2)}) copy-start(f32[16,128]{1,0:T(8,128)} %get-tuple-element.43.vec_ref) | copy-start | bytes 24580
  2.6 15.0 %copy-start.7 = (s32[7,2,128]{2,1,0:T(2,128)S(1)}, s32[7,2,128]{2,1,0:T(2,128)}, u32[]{:S(2)}) copy-start(s32[7,2,128]{2,1,0:T(2,128)} %idx_ref.1) | copy-start | bytes 21508
  24.5 1.3 %collective-permute-start = (f32[136,128]{1,0:T(8,128)S(1)}, f32[136,128]{1,0:T(8,128)S(1)}, u32[]{:S(2)}, u32[]{:S(2)}) collective-permute-start(f32[136,128]{1,0:T(8,128)S(1)} %get-tuple-element.46), channel_id=1, source_target_pairs={{0,8},{8,0},{16,24},{24,16},{1,9},{9,1},{17,25},{25,17},{2,10},{10... | collective-permute-start | bytes 208904 | tf_op jit(solution)/shard_map/ppermute | solution.py:464
  42.1 3.7 %collective-permute-start.3 = (bf16[136,128]{1,0:T(8,128)(2,1)S(1)}, bf16[136,128]{1,0:T(8,128)(2,1)S(1)}, u32[]{:S(2)}, u32[]{:S(2)}) collective-permute-start(bf16[136,128]{1,0:T(8,128)(2,1)S(1)} %get-tuple-element.49.refs_0_), channel_id=1, source_target_pairs={{0,24},{8,16},{16,8},{24,0},{1,25},{9,17},{17,9},{25,1},{2,26},{10... | collective-permute-start | bytes 104456 | tf_op jit(solution)/shard_map/ppermute | solution.py:464
  42.1 4.1 %collective-permute-start.2 = (bf16[136,128]{1,0:T(8,128)(2,1)S(1)}, bf16[136,128]{1,0:T(8,128)(2,1)S(1)}, u32[]{:S(2)}, u32[]{:S(2)}) collective-permute-start(bf16[136,128]{1,0:T(8,128)(2,1)S(1)} %get-tuple-element.49.refs_0_), channel_id=1, source_target_pairs={{0,16},{8,24},{16,0},{24,8},{1,17},{9,25},{17,1},{25,9},{2,18},{10... | collective-permute-start | bytes 104456 | tf_op jit(solution)/shard_map/ppermute | solution.py:464
  43.6 2.6 %collective-permute-start.1 = (bf16[136,128]{1,0:T(8,128)(2,1)S(1)}, bf16[136,128]{1,0:T(8,128)(2,1)S(1)}, u32[]{:S(2)}, u32[]{:S(2)}) collective-permute-start(bf16[136,128]{1,0:T(8,128)(2,1)S(1)} %get-tuple-element.49.refs_0_), channel_id=1, source_target_pairs={{0,8},{8,0},{16,24},{24,16},{1,9},{9,1},{17,25},{25,17},{2,10},{10... | collective-permute-start | bytes 104456 | tf_op jit(solution)/shard_map/ppermute | solution.py:464

commit v4 on v3

v4 whole, which is shorter than its diff:
```python
from functools import partial

import jax
import jax.numpy as jnp
from jax import lax
from jax.experimental import pallas as pl
from jax.experimental.pallas import tpu as pltpu
from jax.sharding import PartitionSpec as P


NS_STEPS = 6
EPS = 1e-05
RIDGE = 0.1
FAR = 640.0
SEG_ROWS = 16
GRAD_ROWS = 272

f32 = jnp.float32
bf16 = jnp.bfloat16


def mm(a, b):
    return lax.dot_general(a, b, (((1,), (0,)), ((), ())), preferred_element_type=f32)


def mm_nt(a, b):
    return lax.dot_general(a, b, (((1,), (1,)), ((), ())), preferred_element_type=f32)


def mm_tn(a, b):
    return lax.dot_general(a, b, (((0,), (0,)), ((), ())), preferred_element_type=f32)


def split(a):
    hi = a.astype(bf16)
    return hi, (a - hi.astype(f32)).astype(bf16)


def wide_right(b):
    hi, lo = split(b)
    return jnp.concatenate(
        [jnp.concatenate([hi, lo], 1), jnp.concatenate([hi, jnp.zeros_like(hi)], 1)], 0
    )


def mm_wide(a, wide):
    n = wide.shape[1] // 2
    both = mm(jnp.concatenate(split(a), 1), wide)
    return both[:, :n] + both[:, n:]


def row_sum(a):
    return jnp.sum(a, axis=1, keepdims=True)


def col_sum(a):
    return jnp.sum(a, axis=0, keepdims=True)


def total_of(a):
    return col_sum(row_sum(a))


def both_parts(product, a, b):
    n = b.shape[1]
    both = product(a, jnp.concatenate(split(b), 1))
    return both[:, :n] + both[:, n:]


def pair(a, b):
    return jnp.concatenate([a, b], 1)


def wide_mm(a_pair, wide):
    n = wide.shape[1] // 2
    both = mm(a_pair, wide)
    return both[:, :n] + both[:, n:]


def norm_stats(values):
    n = 1.0 / values.shape[0]
    centre = values - col_sum(values) * n
    scale = lax.rsqrt(col_sum(centre * centre) * n + EPS)
    return centre * scale, scale


def norm_back(d_norm, xhat, scale, gain):
    scaled = d_norm * gain
    n = 1.0 / scaled.shape[0]
    return scale * (scaled - col_sum(scaled) * n - xhat * (col_sum(scaled * xhat) * n))


def iota(shape, dim):
    return lax.broadcasted_iota(jnp.int32, shape, dim)


def row_work(xg, onehot_t, idx, par):
    (gain1, bias1, wq, bq, wk, bk, wv, bv, wo, bo, gain2, bias2, wup, bup, wdown_t, bdown) = par
    tokens = xg.shape[0]
    width = wq.shape[0]
    heads, marks = idx.shape
    size = width // heads
    sharp = size**-0.5
    out_scale = tokens**-0.5
    hm = heads * marks
    hs = range(heads)
    at = [slice(h * marks, (h + 1) * marks) for h in hs]
    rows_of = [slice(h * size, (h + 1) * size) for h in hs]
    chunk = tokens // 4
    chunks = [slice(lo, lo + chunk) for lo in range(0, tokens, chunk)]

    xg_t = xg.astype(f32).T
    x_t, g_t = xg_t[:width], xg_t[width:]
    g16_t = g_t.astype(bf16)
    wqkv = jnp.concatenate([wq, wk, wv], 1)
    wqkv_t = wqkv.astype(f32).T.astype(bf16)
    xhat1, scale1 = norm_stats(x_t)
    normed_t = (xhat1 * gain1 + bias1).astype(bf16)
    qkv_t = mm(wqkv_t, normed_t) + jnp.concatenate([bq, bk, bv], 0)
    qkv16_t = qkv_t.astype(bf16)
    q_t, k_t, v_t = (qkv16_t[i * width : (i + 1) * width] for i in range(3))
    seg_rows = jnp.where(
        (iota(onehot_t.shape, 0) >= 4) & (iota(onehot_t.shape, 0) < 8), 1.0, onehot_t.astype(f32)
    )
    seg_rows = jnp.concatenate(
        [seg_rows, jnp.zeros((width - SEG_ROWS, tokens), f32)], 0
    ).astype(bf16)

    def features(p_t):
        p = p_t.astype(f32)
        sq = p * p
        hi = sq.astype(bf16)
        return jnp.concatenate([p_t, hi, (sq - hi.astype(f32)).astype(bf16), seg_rows], 0)

    feats_q, feats_k = features(q_t), features(k_t)

    idx_row = jnp.concatenate([idx[h : h + 1] for h in hs], 1)
    pick_t = (iota((2 * tokens, hm), 0) == idx_row).astype(f32).astype(bf16)
    qk_t = jnp.concatenate([q_t, k_t], 1)
    seg2 = jnp.concatenate([onehot_t, onehot_t], 1)
    picked = mm(jnp.concatenate([qk_t, seg2], 0), pick_t)
    own = ((iota((width, hm), 0) // size) == (iota((width, hm), 1) // marks)).astype(f32)
    mark_t = picked[:width] * own
    mark_seg = picked[width : width + 8]
    sq = mark_t * mark_t
    half = -0.5 * col_sum(sq)
    half_hi = half.astype(bf16).astype(f32)
    half_mid = (half - half_hi).astype(bf16).astype(f32)
    half_lo = half - half_hi - half_mid
    row8 = iota((8, hm), 0)
    extra = jnp.where(row8 < 4, mark_seg * FAR, 0.0)
    extra = jnp.where(row8 == 4, half_hi, extra)
    extra = jnp.where(row8 == 5, half_mid, extra)
    extra = jnp.where(row8 == 6, half_lo, extra)
    extra = jnp.where(row8 == 7, -FAR, extra)
    pad = jnp.zeros((width - 8, hm), f32)
    right_m = jnp.concatenate([mark_t, -0.5 * own, -0.5 * own, extra, pad], 0).T.astype(bf16)
    sq_hi = sq.astype(bf16).astype(f32)
    left = jnp.concatenate(
        [mark_t, sq_hi, sq - sq_hi, jnp.where(row8 < 4, mark_seg, 1.0), pad], 0
    ).astype(bf16)
    mark16 = mark_t.astype(bf16)

    def near_of(points):
        return jnp.exp(sharp * mm(right_m, points)).astype(bf16)

    eye = (iota((marks, marks), 0) == iota((marks, marks), 1)).astype(f32)
    kernel = [jnp.exp(sharp * mm(right_m[at[h]], left[:, at[h]])) for h in hs]
    gram = [kernel[h] + RIDGE * eye for h in hs]
    sums = [col_sum(gram[h]) for h in hs]
    widest = [jnp.max(sums[h], axis=1, keepdims=True) for h in hs]
    inv2 = [1.0 / (widest[h] * widest[h]) for h in hs]
    gram_wide = [wide_right(gram[h]) for h in hs]
    wo_of = [wo[rows_of[h]] for h in hs]
    rest = [eye - mm_wide(gram[h] * inv2[h], gram_wide[h]) for h in hs]
    v_tok = v_t.astype(f32).T.astype(bf16)
    rests, wides = [rest], []
    near_k, near_q, near_q_tok, summed_t, sent_t, grown = [], [], [], [], [], []
    rest_pair, grown_pair = [], []

    def add_near_k(i):
        half = tokens // 2
        near_k.append(near_of(feats_k[:, i * half : (i + 1) * half]))

    def add_near_q(i):
        near_q.append(near_of(feats_q[:, chunks[i]]))
        near_q_tok.append(near_q[-1].T)

    def add_sums():
        near_k[:] = [jnp.concatenate(near_k, 1)]
        both = mm(near_k[0], v_tok).T
        summed_t.extend(both[rows_of[h], at[h]] for h in hs)

    def add_sent():
        sent_t.extend(both_parts(mm_tn, wo_of[h], summed_t[h]) for h in hs)
        grown.append([mm_wide(sent_t[h], gram_wide[h]) * inv2[h] for h in hs])

    def two_steps(step):
        nxt = rests[step + 1]
        return [rests[step][h] + nxt[h] + mm_wide(rests[step][h], wides[step + 1][h]) for h in hs]

    def grown_by(now, wide):
        return [now[h] + mm_wide(now[h], wide[h]) for h in hs]

    def widen(both):
        return [wide_right(both[h]) for h in hs]

    def add_pairs(step):
        rest_pair.append([pair(*split(rests[step][h])) for h in hs])

    def next_rest():
        wides.append(widen(rests[-1]))
        if len(rests) < NS_STEPS:
            rests.append([mm_wide(rests[-1][h], wides[-1][h]) for h in hs])

    add_near_k(0)
    next_rest()
    add_near_k(1)
    next_rest()
    twice = [widen(two_steps(0))]
    add_sums()
    next_rest()
    add_pairs(0)
    add_near_q(0)
    add_sent()
    next_rest()
    twice.append(widen(two_steps(2)))
    add_pairs(1)
    add_near_q(1)
    grown.extend([None] * NS_STEPS)
    grown[2] = grown_by(grown[0], twice[0])
    next_rest()
    add_near_q(2)
    grown[4] = grown_by(grown[2], twice[1])
    next_rest()
    grown[5] = grown_by(grown[4], wides[4])
    add_near_q(3)
    grown[6] = grown_by(grown[5], wides[5])
    near_k, now = near_k[0], grown[-1]
    near_q = jnp.concatenate(near_q, 1)
    near_q_tok = jnp.concatenate(near_q_tok, 0)
    mixed_t = jnp.concatenate(now, 1).astype(bf16)
    hidden = x_t + (mm(mixed_t, near_q) * out_scale + bo)
    twice.append(widen(two_steps(4)))
    inverse = [gram[h] * inv2[h] for h in hs]
    for wide in twice:
        inverse = grown_by(inverse, wide)
    inverse_wide = widen(inverse)
    grown[1] = grown_by(grown[0], wides[0])
    grown[3] = grown_by(grown[2], wides[2])
    for step in range(2, NS_STEPS):
        add_pairs(step)
    grown_pair = [[grown[step][h].T.astype(bf16) for h in hs] for step in range(NS_STEPS)]
    wup_t = wup.astype(f32).T.astype(bf16)
    d_act = mm_tn(wdown_t, g16_t)
    xhat2, scale2 = norm_stats(hidden)
    normed2_t = (xhat2 * gain2 + bias2).astype(bf16)
    inner = mm(wup_t, normed2_t) + bup
    c = (2.0 / jnp.pi) ** 0.5
    inner2 = inner * inner
    th = jnp.tanh(c * inner * (1.0 + 0.044715 * inner2))
    act = (0.5 * inner * (1.0 + th)).astype(bf16)

    slope = 0.5 * (1.0 + th) + 0.5 * inner * (1.0 - th * th) * (
        c * (1.0 + (3.0 * 0.044715) * inner2)
    )
    d_inner = (d_act * slope).astype(bf16)
    d_norm2 = mm(wup, d_inner)
    layer_out = hidden + (mm(wdown_t, act) + bdown)
    d_hidden = g_t + norm_back(d_norm2, xhat2, scale2, gain2)
    d_branch = d_hidden.astype(bf16)
    d_sent_t = mm(d_branch, near_q_tok) * out_scale
    back = [d_sent_t[:, at[h]] for h in hs]

    gram_pair = [pair(*split(gram[h])) for h in hs]
    sent_pair = [pair(*split(sent_t[h].T)) for h in hs]
    kernel_inv = [kernel[h] * inv2[h] for h in hs]
    widest_a = [(2.0 / widest[h]) * (eye - rests[0][h]) for h in hs]
    widest_b = [(2.0 / widest[h]) * grown[0][h] for h in hs]
    mark_both = jnp.concatenate([mark16, own.astype(bf16)], 0)
    mark_ones = [
        jnp.concatenate([mark16[:, at[h]], jnp.ones((16, marks), bf16)], 0) for h in hs
    ]
    top_part = []
    for h in hs:
        top = (sums[h] == widest[h]).astype(f32)
        top = top * (1.0 / row_sum(top))
        seen = kernel[h].astype(bf16)
        along = jnp.broadcast_to(top, (16, marks)).astype(bf16)
        top_part.append(
            top * mm(mark_ones[h], seen)
            + mm_nt(mark_ones[h], along)[:, :1] * mm(along, seen)[:1]
        )
    mixed_m = mixed_t.astype(f32).T.astype(bf16)
    q_tok = q_t.astype(f32).T.astype(bf16)
    k_tok = k_t.astype(f32).T.astype(bf16)
    ones_tok = jnp.ones((tokens, width), bf16)
    d_start = [mm_wide(back[h], inverse_wide[h]) for h in hs]
    d_summed = [both_parts(mm, wo_of[h], d_start[h]) for h in hs]
    none = jnp.zeros((size, marks), f32)
    d_summed_t = jnp.concatenate(
        [jnp.concatenate([d_summed[h] if g == h else none for g in hs], 1) for h in hs], 0
    )
    d_summed_m = d_summed_t.T.astype(bf16)
    def stays(pull, p_t):
        both = mm(mark_both, pull)
        return sharp * (both[:width] - both[width:] * p_t.astype(f32))

    pulls_q, toks = [], []

    def pull_some(i):
        now_at = chunks[i]
        pull = mm(mixed_m, d_branch[:, now_at]) * out_scale
        pulls_q.append((pull * near_q[:, now_at].astype(f32)).astype(bf16))

    def pull_rest():
        pull = mm(d_summed_m, v_t)
        pulls_q.append((pull * near_k.astype(f32)).astype(bf16))

    def add_tok(pull, tok):
        toks.append(mm(pull, pair(tok, ones_tok)))

    def add_tok_q():
        pulls_q[:4] = [jnp.concatenate(pulls_q[:4], 1)]
        add_tok(pulls_q[0], q_tok)

    def add_tok_k():
        add_tok(pulls_q[1], k_tok)

    beside = [
        [partial(pull_some, 0), partial(pull_some, 1)],
        [partial(pull_some, 2), partial(pull_some, 3)],
        [add_tok_q],
        [pull_rest],
        [add_tok_k],
        [],
    ]
    d_rest = None
    for step in reversed(range(NS_STEPS)):
        outer = [mm(grown_pair[step][h], back[h].astype(bf16)) for h in hs]
        back = [back[h] + mm_wide(back[h], wides[step][h]) for h in hs]
        if d_rest is None:
            d_rest = outer
        else:
            d_rest = [
                mm_wide(d_rest[h], wides[step][h])
                + wide_mm(rest_pair[step][h], wide_right(d_rest[h]))
                + outer[h]
                for h in hs
            ]
        for work in beside[NS_STEPS - 1 - step]:
            work()
    pull_q, pull_k = pulls_q
    d_gram = [
        wide_mm(sent_pair[h], wide_right(back[h]))
        - mm_wide(d_rest[h], gram_wide[h])
        - wide_mm(gram_pair[h], wide_right(d_rest[h]))
        for h in hs
    ]
    tok_both = (toks[0] + toks[1]).T
    tok_t, tok_sum = tok_both[:width], tok_both[width : width + 1]
    stay_q, stay_k = stays(pull_q, q_t), stays(pull_k, k_t)
    gram_part = []
    for h in hs:
        d_widest = total_of(d_rest[h] * widest_a[h]) - total_of(back[h] * widest_b[h])
        weighted = ((d_gram[h] + d_gram[h].T) * kernel_inv[h]).astype(bf16)
        gram_part.append(mm(mark_ones[h], weighted) + d_widest * top_part[h])
    gram_part = jnp.concatenate(gram_part, 1)
    d_mark_t = (
        (tok_t + gram_part[:width] - mark_t * (tok_sum + gram_part[width : width + 1])) * own
    ).astype(bf16)
    idx_col = jnp.broadcast_to(idx_row.astype(f32), (8, hm)).T[:, :1].astype(jnp.int32)
    pick_m = (iota((hm, 2 * tokens), 1) == idx_col).astype(f32).astype(bf16)
    moved = mm(d_mark_t, pick_m)
    dq = (stay_q + sharp * moved[:, :tokens]).astype(bf16)
    dk = (stay_k + sharp * moved[:, tokens:]).astype(bf16)
    dv = mm(d_summed_t.astype(bf16), near_k).astype(bf16)
    dqkv = jnp.concatenate([dq, dk, dv], 0)
    d_normed = mm(wqkv, dqkv)
    grad_in = d_hidden + norm_back(d_normed, xhat1, scale1, gain1)
    out = jnp.concatenate([layer_out, grad_in], 0).T.astype(bf16)

    ones16 = jnp.ones((16, tokens), bf16)
    g_down = mm_nt(g16_t, act)
    g_up = mm_nt(jnp.concatenate([normed2_t, ones16], 0), d_inner)
    g_qkv = mm_nt(jnp.concatenate([normed_t, ones16], 0), dqkv)
    g_bias = mm_nt(ones16, jnp.concatenate([g16_t, d_branch], 0))
    g_wo = jnp.concatenate(
        [mm_nt(summed_t[h].astype(bf16), d_start[h].astype(bf16)) for h in hs], 0
    )
    columns = [
        row_sum(d_normed * xhat1),
        row_sum(d_normed),
        row_sum(d_norm2 * xhat2),
        row_sum(d_norm2),
    ]
    lane = iota((width, 128), 1)
    norms = sum(jnp.where(lane == i, col, 0.0) for i, col in enumerate(columns)).T[:8]
    g_bqkv = g_qkv[width : width + 1]
    vecs = [
        g_up[width : width + 1],
        pair(g_bias[:1, :width], g_bqkv[:, :width]),
        g_bqkv[:, width:],
        pair(g_bias[:1, width:], norms[0:1]),
        pair(norms[1:2], norms[2:3]),
        pair(norms[3:4], jnp.zeros((1, width), f32)),
        jnp.zeros((GRAD_ROWS - 262, 128), f32),
    ]
    grads = jnp.concatenate(
        [
            g_up[:width],
            g_down[:width],
            g_qkv[:width, : 2 * width],
            pair(g_qkv[:width, 2 * width :], g_wo),
        ]
        + vecs,
        0,
    )
    return out, grads


MATRICES = (2, 4, 6, 8, 12, 14)
VECTORS = (0, 1, 3, 5, 7, 9, 10, 11, 13, 15)


def read_params(mats, vec_cols):
    par = [None] * 16
    for i, ref in zip(MATRICES, mats):
        par[i] = ref[...]
    for row, i in enumerate(VECTORS):
        wide = par[12].shape[1] if i == 13 else par[2].shape[0]
        par[i] = vec_cols[:wide, row : row + 1]
    return tuple(par)


def main_kernel(tok_block, blk_ref, idx_ref, vec_ref, *refs):
    mats, (out_ref, keep_ref, send_ref) = refs[:6], refs[6:]
    vec_cols = vec_ref[...].T
    blocks = blk_ref.shape[0]
    tokens = blocks * tok_block
    row = jnp.minimum(lax.axis_index("tok"), idx_ref.shape[0] - 1)
    xg = blk_ref[:, :tok_block, :].reshape(tokens, 128)
    ids = blk_ref[:, tok_block:, :].astype(f32)
    half = iota((SEG_ROWS, 128), 1) < tok_block
    onehot_t = jnp.concatenate(
        [jnp.where(half, ids[2 * j], ids[2 * j + 1]) for j in range(blocks // 2)], 1
    ).astype(bf16)
    out, grads = row_work(xg, onehot_t, idx_ref[row], read_params(mats, vec_cols))
    out_ref[...] = out.reshape(blocks, tok_block, 128)
    first = lax.rem(lax.axis_index("rows"), 2) == 0
    h = GRAD_ROWS // 2
    keep_ref[...] = jnp.where(first, grads[:h], grads[h:])
    send_ref[...] = jnp.where(first, grads[h:], grads[:h])


def pack_kernel(xg_ref, s_ref, *refs):
    vecs, (out_ref, vec_ref) = refs[:-2], refs[-2:]
    rows, tok, width = xg_ref.shape
    out_ref[:rows, :tok, :] = xg_ref[...]
    out_ref[rows:] = jnp.zeros((out_ref.shape[0] - rows,) + out_ref.shape[1:], bf16)
    seg = s_ref[...]
    seg = jnp.concatenate([seg, seg], 1)
    for r in range(rows):
        ids = jnp.broadcast_to(seg[r : r + 1], (SEG_ROWS, width))
        out_ref[r, tok:, :] = (ids == iota((SEG_ROWS, width), 0)).astype(f32).astype(bf16)
    for i, ref in enumerate(vecs):
        vec_ref[i : i + 1, : ref.shape[0]] = ref[...].astype(f32).reshape(1, -1)


def sum_kernel(tok, got_ref, sum_ref):
    total = got_ref[0, tok:, :].astype(f32)
    for j in range(1, got_ref.shape[0]):
        total = total + got_ref[j, tok:, :].astype(f32)
    sum_ref[...] = total.astype(bf16)


def rows_kernel(got_ref, out_ref, grad_ref):
    rows, tok, width = out_ref.shape
    out_ref[...] = got_ref[:rows, :tok, :width]
    grad_ref[...] = got_ref[:rows, :tok, width:].astype(f32)


def unpack_kernel(n_parts, *refs):
    parts, outs = refs[:n_parts], refs[n_parts:]
    halves = [
        sum([p[...].astype(f32) for p in parts[core + 2 :: 2]], parts[core][...].astype(f32))
        for core in range(2)
    ]
    first = lax.rem(lax.axis_index("rows"), 2) == 0
    a = jnp.where(first, halves[0], halves[1])
    b = jnp.where(first, halves[1], halves[0])
    whole = jnp.concatenate([a, b], 0)
    (gain1, bias1, wq, bq, wk, bk, wv, bv, wo, bo, gain2, bias2, wup, bup, wdown_t, bdown) = outs
    wup[...] = whole[0:64]
    wdown_t[...] = whole[64:128]
    wq[...] = whole[128:192, :64]
    wk[...] = whole[128:192, 64:]
    wv[...] = whole[192:256, :64]
    wo[...] = whole[192:256, 64:]
    bup[...] = whole[256]
    bdown[...] = whole[257, :64]
    bq[...] = whole[257, 64:]
    bk[...] = whole[258, :64]
    bv[...] = whole[258, 64:]
    bo[...] = whole[259, :64]
    gain1[...] = whole[259, 64:]
    bias1[...] = whole[260, :64]
    gain2[...] = whole[260, 64:]
    bias2[...] = whole[261, :64]


def call(kernel, outs, *args, mib=12):
    vmem = pl.BlockSpec(memory_space=pltpu.VMEM)
    return pl.pallas_call(
        kernel,
        out_shape=outs,
        in_specs=[vmem] * len(args),
        out_specs=jax.tree.map(lambda _: vmem, outs),
        compiler_params=pltpu.CompilerParams(vmem_limit_bytes=mib * 1024 * 1024),
    )(*args)


def shards(tokens_in, segments, landmark_index, *rest):
    params, grad_out = rest[:14] + (rest[14].T, rest[15]), rest[16]
    rows, tok, width = tokens_in.shape
    n_tok = lax.axis_size("tok")
    n_rows = lax.axis_size("rows")
    sds = jax.ShapeDtypeStruct
    sent, vecs = call(
        pack_kernel,
        (sds((n_tok, tok + SEG_ROWS, 128), bf16), sds((16, 128), f32)),
        jnp.concatenate([tokens_in, grad_out], 2),
        segments,
        *[params[i] for i in VECTORS],
        mib=4,
    )
    got = lax.all_to_all(sent, "tok", 0, 0, tiled=True)
    h = GRAD_ROWS // 2
    out, keep, send = call(
        partial(main_kernel, tok),
        (sds((n_tok, tok, 128), bf16), sds((h, 128), f32), sds((h, 128), f32)),
        got,
        landmark_index,
        vecs,
        *[params[i] for i in MATRICES],
        mib=12 * max(1, n_tok * tok // 512),
    )
    def from_xor(array, m):
        return lax.ppermute(array, "rows", [(i, i ^ m) for i in range(n_rows)])

    total = (keep + from_xor(send, 1)).astype(bf16)
    back = jnp.concatenate([out, jnp.broadcast_to(total, (n_tok, h, 128))], 1)
    got = lax.all_to_all(back, "tok", 0, 0, tiled=True)
    mine = call(partial(sum_kernel, tok), sds((h, 128), bf16), got)
    parts = [mine] + [from_xor(mine, m) for m in range(1, n_rows)]
    layer_out, grad_input = call(
        rows_kernel, (sds((rows, tok, width), bf16), sds((rows, tok, width), f32)), got
    )
    sums = call(
        partial(unpack_kernel, n_rows), tuple(sds(p.shape, f32) for p in params), *parts
    )
    sums = sums[:14] + (sums[14].T,) + sums[15:]
    return (layer_out, grad_input) + tuple(sums)


def solution(mesh):
    split3 = P("rows", "tok", None)
    return jax.shard_map(
        shards,
        mesh=mesh,
        in_specs=(split3, P("rows", "tok"), P("rows", None, None)) + (P(),) * 16 + (split3,),
        out_specs=(split3, split3) + (P(),) * 16,
        check_vma=False,
    )
```

time: 47.3 us -> 45.1 us (0.953)
  Pallas kernels: 10.3 us -> 7.82 us
  other arithmetic: 0.04 us -> 1.17 us
  waiting for transfers between devices: 3.49 us -> 2.71 us
    pallas_call x4 -> x5, Pallas kernels: 10.3 us -> 7.82 us  [call(): pl.pallas_call(kernel, out_shape=outs, in_specs=[vmem] * len(args), out_s...]
    concatenate x0 -> x1, other arithmetic: none -> 1.12 us  [shards(): jnp.concatenate([tokens_in, grad_out], 2)]
    ppermute x4, waiting for transfers between devices: 3.49 us -> 2.71 us  [from_xor(): return lax.ppermute(array, 'rows', [(i, i ^ m) for i in range(n_rows)])]
  transfers between devices with their start and end apart: 4 -> 4, of which waited for: 3 -> 3; matrix products, arithmetic and copies ran while one was open for 0% -> 0% of each run, Pallas kernels for 0% -> 2%
where the time goes in v4:
time: 45.1 us; the launch traced here: 44.9 us
  blocking collectives  30.1 us (67%)
  Pallas kernels  7.82 us (17%)
  waiting for transfers between devices  2.71 us (6%)
  starting transfers between devices  1.99 us (4%)
  other arithmetic  1.17 us (3%)
  between operations  0.97 us (2%)
    all_to_all x1, blocking collectives, shards(): got = lax.all_to_all(back, 'tok', 0, 0, tiled=True)  15.3 us
    all_to_all x1, blocking collectives, shards(): got = lax.all_to_all(sent, 'tok', 0, 0, tiled=True)  14.7 us
    pallas_call x5, Pallas kernels, call(): pl.pallas_call(kernel, out_shape=outs, in_specs=[vmem] * len(args), out_s...  7.82 us
    ppermute x4, waiting for transfers between devices, from_xor(): return lax.ppermute(array, 'rows', [(i, i ^ m) for i in range(n_rows)])  2.71 us
    ppermute x4, starting transfers between devices, from_xor(): return lax.ppermute(array, 'rows', [(i, i ^ m) for i in range(n_rows)])  1.99 us
    concatenate x1, other arithmetic, shards(): jnp.concatenate([tokens_in, grad_out], 2)  1.12 us
  transfers between devices with their start and end apart: 4, of which 3 were waited for; matrix products, arithmetic and copies ran while one was open for 0% of the time, Pallas kernels for 2%

profile of v4, /device:TPU:0, one launch (start us, length us, event | category | flops | bytes accessed | tf_op | source)
XLA Modules:
  0.0 44.9 jit_solution(8928881921548661847)
XLA Ops:
  0.7 0.0 copy-start.17
  0.7 0.0 copy-start.16
  0.7 0.0 copy-start.15
  0.7 0.0 copy-start.14
  0.7 0.0 copy-start.13
  0.7 0.0 copy-start.12
  0.7 0.0 copy-start.11
  0.7 0.0 copy-start.10
  0.7 0.0 copy-start.9
  0.8 0.0 copy-start.8
  0.8 0.0 copy-start.7
  0.8 1.1 %pad_maximum_fusion.1.xg_ref = bf16[7,64,128]{2,1,0:T(8,128)(2,1)S(1)} fusion(bf16[7,64,64]{2,1,0:T(8,128)(2,1)} %param.39, bf16[7,64,64]{2,1,0:T(8,128)(2,1)} %param.20), kind=kLoop, calls=%fused_computation.1 | loop fusion | flops 229376 | bytes 229376 | tf_op jit(solution)/shard_map/concatenate | solution.py:532
  1.9 0.0 copy-done.17
  1.9 0.0 copy-done.16
  1.9 0.0 copy-done.15
  1.9 0.0 copy-done.14
  1.9 0.0 copy-done.13
  1.9 0.0 copy-done.12
  2.0 0.0 copy-done.11
  2.0 0.0 copy-done.10
  2.0 0.0 copy-done.9
  2.0 0.0 copy-done.8
  2.0 0.0 copy-done.7
  2.0 0.1 shard_map.331
  2.1 0.0 copy-start.1
  2.1 0.0 copy-start.2
  2.1 0.0 copy-start.3
  2.1 0.0 copy-start.4
  2.1 0.0 copy-start.5
  2.2 0.0 copy-start.6
  2.2 14.7 %all_to_all.10.blk_ref = bf16[8,80,128]{2,1,0:T(8,128)(2,1)S(1)} all-to-all(bf16[8,80,128]{2,1,0:T(8,128)(2,1)S(1)} %get-tuple-element.41), channel_id=1, replica_groups=mesh['rows'=4,'tok'=8] {'tok'}, dimensions={0} | all-to-all | bytes 327680 | tf_op jit(solution)/shard_map/all_to_all | solution.py:537
  16.9 0.0 copy-done
  16.9 0.0 copy-done.1
  16.9 0.0 copy-done.2
  16.9 0.0 copy-done.3
  16.9 0.0 copy-done.4
  17.0 6.2 %shard_map.332 = (bf16[8,64,128]{2,1,0:T(8,128)(2,1)S(1)}, f32[136,128]{1,0:T(8,128)S(1)}, f32[136,128]{1,0:T(8,128)S(1)}) custom-call(bf16[8,80,128]{2,1,0:T(8,128)(2,1)S(1)} %all_to_all.10.blk_ref, s32[7,2,128]{2,1,0:T(2,128)S(1)} %copy-done.6, f32[16,128]{1,0:T(8,128)S(1)} %get-tuple-element.42.vec_ref, bf16[64,64]{1,0:T(8,128)(2,1)S(1)} %copy-done, ...), custom_call_target="tpu_custom_call" | custom-call | tf_op jit(solution)/shard_map/pallas_call | solution.py:514
  23.1 0.1 collective-permute-start
  23.2 1.2 %collective-permute-done = f32[136,128]{1,0:T(8,128)S(1)} collective-permute-done((f32[136,128]{1,0:T(8,128)S(1)}, f32[136,128]{1,0:T(8,128)S(1)}, u32[]{:S(2)}, u32[]{:S(2)}) %collective-permute-start) | collective-permute-done | bytes 69664 | tf_op jit(solution)/shard_map/ppermute | solution.py:549
  24.6 15.3 %all_to_all.11.got_ref = bf16[8,200,128]{2,1,0:T(8,128)(2,1)S(1)} all-to-all(bf16[8,200,128]{2,1,0:T(8,128)(2,1)S(1)} %pad_maximum_fusion), channel_id=1, replica_groups=mesh['rows'=4,'tok'=8] {'tok'}, dimensions={0} | all-to-all | bytes 819200 | tf_op jit(solution)/shard_map/all_to_all | solution.py:553
  39.9 0.1 collective-permute-start.3
  40.0 1.6 %collective-permute-start.2 = (bf16[136,128]{1,0:T(8,128)(2,1)S(1)}, bf16[136,128]{1,0:T(8,128)(2,1)S(1)}, u32[]{:S(2)}, u32[]{:S(2)}) collective-permute-start(bf16[136,128]{1,0:T(8,128)(2,1)S(1)} %shard_map.334.refs_0_), channel_id=1, source_target_pairs={{0,16},{8,24},{16,0},{24,8},{1,17},{9,25},{17,1},{25,9},{2,18},{10... | collective-permute-start | bytes 104456 | tf_op jit(solution)/shard_map/ppermute | solution.py:549
  41.6 0.3 collective-permute-start.1
  41.9 0.8 %shard_map.333 = (bf16[7,64,64]{2,1,0:T(8,128)(2,1)}, f32[7,64,64]{2,1,0:T(8,128)}) custom-call(bf16[8,200,128]{2,1,0:T(8,128)(2,1)S(1)} %all_to_all.11.got_ref), custom_call_target="tpu_custom_call" | custom-call | tf_op jit(solution)/shard_map/pallas_call | solution.py:514
  42.6 1.0 %collective-permute-done.3.refs_3_ = bf16[136,128]{1,0:T(8,128)(2,1)S(1)} collective-permute-done((bf16[136,128]{1,0:T(8,128)(2,1)S(1)}, bf16[136,128]{1,0:T(8,128)(2,1)S(1)}, u32[]{:S(2)}, u32[]{:S(2)}) %collective-permute-start.3) | collective-permute-done | bytes 34848 | tf_op jit(solution)/shard_map/ppermute | solution.py:549
  43.7 0.4 collective-permute-done.2.refs_2_
  44.1 0.0 collective-permute-done.1.refs_1_
  44.1 0.7 %shard_map.335 = (f32[64]{0:T(128)}, f32[64]{0:T(128)}, f32[64,64]{1,0:T(8,128)}, f32[64]{0:T(128)}, f32[64,64]{1,0:T(8,128)}, /*index=5*/f32[64]{0:T(128)}, f32...) custom-call(bf16[136,128]{1,0:T(8,128)(2,1)S(1)} %shard_map.334.refs, ...), custom_call_target="tpu_custom_call" | custom-call | tf_op jit(solution)/shard_map/pallas_call | solution.py:514
  (7 shorter events, 0.1 us)
Async XLA Ops:
  0.7 1.2 %copy-start.17 = (bf16[64]{0:T(256)(128)(2,1)S(1)}, bf16[64]{0:T(256)(128)(2,1)}, u32[]{:S(2)}) copy-start(bf16[64]{0:T(256)(128)(2,1)} %refs_9_.1) | copy-start | bytes 388
  0.7 1.2 %copy-start.16 = (bf16[128]{0:T(256)(128)(2,1)S(1)}, bf16[128]{0:T(256)(128)(2,1)}, u32[]{:S(2)}) copy-start(bf16[128]{0:T(256)(128)(2,1)} %refs_8_.1) | copy-start | bytes 772
  0.7 1.2 %copy-start.15 = (bf16[64]{0:T(256)(128)(2,1)S(1)}, bf16[64]{0:T(256)(128)(2,1)}, u32[]{:S(2)}) copy-start(bf16[64]{0:T(256)(128)(2,1)} %refs_7_.1) | copy-start | bytes 388
  0.7 1.2 %copy-start.14 = (bf16[64]{0:T(256)(128)(2,1)S(1)}, bf16[64]{0:T(256)(128)(2,1)}, u32[]{:S(2)}) copy-start(bf16[64]{0:T(256)(128)(2,1)} %refs_6_.1) | copy-start | bytes 388
  0.7 1.2 %copy-start.13 = (bf16[64]{0:T(256)(128)(2,1)S(1)}, bf16[64]{0:T(256)(128)(2,1)}, u32[]{:S(2)}) copy-start(bf16[64]{0:T(256)(128)(2,1)} %refs_5_.1) | copy-start | bytes 388
  0.7 1.2 %copy-start.12 = (bf16[64]{0:T(256)(128)(2,1)S(1)}, bf16[64]{0:T(256)(128)(2,1)}, u32[]{:S(2)}) copy-start(bf16[64]{0:T(256)(128)(2,1)} %refs_4_.2) | copy-start | bytes 388
  0.7 1.2 %copy-start.11 = (bf16[64]{0:T(256)(128)(2,1)S(1)}, bf16[64]{0:T(256)(128)(2,1)}, u32[]{:S(2)}) copy-start(bf16[64]{0:T(256)(128)(2,1)} %refs_3_.2) | copy-start | bytes 388
  0.7 1.2 %copy-start.10 = (bf16[64]{0:T(256)(128)(2,1)S(1)}, bf16[64]{0:T(256)(128)(2,1)}, u32[]{:S(2)}) copy-start(bf16[64]{0:T(256)(128)(2,1)} %refs_2_.2) | copy-start | bytes 388
  0.7 1.2 %copy-start.9 = (bf16[64]{0:T(256)(128)(2,1)S(1)}, bf16[64]{0:T(256)(128)(2,1)}, u32[]{:S(2)}) copy-start(bf16[64]{0:T(256)(128)(2,1)} %refs_1_.2) | copy-start | bytes 388
  0.8 1.2 %copy-start.8 = (bf16[64]{0:T(256)(128)(2,1)S(1)}, bf16[64]{0:T(256)(128)(2,1)}, u32[]{:S(2)}) copy-start(bf16[64]{0:T(256)(128)(2,1)} %refs_0_.2) | copy-start | bytes 388
  0.8 1.2 %copy-start.7 = (s32[7,64]{1,0:T(8,128)S(1)}, s32[7,64]{1,0:T(8,128)}, u32[]{:S(2)}) copy-start(s32[7,64]{1,0:T(8,128)} %s_ref.1) | copy-start | bytes 5380
  2.1 14.8 %copy-start = (bf16[64,64]{1,0:T(8,128)(2,1)S(1)}, bf16[64,64]{1,0:T(8,128)(2,1)}, u32[]{:S(2)}) copy-start(bf16[64,64]{1,0:T(8,128)(2,1)} %refs_0_.3) | copy-start | bytes 24580
  2.1 14.8 %copy-start.1 = (bf16[64,64]{1,0:T(8,128)(2,1)S(1)}, bf16[64,64]{1,0:T(8,128)(2,1)}, u32[]{:S(2)}) copy-start(bf16[64,64]{1,0:T(8,128)(2,1)} %refs_1_.3) | copy-start | bytes 24580
  2.1 14.8 %copy-start.2 = (bf16[64,64]{1,0:T(8,128)(2,1)S(1)}, bf16[64,64]{1,0:T(8,128)(2,1)}, u32[]{:S(2)}) copy-start(bf16[64,64]{1,0:T(8,128)(2,1)} %refs_2_.3) | copy-start | bytes 24580
  2.1 14.8 %copy-start.3 = (bf16[64,64]{1,0:T(8,128)(2,1)S(1)}, bf16[64,64]{1,0:T(8,128)(2,1)}, u32[]{:S(2)}) copy-start(bf16[64,64]{1,0:T(8,128)(2,1)} %refs_3_.3) | copy-start | bytes 24580
  2.1 14.8 %copy-start.4 = (bf16[64,128]{1,0:T(8,128)(2,1)S(1)}, bf16[64,128]{1,0:T(8,128)(2,1)}, u32[]{:S(2)}) copy-start(bf16[64,128]{1,0:T(8,128)(2,1)} %refs_4_.3) | copy-start | bytes 49156
  2.1 14.8 %copy-start.5 = (bf16[128,64]{0,1:T(8,128)(2,1)S(1)}, bf16[128,64]{0,1:T(8,128)(2,1)}, u32[]{:S(2)}) copy-start(bf16[128,64]{0,1:T(8,128)(2,1)} %param.37) | copy-start | bytes 49156
  2.2 14.8 %copy-start.6 = (s32[7,2,128]{2,1,0:T(2,128)S(1)}, s32[7,2,128]{2,1,0:T(2,128)}, u32[]{:S(2)}) copy-start(s32[7,2,128]{2,1,0:T(2,128)} %idx_ref.1) | copy-start | bytes 21508
  23.1 1.3 %collective-permute-start = (f32[136,128]{1,0:T(8,128)S(1)}, f32[136,128]{1,0:T(8,128)S(1)}, u32[]{:S(2)}, u32[]{:S(2)}) collective-permute-start(f32[136,128]{1,0:T(8,128)S(1)} %get-tuple-element.45), channel_id=1, source_target_pairs={{0,8},{8,0},{16,24},{24,16},{1,9},{9,1},{17,25},{25,17},{2,10},{10... | collective-permute-start | bytes 208904 | tf_op jit(solution)/shard_map/ppermute | solution.py:549
  39.9 3.7 %collective-permute-start.3 = (bf16[136,128]{1,0:T(8,128)(2,1)S(1)}, bf16[136,128]{1,0:T(8,128)(2,1)S(1)}, u32[]{:S(2)}, u32[]{:S(2)}) collective-permute-start(bf16[136,128]{1,0:T(8,128)(2,1)S(1)} %shard_map.334.refs_0_), channel_id=1, source_target_pairs={{0,24},{8,16},{16,8},{24,0},{1,25},{9,17},{17,9},{25,1},{2,26},{10... | collective-permute-start | bytes 104456 | tf_op jit(solution)/shard_map/ppermute | solution.py:549
  40.0 4.1 %collective-permute-start.2 = (bf16[136,128]{1,0:T(8,128)(2,1)S(1)}, bf16[136,128]{1,0:T(8,128)(2,1)S(1)}, u32[]{:S(2)}, u32[]{:S(2)}) collective-permute-start(bf16[136,128]{1,0:T(8,128)(2,1)S(1)} %shard_map.334.refs_0_), channel_id=1, source_target_pairs={{0,16},{8,24},{16,0},{24,8},{1,17},{9,25},{17,1},{25,9},{2,18},{10... | collective-permute-start | bytes 104456 | tf_op jit(solution)/shard_map/ppermute | solution.py:549
  41.6 2.5 %collective-permute-start.1 = (bf16[136,128]{1,0:T(8,128)(2,1)S(1)}, bf16[136,128]{1,0:T(8,128)(2,1)S(1)}, u32[]{:S(2)}, u32[]{:S(2)}) collective-permute-start(bf16[136,128]{1,0:T(8,128)(2,1)S(1)} %shard_map.334.refs_0_), channel_id=1, source_target_pairs={{0,8},{8,0},{16,24},{24,16},{1,9},{9,1},{17,25},{25,17},{2,10},{10... | collective-permute-start | bytes 104456 | tf_op jit(solution)/shard_map/ppermute | solution.py:549

commit v5 on v4

--- a/solution.py
+++ b/solution.py
@@ -12,8 +12,11 @@
 EPS = 1e-05
 RIDGE = 0.1
 FAR = 640.0
-SEG_ROWS = 16
+SEG_ROWS = 8
 GRAD_ROWS = 272
+NORM_ROW = 131
+
+LOG2_E = 1.4426950408889634
 
 f32 = jnp.float32
 bf16 = jnp.bfloat16
@@ -101,6 +104,7 @@
     heads, marks = idx.shape
     size = width // heads
     sharp = size**-0.5
+    sharp2 = sharp * LOG2_E
     out_scale = tokens**-0.5
     hm = heads * marks
     hs = range(heads)
@@ -130,13 +134,15 @@
         p = p_t.astype(f32)
         sq = p * p
         hi = sq.astype(bf16)
-        return jnp.concatenate([p_t, hi, (sq - hi.astype(f32)).astype(bf16), seg_rows], 0)
+        return jnp.concatenate([p_t, seg_rows, hi, (sq - hi.astype(f32)).astype(bf16)], 0)
 
     feats_q, feats_k = features(q_t), features(k_t)
 
     idx_row = jnp.concatenate([idx[h : h + 1] for h in hs], 1)
     pick_t = (iota((2 * tokens, hm), 0) == idx_row).astype(f32).astype(bf16)
     qk_t = jnp.concatenate([q_t, k_t], 1)
+    ones16 = jnp.ones((16, tokens), bf16)
+    normed_ones = jnp.concatenate([normed_t, ones16], 0)
     seg2 = jnp.concatenate([onehot_t, onehot_t], 1)
     picked = mm(jnp.concatenate([qk_t, seg2], 0), pick_t)
     own = ((iota((width, hm), 0) // size) == (iota((width, hm), 1) // marks)).astype(f32)
@@ -154,18 +160,22 @@
     extra = jnp.where(row8 == 6, half_lo, extra)
     extra = jnp.where(row8 == 7, -FAR, extra)
     pad = jnp.zeros((width - 8, hm), f32)
-    right_m = jnp.concatenate([mark_t, -0.5 * own, -0.5 * own, extra, pad], 0).T.astype(bf16)
+    squares = iota((hm, 2 * width), 1) % width // size == iota((hm, 2 * width), 0) // marks
+    right_m = pair(
+        jnp.concatenate([mark_t, extra, pad], 0).T.astype(bf16),
+        jnp.where(squares, -0.5, 0.0).astype(bf16),
+    )
     sq_hi = sq.astype(bf16).astype(f32)
     left = jnp.concatenate(
-        [mark_t, sq_hi, sq - sq_hi, jnp.where(row8 < 4, mark_seg, 1.0), pad], 0
+        [mark_t, jnp.where(row8 < 4, mark_seg, 1.0), pad, sq_hi, sq - sq_hi], 0
     ).astype(bf16)
     mark16 = mark_t.astype(bf16)
 
     def near_of(points):
-        return jnp.exp(sharp * mm(right_m, points)).astype(bf16)
+        return jnp.exp2(sharp2 * mm(right_m, points)).astype(bf16)
 
     eye = (iota((marks, marks), 0) == iota((marks, marks), 1)).astype(f32)
-    kernel = [jnp.exp(sharp * mm(right_m[at[h]], left[:, at[h]])) for h in hs]
+    kernel = [jnp.exp2(sharp2 * mm(right_m[at[h]], left[:, at[h]])) for h in hs]
     gram = [kernel[h] + RIDGE * eye for h in hs]
     sums = [col_sum(gram[h]) for h in hs]
     widest = [jnp.max(sums[h], axis=1, keepdims=True) for h in hs]
@@ -176,7 +186,6 @@
     v_tok = v_t.astype(f32).T.astype(bf16)
     rests, wides = [rest], []
     near_k, near_q, near_q_tok, summed_t, sent_t, grown = [], [], [], [], [], []
-    rest_pair, grown_pair = [], []
 
     def add_near_k(i):
         half = tokens // 2
@@ -204,9 +213,6 @@
 
     def widen(both):
         return [wide_right(both[h]) for h in hs]
-
-    def add_pairs(step):
-        rest_pair.append([pair(*split(rests[step][h])) for h in hs])
 
     def next_rest():
         wides.append(widen(rests[-1]))
@@ -220,12 +226,10 @@
     twice = [widen(two_steps(0))]
     add_sums()
     next_rest()
-    add_pairs(0)
     add_near_q(0)
     add_sent()
     next_rest()
     twice.append(widen(two_steps(2)))
-    add_pairs(1)
     add_near_q(1)
     grown.extend([None] * NS_STEPS)
     grown[2] = grown_by(grown[0], twice[0])
@@ -248,9 +252,11 @@
     inverse_wide = widen(inverse)
     grown[1] = grown_by(grown[0], wides[0])
     grown[3] = grown_by(grown[2], wides[2])
-    for step in range(2, NS_STEPS):
-        add_pairs(step)
-    grown_pair = [[grown[step][h].T.astype(bf16) for h in hs] for step in range(NS_STEPS)]
+    beside_rest = [
+        [pair(rests[step][h], grown[step][h].T).astype(bf16) for h in hs]
+        for step in range(NS_STEPS)
+    ]
+    normed_mark = pair(mm(normed_ones, pick_t[:tokens]), mm(normed_ones, pick_t[tokens:])).astype(bf16)
     wup_t = wup.astype(f32).T.astype(bf16)
     d_act = mm_tn(wdown_t, g16_t)
     xhat2, scale2 = norm_stats(hidden)
@@ -272,8 +278,7 @@
     d_sent_t = mm(d_branch, near_q_tok) * out_scale
     back = [d_sent_t[:, at[h]] for h in hs]
 
-    gram_pair = [pair(*split(gram[h])) for h in hs]
-    sent_pair = [pair(*split(sent_t[h].T)) for h in hs]
+    beside_gram = [pair(sent_t[h].T, -gram[h]).astype(bf16) for h in hs]
     kernel_inv = [kernel[h] * inv2[h] for h in hs]
     widest_a = [(2.0 / widest[h]) * (eye - rests[0][h]) for h in hs]
     widest_b = [(2.0 / widest[h]) * grown[0][h] for h in hs]
@@ -291,7 +296,7 @@
             top * mm(mark_ones[h], seen)
             + mm_nt(mark_ones[h], along)[:, :1] * mm(along, seen)[:1]
         )
-    mixed_m = mixed_t.astype(f32).T.astype(bf16)
+    mixed_m = (jnp.concatenate(now, 1) * out_scale).T.astype(bf16)
     q_tok = q_t.astype(f32).T.astype(bf16)
     k_tok = k_t.astype(f32).T.astype(bf16)
     ones_tok = jnp.ones((tokens, width), bf16)
@@ -310,12 +315,10 @@
 
     def pull_some(i):
         now_at = chunks[i]
-        pull = mm(mixed_m, d_branch[:, now_at]) * out_scale
-        pulls_q.append((pull * near_q[:, now_at].astype(f32)).astype(bf16))
+        pulls_q.append(mm(mixed_m, d_branch[:, now_at]).astype(bf16) * near_q[:, now_at])
 
     def pull_rest():
-        pull = mm(d_summed_m, v_t)
-        pulls_q.append((pull * near_k.astype(f32)).astype(bf16))
+        pulls_q.append(mm(d_summed_m, v_t).astype(bf16) * near_k)
 
     def add_tok(pull, tok):
         toks.append(mm(pull, pair(tok, ones_tok)))
@@ -327,39 +330,64 @@
     def add_tok_k():
         add_tok(pulls_q[1], k_tok)
 
+    early = {}
+
+    def add_down():
+        early["down"] = mm_nt(g16_t, act)
+
+    def add_up():
+        early["up"] = mm_nt(jnp.concatenate([normed2_t, ones16], 0), d_inner)
+
+    def add_bias():
+        early["bias"] = mm_nt(ones16, jnp.concatenate([g16_t, d_branch], 0))
+
+    def add_wo():
+        early["wo"] = jnp.concatenate(
+            [mm_nt(summed_t[h].astype(bf16), d_start[h].astype(bf16)) for h in hs], 0
+        )
+
+    def add_stay():
+        stay_q, stay_k = stays(pulls_q[0], q_t), stays(pulls_q[1], k_t)
+        dv = mm(d_summed_t.astype(bf16), near_k)
+        early["stay"] = jnp.concatenate([stay_q, stay_k, dv], 0).astype(bf16)
+
+    def add_qkv():
+        early["qkv"] = mm_nt(normed_ones, early["stay"])
+
+    def add_normed():
+        early["normed"] = mm(wqkv, early["stay"])
+
     beside = [
-        [partial(pull_some, 0), partial(pull_some, 1)],
-        [partial(pull_some, 2), partial(pull_some, 3)],
-        [add_tok_q],
-        [pull_rest],
+        [partial(pull_some, 0), partial(pull_some, 1), partial(pull_some, 2), partial(pull_some, 3)],
+        [add_tok_q, pull_rest],
         [add_tok_k],
-        [],
+        [add_stay],
+        [add_up, add_down],
+        [add_qkv, add_normed, add_bias, add_wo],
     ]
-    d_rest = None
+    b16 = [back[h].astype(bf16) for h in hs]
+    last = NS_STEPS - 1
+    d_rest = [mm(beside_rest[last][h][:, marks:], b16[h]) for h in hs]
+    back = [back[h] + wide_mm(b16[h], wides[last][h][:marks]) for h in hs]
     for step in reversed(range(NS_STEPS)):
-        outer = [mm(grown_pair[step][h], back[h].astype(bf16)) for h in hs]
-        back = [back[h] + mm_wide(back[h], wides[step][h]) for h in hs]
-        if d_rest is None:
-            d_rest = outer
-        else:
-            d_rest = [
-                mm_wide(d_rest[h], wides[step][h])
-                + wide_mm(rest_pair[step][h], wide_right(d_rest[h]))
-                + outer[h]
-                for h in hs
+        if step < last:
+            both16 = [
+                jnp.concatenate([d_rest[h].astype(bf16), back[h].astype(bf16)], 0) for h in hs
             ]
-        for work in beside[NS_STEPS - 1 - step]:
+            turned = [wide_mm(both16[h], wides[step][h][:marks]) for h in hs]
+            back = [back[h] + turned[h][marks:] for h in hs]
+            d_rest = [turned[h][:marks] + mm(beside_rest[step][h], both16[h]) for h in hs]
+        for work in beside[last - step]:
             work()
-    pull_q, pull_k = pulls_q
+    d16 = [d_rest[h].astype(bf16) for h in hs]
     d_gram = [
-        wide_mm(sent_pair[h], wide_right(back[h]))
-        - mm_wide(d_rest[h], gram_wide[h])
-        - wide_mm(gram_pair[h], wide_right(d_rest[h]))
+        mm(beside_gram[h], jnp.concatenate([back[h].astype(bf16), d16[h]], 0))
+        - wide_mm(d16[h], gram_wide[h][:marks])
         for h in hs
     ]
     tok_both = (toks[0] + toks[1]).T
     tok_t, tok_sum = tok_both[:width], tok_both[width : width + 1]
-    stay_q, stay_k = stays(pull_q, q_t), stays(pull_k, k_t)
+    stay, d_normed_tok = early["stay"], early["normed"]
     gram_part = []
     for h in hs:
         d_widest = total_of(d_rest[h] * widest_a[h]) - total_of(back[h] * widest_b[h])
@@ -369,54 +397,63 @@
     d_mark_t = (
         (tok_t + gram_part[:width] - mark_t * (tok_sum + gram_part[width : width + 1])) * own
     ).astype(bf16)
-    idx_col = jnp.broadcast_to(idx_row.astype(f32), (8, hm)).T[:, :1].astype(jnp.int32)
-    pick_m = (iota((hm, 2 * tokens), 1) == idx_col).astype(f32).astype(bf16)
-    moved = mm(d_mark_t, pick_m)
-    dq = (stay_q + sharp * moved[:, :tokens]).astype(bf16)
-    dk = (stay_k + sharp * moved[:, tokens:]).astype(bf16)
-    dv = mm(d_summed_t.astype(bf16), near_k).astype(bf16)
-    dqkv = jnp.concatenate([dq, dk, dv], 0)
-    d_normed = mm(wqkv, dqkv)
-    grad_in = d_hidden + norm_back(d_normed, xhat1, scale1, gain1)
-    out = jnp.concatenate([layer_out, grad_in], 0).T.astype(bf16)
-
-    ones16 = jnp.ones((16, tokens), bf16)
-    g_down = mm_nt(g16_t, act)
-    g_up = mm_nt(jnp.concatenate([normed2_t, ones16], 0), d_inner)
-    g_qkv = mm_nt(jnp.concatenate([normed_t, ones16], 0), dqkv)
-    g_bias = mm_nt(ones16, jnp.concatenate([g16_t, d_branch], 0))
-    g_wo = jnp.concatenate(
-        [mm_nt(summed_t[h].astype(bf16), d_start[h].astype(bf16)) for h in hs], 0
-    )
+    g_bias, g_wo = early["bias"], early["wo"]
+    g_down, g_up = early["down"], early["up"]
+    by_mark = sharp * pair(
+        mm_nt(normed_mark[:, :hm], d_mark_t), mm_nt(normed_mark[:, hm:], d_mark_t)
+    )
+    g_qkv = early["qkv"] + pair(by_mark, jnp.zeros((width + 16, width), f32))
     columns = [
-        row_sum(d_normed * xhat1),
-        row_sum(d_normed),
         row_sum(d_norm2 * xhat2),
         row_sum(d_norm2),
     ]
     lane = iota((width, 128), 1)
     norms = sum(jnp.where(lane == i, col, 0.0) for i, col in enumerate(columns)).T[:8]
     g_bqkv = g_qkv[width : width + 1]
-    vecs = [
-        g_up[width : width + 1],
-        pair(g_bias[:1, :width], g_bqkv[:, :width]),
-        g_bqkv[:, width:],
-        pair(g_bias[:1, width:], norms[0:1]),
-        pair(norms[1:2], norms[2:3]),
-        pair(norms[3:4], jnp.zeros((1, width), f32)),
-        jnp.zeros((GRAD_ROWS - 262, 128), f32),
-    ]
+    blank = jnp.zeros((1, 2 * width), f32)
     grads = jnp.concatenate(
         [
             g_up[:width],
             g_down[:width],
+            g_up[width : width + 1],
+            pair(g_bias[:1, :width], g_bqkv[:, :width]),
+            g_bqkv[:, width:],
+        ]
+        + [blank] * 5
+        + [
             g_qkv[:width, : 2 * width],
             pair(g_qkv[:width, 2 * width :], g_wo),
+            pair(g_bias[:1, width:], norms[0:1]),
+            pair(norms[1:2], blank[:, :width]),
         ]
-        + vecs,
+        + [blank] * 6,
         0,
     )
-    return out, grads
+    later = (d_mark_t, d_normed_tok, d_hidden, xhat1, scale1, layer_out)
+    return later, grads
+
+
+def row_end(later, idx, par):
+    gain1, wq, wk = par
+    d_mark_t, d_normed_tok, d_hidden, xhat1, scale1, layer_out = later
+    width, tokens = xhat1.shape
+    heads, marks = idx.shape
+    hm = heads * marks
+    idx_row = jnp.concatenate([idx[h : h + 1] for h in range(heads)], 1)
+    idx_col = jnp.broadcast_to(idx_row.astype(f32), (8, hm)).T[:, :1].astype(jnp.int32)
+    tok_lane = iota((hm, tokens), 1)
+    pick_m = jnp.concatenate([tok_lane == idx_col, tok_lane + tokens == idx_col], 0)
+    pick_m = pick_m.astype(f32).astype(bf16)
+    onto = mm(jnp.concatenate([wq, wk], 0), d_mark_t).astype(bf16)
+    moved = mm(pair(onto[:width], onto[width:]), pick_m)
+    d_normed = d_normed_tok + (width // heads) ** -0.5 * moved
+    grad_in = d_hidden + norm_back(d_normed, xhat1, scale1, gain1)
+    lane = iota((width, 128), 1)
+    sums = jnp.where(lane == 0, row_sum(d_normed * xhat1), 0.0) + jnp.where(
+        lane == 1, row_sum(d_normed), 0.0
+    )
+    sums = sums.T
+    return jnp.concatenate([layer_out, grad_in], 0).T.astype(bf16), pair(sums[:1], sums[1:2])
 
 
 MATRICES = (2, 4, 6, 8, 12, 14)
@@ -433,24 +470,35 @@
     return tuple(par)
 
 
+def own_row(idx_ref):
+    return idx_ref[jnp.minimum(lax.axis_index("tok"), idx_ref.shape[0] - 1)]
+
+
 def main_kernel(tok_block, blk_ref, idx_ref, vec_ref, *refs):
-    mats, (out_ref, keep_ref, send_ref) = refs[:6], refs[6:]
-    vec_cols = vec_ref[...].T
+    mats, later_refs, (keep_ref, send_ref) = refs[:6], refs[6:-2], refs[-2:]
     blocks = blk_ref.shape[0]
     tokens = blocks * tok_block
-    row = jnp.minimum(lax.axis_index("tok"), idx_ref.shape[0] - 1)
     xg = blk_ref[:, :tok_block, :].reshape(tokens, 128)
     ids = blk_ref[:, tok_block:, :].astype(f32)
     half = iota((SEG_ROWS, 128), 1) < tok_block
     onehot_t = jnp.concatenate(
         [jnp.where(half, ids[2 * j], ids[2 * j + 1]) for j in range(blocks // 2)], 1
     ).astype(bf16)
-    out, grads = row_work(xg, onehot_t, idx_ref[row], read_params(mats, vec_cols))
-    out_ref[...] = out.reshape(blocks, tok_block, 128)
+    later, grads = row_work(xg, onehot_t, own_row(idx_ref), read_params(mats, vec_ref[...].T))
+    for ref, value in zip(later_refs, later):
+        ref[...] = value
     first = lax.rem(lax.axis_index("rows"), 2) == 0
     h = GRAD_ROWS // 2
     keep_ref[...] = jnp.where(first, grads[:h], grads[h:])
     send_ref[...] = jnp.where(first, grads[h:], grads[:h])
+
+
+def end_kernel(idx_ref, vec_ref, wq_ref, wk_ref, *refs):
+    later, out_ref, norm_ref = [ref[...] for ref in refs[:-2]], refs[-2], refs[-1]
+    gain1 = vec_ref[...].T[: wq_ref.shape[0], :1]
+    out, sums = row_end(later, own_row(idx_ref), (gain1, wq_ref[...], wk_ref[...]))
+    out_ref[...] = out.reshape(out_ref.shape)
+    norm_ref[...] = jnp.where(iota(norm_ref.shape, 0) == NORM_ROW, sums, 0.0)
 
 
 def pack_kernel(xg_ref, s_ref, *refs):
@@ -482,10 +530,9 @@
 
 def unpack_kernel(n_parts, *refs):
     parts, outs = refs[:n_parts], refs[n_parts:]
-    halves = [
-        sum([p[...].astype(f32) for p in parts[core + 2 :: 2]], parts[core][...].astype(f32))
-        for core in range(2)
-    ]
+    parts = [p[...].astype(f32) for p in parts]
+    halves = [sum(parts[core + 2 :: 2], parts[core]) for core in range(2)]
+    norms = halves[0][NORM_ROW] + halves[1][NORM_ROW]
     first = lax.rem(lax.axis_index("rows"), 2) == 0
     a = jnp.where(first, halves[0], halves[1])
     b = jnp.where(first, halves[1], halves[0])
@@ -493,20 +540,20 @@
     (gain1, bias1, wq, bq, wk, bk, wv, bv, wo, bo, gain2, bias2, wup, bup, wdown_t, bdown) = outs
     wup[...] = whole[0:64]
     wdown_t[...] = whole[64:128]
-    wq[...] = whole[128:192, :64]
-    wk[...] = whole[128:192, 64:]
-    wv[...] = whole[192:256, :64]
-    wo[...] = whole[192:256, 64:]
-    bup[...] = whole[256]
-    bdown[...] = whole[257, :64]
-    bq[...] = whole[257, 64:]
-    bk[...] = whole[258, :64]
-    bv[...] = whole[258, 64:]
-    bo[...] = whole[259, :64]
-    gain1[...] = whole[259, 64:]
-    bias1[...] = whole[260, :64]
-    gain2[...] = whole[260, 64:]
-    bias2[...] = whole[261, :64]
+    bup[...] = whole[128]
+    bdown[...] = whole[129, :64]
+    bq[...] = whole[129, 64:]
+    bk[...] = whole[130, :64]
+    bv[...] = whole[130, 64:]
+    wq[...] = whole[136:200, :64]
+    wk[...] = whole[136:200, 64:]
+    wv[...] = whole[200:264, :64]
+    wo[...] = whole[200:264, 64:]
+    bo[...] = whole[264, :64]
+    gain2[...] = whole[264, 64:]
+    bias2[...] = whole[265, :64]
+    gain1[...] = norms[:64]
+    bias1[...] = norms[64:]
 
 
 def call(kernel, outs, *args, mib=12):
@@ -536,19 +583,37 @@
     )
     got = lax.all_to_all(sent, "tok", 0, 0, tiled=True)
     h = GRAD_ROWS // 2
-    out, keep, send = call(
+    tokens = n_tok * tok
+    mib = 12 * max(1, tokens // 512)
+    by_token = sds((width, tokens), f32)
+    marks = landmark_index.shape[1] * landmark_index.shape[2]
+    *later, keep, send = call(
         partial(main_kernel, tok),
-        (sds((n_tok, tok, 128), bf16), sds((h, 128), f32), sds((h, 128), f32)),
+        (sds((width, marks), bf16),)
+        + (by_token,) * 3
+        + (sds((1, tokens), f32), by_token)
+        + (sds((h, 128), f32),) * 2,
         got,
         landmark_index,
         vecs,
         *[params[i] for i in MATRICES],
-        mib=12 * max(1, n_tok * tok // 512),
+        mib=mib,
+    )
+    send = lax.ppermute(send, "rows", [(i, i ^ 1) for i in range(n_rows)])
+    out, norms = call(
+        end_kernel,
+        (sds((n_tok, tok, 128), bf16), sds((h, 128), f32)),
+        landmark_index,
+        vecs,
+        params[2],
+        params[4],
+        *later,
+        mib=mib,
     )
     def from_xor(array, m):
         return lax.ppermute(array, "rows", [(i, i ^ m) for i in range(n_rows)])
 
-    total = (keep + from_xor(send, 1)).astype(bf16)
+    total = (keep + send + norms).astype(bf16)
     back = jnp.concatenate([out, jnp.broadcast_to(total, (n_tok, h, 128))], 1)
     got = lax.all_to_all(back, "tok", 0, 0, tiled=True)
     mine = call(partial(sum_kernel, tok), sds((h, 128), bf16), got)

time: 45.1 us -> 44.5 us (0.987)
  waiting for transfers between devices: 2.71 us -> 2.02 us
    ppermute x4 -> x3, waiting for transfers between devices: 2.71 us -> 1.46 us  [from_xor(): return lax.ppermute(array, 'rows', [(i, i ^ m) for i in range(n_rows)])]
    ppermute x0 -> x1, waiting for transfers between devices: none -> 0.56 us  [shards(): send = lax.ppermute(send, 'rows', [(i, i ^ 1) for i in range(n_rows)])]
    pallas_call x5 -> x6, Pallas kernels: 7.82 us -> 8.06 us  [call(): pl.pallas_call(kernel, out_shape=outs, in_specs=[vmem] * len(args), out_s...]
    ppermute x4 -> x3, starting transfers between devices: 1.99 us -> 1.93 us  [from_xor(): return lax.ppermute(array, 'rows', [(i, i ^ m) for i in range(n_rows)])]
  transfers between devices with their start and end apart: 4 -> 4, of which waited for: 3 -> 3; matrix products, arithmetic and copies ran while one was open for 0% -> 0% of each run, Pallas kernels for 2% -> 3%
where the time goes in v5:
time: 44.5 us; the launch traced here: 44.3 us
  blocking collectives  30 us (67%)
  Pallas kernels  8.06 us (18%)
  waiting for transfers between devices  2.02 us (5%)
  starting transfers between devices  1.99 us (4%)
  other arithmetic  1.17 us (3%)
  between operations  0.95 us (2%)
    all_to_all x1, blocking collectives, shards(): got = lax.all_to_all(back, 'tok', 0, 0, tiled=True)  15.3 us
    all_to_all x1, blocking collectives, shards(): got = lax.all_to_all(sent, 'tok', 0, 0, tiled=True)  14.6 us
    pallas_call x6, Pallas kernels, call(): pl.pallas_call(kernel, out_shape=outs, in_specs=[vmem] * len(args), out_s...  8.06 us
    ppermute x3, starting transfers between devices, from_xor(): return lax.ppermute(array, 'rows', [(i, i ^ m) for i in range(n_rows)])  1.93 us
    ppermute x3, waiting for transfers between devices, from_xor(): return lax.ppermute(array, 'rows', [(i, i ^ m) for i in range(n_rows)])  1.46 us
    concatenate x1, other arithmetic, shards(): jnp.concatenate([tokens_in, grad_out], 2)  1.12 us
  transfers between devices with their start and end apart: 4, of which 3 were waited for; matrix products, arithmetic and copies ran while one was open for 0% of the time, Pallas kernels for 3%

profile of v5, /device:TPU:0, one launch (start us, length us, event | category | flops | bytes accessed | tf_op | source)
XLA Modules:
  0.0 44.3 jit_solution(9843495671302164972)
XLA Ops:
  0.7 0.0 copy-start.17
  0.7 0.0 copy-start.16
  0.7 0.0 copy-start.15
  0.7 0.0 copy-start.14
  0.7 0.0 copy-start.13
  0.7 0.0 copy-start.12
  0.7 0.0 copy-start.11
  0.7 0.0 copy-start.10
  0.7 0.0 copy-start.9
  0.8 0.0 copy-start.8
  0.8 0.0 copy-start.7
  0.8 1.1 %pad_maximum_fusion.1.xg_ref = bf16[7,64,128]{2,1,0:T(8,128)(2,1)S(1)} fusion(bf16[7,64,64]{2,1,0:T(8,128)(2,1)} %param.39, bf16[7,64,64]{2,1,0:T(8,128)(2,1)} %param.20), kind=kLoop, calls=%fused_computation.1 | loop fusion | flops 229376 | bytes 229376 | tf_op jit(solution)/shard_map/concatenate | solution.py:579
  1.9 0.0 copy-done.17
  1.9 0.0 copy-done.16
  1.9 0.0 copy-done.15
  1.9 0.0 copy-done.14
  1.9 0.0 copy-done.13
  1.9 0.0 copy-done.12
  2.0 0.0 copy-done.11
  2.0 0.0 copy-done.10
  2.0 0.0 copy-done.9
  2.0 0.0 copy-done.8
  2.0 0.0 copy-done.7
  2.0 0.1 shard_map.331
  2.1 0.0 copy-start.2
  2.1 0.0 copy-start.3
  2.1 0.0 copy-start.4
  2.1 0.0 copy-start.5
  2.2 0.0 copy-start.6
  2.2 14.6 %all_to_all.10.blk_ref = bf16[8,72,128]{2,1,0:T(8,128)(2,1)S(1)} all-to-all(bf16[8,72,128]{2,1,0:T(8,128)(2,1)S(1)} %get-tuple-element.49), channel_id=1, replica_groups=mesh['rows'=4,'tok'=8] {'tok'}, dimensions={0} | all-to-all | bytes 294912 | tf_op jit(solution)/shard_map/all_to_all | solution.py:584
  16.8 0.0 copy-done
  16.8 0.0 copy-done.1
  16.8 0.0 copy-done.2
  16.8 0.0 copy-done.3
  16.8 0.0 copy-done.4
  16.8 5.7 %shard_map.332 = (bf16[64,256]{1,0:T(8,128)(2,1)S(1)}, f32[64,512]{1,0:T(8,128)S(1)}, f32[64,512]{1,0:T(8,128)S(1)}, f32[64,512]{1,0:T(8,128)S(1)}, f32[1,512]{1...) custom-call(bf16[8,72,128]{2,1,0:T(8,128)(2,1)S(1)} %all_to_all.10.blk_ref, ...), custom_call_target="tpu_custom_call" | custom-call | tf_op jit(solution)/shard_map/pallas_call | solution.py:561
  22.5 0.1 collective-permute-start
  22.6 0.7 %shard_map.333 = (bf16[8,64,128]{2,1,0:T(8,128)(2,1)S(1)}, f32[136,128]{1,0:T(8,128)S(1)}) custom-call(s32[7,2,128]{2,1,0:T(2,128)S(1)} %copy-done.2, f32[16,128]{1,0:T(8,128)S(1)} %get-tuple-element.48.vec_ref, bf16[64,64]{1,0:T(8,128)(2,1)S(1)} %copy-done, bf16[64,64]{1,0:T(8,128)(2,1)S(1)} %copy-done.1, bf16[64,256]{1,0:T(8,128)(2,1)S(1)} %get-tuple-element.50.refs_0_, ...), custom_call_target="tpu_custom_call" | custom-call | tf_op jit(solution)/shard_map/pallas_call | solution.py:561
  23.3 0.6 %collective-permute-done = f32[136,128]{1,0:T(8,128)S(1)} collective-permute-done((f32[136,128]{1,0:T(8,128)S(1)}, f32[136,128]{1,0:T(8,128)S(1)}, u32[]{:S(2)}, u32[]{:S(2)}) %collective-permute-start) | collective-permute-done | bytes 69664 | tf_op jit(solution)/shard_map/ppermute | solution.py:602
  24.0 15.3 %all_to_all.11.got_ref = bf16[8,200,128]{2,1,0:T(8,128)(2,1)S(1)} all-to-all(bf16[8,200,128]{2,1,0:T(8,128)(2,1)S(1)} %pad_maximum_fusion), channel_id=1, replica_groups=mesh['rows'=4,'tok'=8] {'tok'}, dimensions={0} | all-to-all | bytes 819200 | tf_op jit(solution)/shard_map/all_to_all | solution.py:618
  39.3 0.2 collective-permute-start.3
  39.5 1.5 %collective-permute-start.2 = (bf16[136,128]{1,0:T(8,128)(2,1)S(1)}, bf16[136,128]{1,0:T(8,128)(2,1)S(1)}, u32[]{:S(2)}, u32[]{:S(2)}) collective-permute-start(bf16[136,128]{1,0:T(8,128)(2,1)S(1)} %shard_map.335.refs_0_), channel_id=1, source_target_pairs={{0,16},{8,24},{16,0},{24,8},{1,17},{9,25},{17,1},{25,9},{2,18},{10... | collective-permute-start | bytes 104456 | tf_op jit(solution)/shard_map/ppermute | solution.py:614
  41.0 0.3 collective-permute-start.1
  41.3 0.8 %shard_map.334 = (bf16[7,64,64]{2,1,0:T(8,128)(2,1)}, f32[7,64,64]{2,1,0:T(8,128)}) custom-call(bf16[8,200,128]{2,1,0:T(8,128)(2,1)S(1)} %all_to_all.11.got_ref), custom_call_target="tpu_custom_call" | custom-call | tf_op jit(solution)/shard_map/pallas_call | solution.py:561
  42.1 1.0 %collective-permute-done.3.refs_3_ = bf16[136,128]{1,0:T(8,128)(2,1)S(1)} collective-permute-done((bf16[136,128]{1,0:T(8,128)(2,1)S(1)}, bf16[136,128]{1,0:T(8,128)(2,1)S(1)}, u32[]{:S(2)}, u32[]{:S(2)}) %collective-permute-start.3) | collective-permute-done | bytes 34848 | tf_op jit(solution)/shard_map/ppermute | solution.py:614
  43.1 0.4 %collective-permute-done.2.refs_2_ = bf16[136,128]{1,0:T(8,128)(2,1)S(1)} collective-permute-done((bf16[136,128]{1,0:T(8,128)(2,1)S(1)}, bf16[136,128]{1,0:T(8,128)(2,1)S(1)}, u32[]{:S(2)}, u32[]{:S(2)}) %collective-permute-start.2) | collective-permute-done | bytes 34848 | tf_op jit(solution)/shard_map/ppermute | solution.py:614
  43.5 0.0 collective-permute-done.1.refs_1_
  43.5 0.8 %shard_map.336 = (f32[64]{0:T(128)}, f32[64]{0:T(128)}, f32[64,64]{1,0:T(8,128)}, f32[64]{0:T(128)}, f32[64,64]{1,0:T(8,128)}, /*index=5*/f32[64]{0:T(128)}, f32...) custom-call(bf16[136,128]{1,0:T(8,128)(2,1)S(1)} %shard_map.335.refs, ...), custom_call_target="tpu_custom_call" | custom-call | tf_op jit(solution)/shard_map/pallas_call | solution.py:561
  (8 shorter events, 0.1 us)
Async XLA Ops:
  0.7 1.2 %copy-start.17 = (bf16[64]{0:T(256)(128)(2,1)S(1)}, bf16[64]{0:T(256)(128)(2,1)}, u32[]{:S(2)}) copy-start(bf16[64]{0:T(256)(128)(2,1)} %refs_9_.1) | copy-start | bytes 388
  0.7 1.2 %copy-start.16 = (bf16[128]{0:T(256)(128)(2,1)S(1)}, bf16[128]{0:T(256)(128)(2,1)}, u32[]{:S(2)}) copy-start(bf16[128]{0:T(256)(128)(2,1)} %refs_8_.1) | copy-start | bytes 772
  0.7 1.2 %copy-start.15 = (bf16[64]{0:T(256)(128)(2,1)S(1)}, bf16[64]{0:T(256)(128)(2,1)}, u32[]{:S(2)}) copy-start(bf16[64]{0:T(256)(128)(2,1)} %refs_7_.1) | copy-start | bytes 388
  0.7 1.2 %copy-start.14 = (bf16[64]{0:T(256)(128)(2,1)S(1)}, bf16[64]{0:T(256)(128)(2,1)}, u32[]{:S(2)}) copy-start(bf16[64]{0:T(256)(128)(2,1)} %refs_6_.1) | copy-start | bytes 388
  0.7 1.2 %copy-start.13 = (bf16[64]{0:T(256)(128)(2,1)S(1)}, bf16[64]{0:T(256)(128)(2,1)}, u32[]{:S(2)}) copy-start(bf16[64]{0:T(256)(128)(2,1)} %refs_5_.1) | copy-start | bytes 388
  0.7 1.2 %copy-start.12 = (bf16[64]{0:T(256)(128)(2,1)S(1)}, bf16[64]{0:T(256)(128)(2,1)}, u32[]{:S(2)}) copy-start(bf16[64]{0:T(256)(128)(2,1)} %refs_4_.2) | copy-start | bytes 388
  0.7 1.2 %copy-start.11 = (bf16[64]{0:T(256)(128)(2,1)S(1)}, bf16[64]{0:T(256)(128)(2,1)}, u32[]{:S(2)}) copy-start(bf16[64]{0:T(256)(128)(2,1)} %refs_3_.2) | copy-start | bytes 388
  0.7 1.2 %copy-start.10 = (bf16[64]{0:T(256)(128)(2,1)S(1)}, bf16[64]{0:T(256)(128)(2,1)}, u32[]{:S(2)}) copy-start(bf16[64]{0:T(256)(128)(2,1)} %refs_2_.2) | copy-start | bytes 388
  0.7 1.2 %copy-start.9 = (bf16[64]{0:T(256)(128)(2,1)S(1)}, bf16[64]{0:T(256)(128)(2,1)}, u32[]{:S(2)}) copy-start(bf16[64]{0:T(256)(128)(2,1)} %refs_1_.2) | copy-start | bytes 388
  0.8 1.2 %copy-start.8 = (bf16[64]{0:T(256)(128)(2,1)S(1)}, bf16[64]{0:T(256)(128)(2,1)}, u32[]{:S(2)}) copy-start(bf16[64]{0:T(256)(128)(2,1)} %refs_0_.2) | copy-start | bytes 388
  0.8 1.2 %copy-start.7 = (s32[7,64]{1,0:T(8,128)S(1)}, s32[7,64]{1,0:T(8,128)}, u32[]{:S(2)}) copy-start(s32[7,64]{1,0:T(8,128)} %s_ref.1) | copy-start | bytes 5380
  2.1 14.7 %copy-start = (bf16[64,64]{1,0:T(8,128)(2,1)S(1)}, bf16[64,64]{1,0:T(8,128)(2,1)}, u32[]{:S(2)}) copy-start(bf16[64,64]{1,0:T(8,128)(2,1)} %wq_ref.1) | copy-start | bytes 24580
  2.1 14.7 %copy-start.1 = (bf16[64,64]{1,0:T(8,128)(2,1)S(1)}, bf16[64,64]{1,0:T(8,128)(2,1)}, u32[]{:S(2)}) copy-start(bf16[64,64]{1,0:T(8,128)(2,1)} %wk_ref.1) | copy-start | bytes 24580
  2.1 14.7 %copy-start.2 = (s32[7,2,128]{2,1,0:T(2,128)S(1)}, s32[7,2,128]{2,1,0:T(2,128)}, u32[]{:S(2)}) copy-start(s32[7,2,128]{2,1,0:T(2,128)} %idx_ref.3) | copy-start | bytes 21508
  2.1 14.7 %copy-start.3 = (bf16[64,64]{1,0:T(8,128)(2,1)S(1)}, bf16[64,64]{1,0:T(8,128)(2,1)}, u32[]{:S(2)}) copy-start(bf16[64,64]{1,0:T(8,128)(2,1)} %refs_2_.3) | copy-start | bytes 24580
  2.1 14.7 %copy-start.4 = (bf16[64,64]{1,0:T(8,128)(2,1)S(1)}, bf16[64,64]{1,0:T(8,128)(2,1)}, u32[]{:S(2)}) copy-start(bf16[64,64]{1,0:T(8,128)(2,1)} %refs_3_.3) | copy-start | bytes 24580
  2.1 14.7 %copy-start.5 = (bf16[64,128]{1,0:T(8,128)(2,1)S(1)}, bf16[64,128]{1,0:T(8,128)(2,1)}, u32[]{:S(2)}) copy-start(bf16[64,128]{1,0:T(8,128)(2,1)} %refs_4_.3) | copy-start | bytes 49156
  2.2 14.7 %copy-start.6 = (bf16[128,64]{0,1:T(8,128)(2,1)S(1)}, bf16[128,64]{0,1:T(8,128)(2,1)}, u32[]{:S(2)}) copy-start(bf16[128,64]{0,1:T(8,128)(2,1)} %param.37) | copy-start | bytes 49156
  22.5 1.3 %collective-permute-start = (f32[136,128]{1,0:T(8,128)S(1)}, f32[136,128]{1,0:T(8,128)S(1)}, u32[]{:S(2)}, u32[]{:S(2)}) collective-permute-start(f32[136,128]{1,0:T(8,128)S(1)} %get-tuple-element.58), channel_id=1, source_target_pairs={{0,8},{8,0},{16,24},{24,16},{1,9},{9,1},{17,25},{25,17},{2,10},{10... | collective-permute-start | bytes 208904 | tf_op jit(solution)/shard_map/ppermute | solution.py:602
  39.3 3.7 %collective-permute-start.3 = (bf16[136,128]{1,0:T(8,128)(2,1)S(1)}, bf16[136,128]{1,0:T(8,128)(2,1)S(1)}, u32[]{:S(2)}, u32[]{:S(2)}) collective-permute-start(bf16[136,128]{1,0:T(8,128)(2,1)S(1)} %shard_map.335.refs_0_), channel_id=1, source_target_pairs={{0,24},{8,16},{16,8},{24,0},{1,25},{9,17},{17,9},{25,1},{2,26},{10... | collective-permute-start | bytes 104456 | tf_op jit(solution)/shard_map/ppermute | solution.py:614
  39.5 4.0 %collective-permute-start.2 = (bf16[136,128]{1,0:T(8,128)(2,1)S(1)}, bf16[136,128]{1,0:T(8,128)(2,1)S(1)}, u32[]{:S(2)}, u32[]{:S(2)}) collective-permute-start(bf16[136,128]{1,0:T(8,128)(2,1)S(1)} %shard_map.335.refs_0_), channel_id=1, source_target_pairs={{0,16},{8,24},{16,0},{24,8},{1,17},{9,25},{17,1},{25,9},{2,18},{10... | collective-permute-start | bytes 104456 | tf_op jit(solution)/shard_map/ppermute | solution.py:614
  41.0 2.5 %collective-permute-start.1 = (bf16[136,128]{1,0:T(8,128)(2,1)S(1)}, bf16[136,128]{1,0:T(8,128)(2,1)S(1)}, u32[]{:S(2)}, u32[]{:S(2)}) collective-permute-start(bf16[136,128]{1,0:T(8,128)(2,1)S(1)} %shard_map.335.refs_0_), channel_id=1, source_target_pairs={{0,8},{8,0},{16,24},{24,16},{1,9},{9,1},{17,25},{25,17},{2,10},{10... | collective-permute-start | bytes 104456 | tf_op jit(solution)/shard_map/ppermute | solution.py:614

commit v6 on v5

--- a/solution.py
+++ b/solution.py
@@ -13,6 +13,7 @@
 RIDGE = 0.1
 FAR = 640.0
 SEG_ROWS = 8
+FIRST = 1
 GRAD_ROWS = 272
 NORM_ROW = 131
 
@@ -471,46 +472,69 @@
 
 
 def own_row(idx_ref):
-    return idx_ref[jnp.minimum(lax.axis_index("tok"), idx_ref.shape[0] - 1)]
+    return idx_ref[jnp.clip(lax.axis_index("tok") - FIRST, 0, idx_ref.shape[0] - 1)]
+
+
+def for_owners(idx_ref, work, zeroed):
+    row = lax.axis_index("tok") - FIRST
+    has_row = (row >= 0) & (row < idx_ref.shape[0])
+    pl.when(has_row)(work)
+
+    @pl.when(jnp.logical_not(has_row))
+    def _():
+        for ref in zeroed:
+            ref[...] = jnp.zeros(ref.shape, ref.dtype)
 
 
 def main_kernel(tok_block, blk_ref, idx_ref, vec_ref, *refs):
     mats, later_refs, (keep_ref, send_ref) = refs[:6], refs[6:-2], refs[-2:]
-    blocks = blk_ref.shape[0]
-    tokens = blocks * tok_block
-    xg = blk_ref[:, :tok_block, :].reshape(tokens, 128)
-    ids = blk_ref[:, tok_block:, :].astype(f32)
-    half = iota((SEG_ROWS, 128), 1) < tok_block
-    onehot_t = jnp.concatenate(
-        [jnp.where(half, ids[2 * j], ids[2 * j + 1]) for j in range(blocks // 2)], 1
-    ).astype(bf16)
-    later, grads = row_work(xg, onehot_t, own_row(idx_ref), read_params(mats, vec_ref[...].T))
-    for ref, value in zip(later_refs, later):
-        ref[...] = value
-    first = lax.rem(lax.axis_index("rows"), 2) == 0
-    h = GRAD_ROWS // 2
-    keep_ref[...] = jnp.where(first, grads[:h], grads[h:])
-    send_ref[...] = jnp.where(first, grads[h:], grads[:h])
+
+    def work():
+        blocks = blk_ref.shape[0]
+        tokens = blocks * tok_block
+        xg = blk_ref[:, :tok_block, :].reshape(tokens, 128)
+        ids = blk_ref[:, tok_block:, :].astype(f32)
+        half = iota((SEG_ROWS, 128), 1) < tok_block
+        onehot_t = jnp.concatenate(
+            [jnp.where(half, ids[2 * j], ids[2 * j + 1]) for j in range(blocks // 2)], 1
+        ).astype(bf16)
+        later, grads = row_work(xg, onehot_t, own_row(idx_ref), read_params(mats, vec_ref[...].T))
+        for ref, value in zip(later_refs, later):
+            ref[...] = value
+        first = lax.rem(lax.axis_index("rows"), 2) == 0
+        h = GRAD_ROWS // 2
+        keep_ref[...] = jnp.where(first, grads[:h], grads[h:])
+        send_ref[...] = jnp.where(first, grads[h:], grads[:h])
+
+    for_owners(idx_ref, work, (keep_ref, send_ref))
 
 
 def end_kernel(idx_ref, vec_ref, wq_ref, wk_ref, *refs):
-    later, out_ref, norm_ref = [ref[...] for ref in refs[:-2]], refs[-2], refs[-1]
-    gain1 = vec_ref[...].T[: wq_ref.shape[0], :1]
-    out, sums = row_end(later, own_row(idx_ref), (gain1, wq_ref[...], wk_ref[...]))
-    out_ref[...] = out.reshape(out_ref.shape)
-    norm_ref[...] = jnp.where(iota(norm_ref.shape, 0) == NORM_ROW, sums, 0.0)
+    later_refs, out_ref, norm_ref = refs[:-2], refs[-2], refs[-1]
+
+    def work():
+        later = [ref[...] for ref in later_refs]
+        gain1 = vec_ref[...].T[: wq_ref.shape[0], :1]
+        out, sums = row_end(later, own_row(idx_ref), (gain1, wq_ref[...], wk_ref[...]))
+        out_ref[...] = out.reshape(out_ref.shape)
+        norm_ref[...] = jnp.where(iota(norm_ref.shape, 0) == NORM_ROW, sums, 0.0)
+
+    for_owners(idx_ref, work, (out_ref, norm_ref))
 
 
 def pack_kernel(xg_ref, s_ref, *refs):
     vecs, (out_ref, vec_ref) = refs[:-2], refs[-2:]
     rows, tok, width = xg_ref.shape
-    out_ref[:rows, :tok, :] = xg_ref[...]
-    out_ref[rows:] = jnp.zeros((out_ref.shape[0] - rows,) + out_ref.shape[1:], bf16)
+    out_ref[:FIRST] = jnp.zeros((FIRST,) + out_ref.shape[1:], bf16)
+    out_ref[FIRST : rows + FIRST, :tok, :] = xg_ref[...]
+    unused = out_ref.shape[0] - rows - FIRST
+    if unused:
+        out_ref[rows + FIRST :] = jnp.zeros((unused,) + out_ref.shape[1:], bf16)
     seg = s_ref[...]
     seg = jnp.concatenate([seg, seg], 1)
     for r in range(rows):
         ids = jnp.broadcast_to(seg[r : r + 1], (SEG_ROWS, width))
-        out_ref[r, tok:, :] = (ids == iota((SEG_ROWS, width), 0)).astype(f32).astype(bf16)
+        out_ref[FIRST + r, tok:, :] = (ids == iota((SEG_ROWS, width), 0)).astype(f32).astype(bf16)
     for i, ref in enumerate(vecs):
         vec_ref[i : i + 1, : ref.shape[0]] = ref[...].astype(f32).reshape(1, -1)
 
@@ -524,8 +548,8 @@
 
 def rows_kernel(got_ref, out_ref, grad_ref):
     rows, tok, width = out_ref.shape
-    out_ref[...] = got_ref[:rows, :tok, :width]
-    grad_ref[...] = got_ref[:rows, :tok, width:].astype(f32)
+    out_ref[...] = got_ref[FIRST : rows + FIRST, :tok, :width]
+    grad_ref[...] = got_ref[FIRST : rows + FIRST, :tok, width:].astype(f32)
 
 
 def unpack_kernel(n_parts, *refs):

time: 44.5 us -> 44.3 us (level)
  Pallas kernels: 8.06 us -> 1.74 us
  blocking collectives: 30 us -> 35.3 us
  waiting for transfers between devices: 2.02 us -> 2.66 us
    pallas_call x6, Pallas kernels: 8.06 us -> 1.74 us  [call(): pl.pallas_call(kernel, out_shape=outs, in_specs=[vmem] * len(args), out_s...]
    all_to_all x1, blocking collectives: 15.3 us -> 20.7 us  [shards(): got = lax.all_to_all(back, 'tok', 0, 0, tiled=True)]
    ppermute x1, waiting for transfers between devices: 0.56 us -> 1.2 us  [shards(): send = lax.ppermute(send, 'rows', [(i, i ^ 1) for i in range(n_rows)])]
  transfers between devices with their start and end apart: 4 -> 4, of which waited for: 3 -> 3; matrix products, arithmetic and copies ran while one was open for 0% -> 0% of each run, Pallas kernels for 3% -> 2%
where the time goes in v6:
time: 44.3 us; the launch traced here: 44 us
  blocking collectives  35.3 us (80%)
  waiting for transfers between devices  2.66 us (6%)
  starting transfers between devices  1.99 us (4%)
  Pallas kernels  1.74 us (4%)
  other arithmetic  1.17 us (3%)
  between operations  0.98 us (2%)
    all_to_all x1, blocking collectives, shards(): got = lax.all_to_all(back, 'tok', 0, 0, tiled=True)  20.7 us
    all_to_all x1, blocking collectives, shards(): got = lax.all_to_all(sent, 'tok', 0, 0, tiled=True)  14.6 us
    ppermute x3, starting transfers between devices, from_xor(): return lax.ppermute(array, 'rows', [(i, i ^ m) for i in range(n_rows)])  1.92 us
    pallas_call x6, Pallas kernels, call(): pl.pallas_call(kernel, out_shape=outs, in_specs=[vmem] * len(args), out_s...  1.74 us
    ppermute x3, waiting for transfers between devices, from_xor(): return lax.ppermute(array, 'rows', [(i, i ^ m) for i in range(n_rows)])  1.46 us
    ppermute x1, waiting for transfers between devices, shards(): send = lax.ppermute(send, 'rows', [(i, i ^ 1) for i in range(n_rows)])  1.2 us
    concatenate x1, other arithmetic, shards(): jnp.concatenate([tokens_in, grad_out], 2)  1.12 us
  transfers between devices with their start and end apart: 4, of which 3 were waited for; matrix products, arithmetic and copies ran while one was open for 0% of the time, Pallas kernels for 2%

profile of v6, /device:TPU:0, one launch (start us, length us, event | category | flops | bytes accessed | tf_op | source)
XLA Modules:
  0.0 44.0 jit_solution(1184718938780784823)
XLA Ops:
  0.7 0.0 copy-start.17
  0.7 0.0 copy-start.16
  0.7 0.0 copy-start.15
  0.7 0.0 copy-start.14
  0.7 0.0 copy-start.13
  0.7 0.0 copy-start.12
  0.7 0.0 copy-start.11
  0.7 0.0 copy-start.10
  0.7 0.0 copy-start.9
  0.8 0.0 copy-start.8
  0.8 0.0 copy-start.7
  0.8 1.1 %pad_maximum_fusion.1.xg_ref = bf16[7,64,128]{2,1,0:T(8,128)(2,1)S(1)} fusion(bf16[7,64,64]{2,1,0:T(8,128)(2,1)} %param.39, bf16[7,64,64]{2,1,0:T(8,128)(2,1)} %param.20), kind=kLoop, calls=%fused_computation.1 | loop fusion | flops 229376 | bytes 229376 | tf_op jit(solution)/shard_map/concatenate | solution.py:603
  1.9 0.0 copy-done.17
  1.9 0.0 copy-done.16
  1.9 0.0 copy-done.15
  1.9 0.0 copy-done.14
  1.9 0.0 copy-done.13
  1.9 0.0 copy-done.12
  2.0 0.0 copy-done.11
  2.0 0.0 copy-done.10
  2.0 0.0 copy-done.9
  2.0 0.0 copy-done.8
  2.0 0.0 copy-done.7
  2.0 0.1 shard_map.331
  2.1 0.0 copy-start.2
  2.1 0.0 copy-start.3
  2.1 0.0 copy-start.4
  2.1 0.0 copy-start.5
  2.2 0.0 copy-start.6
  2.2 14.6 %all_to_all.10.blk_ref = bf16[8,72,128]{2,1,0:T(8,128)(2,1)S(1)} all-to-all(bf16[8,72,128]{2,1,0:T(8,128)(2,1)S(1)} %get-tuple-element.49), channel_id=1, replica_groups=mesh['rows'=4,'tok'=8] {'tok'}, dimensions={0} | all-to-all | bytes 294912 | tf_op jit(solution)/shard_map/all_to_all | solution.py:608
  16.8 0.0 copy-done
  16.8 0.0 copy-done.1
  16.8 0.0 copy-done.2
  16.8 0.0 copy-done.3
  16.8 0.0 copy-done.4
  16.8 0.0 copy-done.5
  16.8 0.0 copy-done.6
  16.9 0.1 collective-permute-start
  17.0 1.2 %collective-permute-done = f32[136,128]{1,0:T(8,128)S(1)} collective-permute-done((f32[136,128]{1,0:T(8,128)S(1)}, f32[136,128]{1,0:T(8,128)S(1)}, u32[]{:S(2)}, u32[]{:S(2)}) %collective-permute-start) | collective-permute-done | bytes 69664 | tf_op jit(solution)/shard_map/ppermute | solution.py:626
  18.3 20.7 %all_to_all.11.got_ref = bf16[8,200,128]{2,1,0:T(8,128)(2,1)S(1)} all-to-all(bf16[8,200,128]{2,1,0:T(8,128)(2,1)S(1)} %pad_maximum_fusion), channel_id=1, replica_groups=mesh['rows'=4,'tok'=8] {'tok'}, dimensions={0} | all-to-all | bytes 819200 | tf_op jit(solution)/shard_map/all_to_all | solution.py:642
  39.1 0.1 collective-permute-start.3
  39.1 1.6 %collective-permute-start.2 = (bf16[136,128]{1,0:T(8,128)(2,1)S(1)}, bf16[136,128]{1,0:T(8,128)(2,1)S(1)}, u32[]{:S(2)}, u32[]{:S(2)}) collective-permute-start(bf16[136,128]{1,0:T(8,128)(2,1)S(1)} %shard_map.335.refs_0_), channel_id=1, source_target_pairs={{0,16},{8,24},{16,0},{24,8},{1,17},{9,25},{17,1},{25,9},{2,18},{10... | collective-permute-start | bytes 104456 | tf_op jit(solution)/shard_map/ppermute | solution.py:638
  40.7 0.3 collective-permute-start.1
  41.0 0.8 %shard_map.334 = (bf16[7,64,64]{2,1,0:T(8,128)(2,1)}, f32[7,64,64]{2,1,0:T(8,128)}) custom-call(bf16[8,200,128]{2,1,0:T(8,128)(2,1)S(1)} %all_to_all.11.got_ref), custom_call_target="tpu_custom_call" | custom-call | tf_op jit(solution)/shard_map/pallas_call | solution.py:585
  41.8 1.0 %collective-permute-done.3.refs_3_ = bf16[136,128]{1,0:T(8,128)(2,1)S(1)} collective-permute-done((bf16[136,128]{1,0:T(8,128)(2,1)S(1)}, bf16[136,128]{1,0:T(8,128)(2,1)S(1)}, u32[]{:S(2)}, u32[]{:S(2)}) %collective-permute-start.3) | collective-permute-done | bytes 34848 | tf_op jit(solution)/shard_map/ppermute | solution.py:638
  42.8 0.5 %collective-permute-done.2.refs_2_ = bf16[136,128]{1,0:T(8,128)(2,1)S(1)} collective-permute-done((bf16[136,128]{1,0:T(8,128)(2,1)S(1)}, bf16[136,128]{1,0:T(8,128)(2,1)S(1)}, u32[]{:S(2)}, u32[]{:S(2)}) %collective-permute-start.2) | collective-permute-done | bytes 34848 | tf_op jit(solution)/shard_map/ppermute | solution.py:638
  43.2 0.0 collective-permute-done.1.refs_1_
  43.2 0.8 %shard_map.336 = (f32[64]{0:T(128)}, f32[64]{0:T(128)}, f32[64,64]{1,0:T(8,128)}, f32[64]{0:T(128)}, f32[64,64]{1,0:T(8,128)}, /*index=5*/f32[64]{0:T(128)}, f32...) custom-call(bf16[136,128]{1,0:T(8,128)(2,1)S(1)} %shard_map.335.refs, ...), custom_call_target="tpu_custom_call" | custom-call | tf_op jit(solution)/shard_map/pallas_call | solution.py:585
  (8 shorter events, 0.2 us)
Async XLA Ops:
  0.7 1.2 %copy-start.17 = (bf16[64]{0:T(256)(128)(2,1)S(1)}, bf16[64]{0:T(256)(128)(2,1)}, u32[]{:S(2)}) copy-start(bf16[64]{0:T(256)(128)(2,1)} %refs_9_.1) | copy-start | bytes 388
  0.7 1.2 %copy-start.16 = (bf16[128]{0:T(256)(128)(2,1)S(1)}, bf16[128]{0:T(256)(128)(2,1)}, u32[]{:S(2)}) copy-start(bf16[128]{0:T(256)(128)(2,1)} %refs_8_.1) | copy-start | bytes 772
  0.7 1.2 %copy-start.15 = (bf16[64]{0:T(256)(128)(2,1)S(1)}, bf16[64]{0:T(256)(128)(2,1)}, u32[]{:S(2)}) copy-start(bf16[64]{0:T(256)(128)(2,1)} %refs_7_.1) | copy-start | bytes 388
  0.7 1.2 %copy-start.14 = (bf16[64]{0:T(256)(128)(2,1)S(1)}, bf16[64]{0:T(256)(128)(2,1)}, u32[]{:S(2)}) copy-start(bf16[64]{0:T(256)(128)(2,1)} %refs_6_.1) | copy-start | bytes 388
  0.7 1.2 %copy-start.13 = (bf16[64]{0:T(256)(128)(2,1)S(1)}, bf16[64]{0:T(256)(128)(2,1)}, u32[]{:S(2)}) copy-start(bf16[64]{0:T(256)(128)(2,1)} %refs_5_.1) | copy-start | bytes 388
  0.7 1.2 %copy-start.12 = (bf16[64]{0:T(256)(128)(2,1)S(1)}, bf16[64]{0:T(256)(128)(2,1)}, u32[]{:S(2)}) copy-start(bf16[64]{0:T(256)(128)(2,1)} %refs_4_.2) | copy-start | bytes 388
  0.7 1.2 %copy-start.11 = (bf16[64]{0:T(256)(128)(2,1)S(1)}, bf16[64]{0:T(256)(128)(2,1)}, u32[]{:S(2)}) copy-start(bf16[64]{0:T(256)(128)(2,1)} %refs_3_.2) | copy-start | bytes 388
  0.7 1.2 %copy-start.10 = (bf16[64]{0:T(256)(128)(2,1)S(1)}, bf16[64]{0:T(256)(128)(2,1)}, u32[]{:S(2)}) copy-start(bf16[64]{0:T(256)(128)(2,1)} %refs_2_.2) | copy-start | bytes 388
  0.7 1.2 %copy-start.9 = (bf16[64]{0:T(256)(128)(2,1)S(1)}, bf16[64]{0:T(256)(128)(2,1)}, u32[]{:S(2)}) copy-start(bf16[64]{0:T(256)(128)(2,1)} %refs_1_.2) | copy-start | bytes 388
  0.8 1.2 %copy-start.8 = (bf16[64]{0:T(256)(128)(2,1)S(1)}, bf16[64]{0:T(256)(128)(2,1)}, u32[]{:S(2)}) copy-start(bf16[64]{0:T(256)(128)(2,1)} %refs_0_.2) | copy-start | bytes 388
  0.8 1.2 %copy-start.7 = (s32[7,64]{1,0:T(8,128)S(1)}, s32[7,64]{1,0:T(8,128)}, u32[]{:S(2)}) copy-start(s32[7,64]{1,0:T(8,128)} %s_ref.1) | copy-start | bytes 5380
  2.1 14.7 %copy-start = (bf16[64,64]{1,0:T(8,128)(2,1)S(1)}, bf16[64,64]{1,0:T(8,128)(2,1)}, u32[]{:S(2)}) copy-start(bf16[64,64]{1,0:T(8,128)(2,1)} %wq_ref.1) | copy-start | bytes 24580
  2.1 14.7 %copy-start.1 = (bf16[64,64]{1,0:T(8,128)(2,1)S(1)}, bf16[64,64]{1,0:T(8,128)(2,1)}, u32[]{:S(2)}) copy-start(bf16[64,64]{1,0:T(8,128)(2,1)} %wk_ref.1) | copy-start | bytes 24580
  2.1 14.7 %copy-start.2 = (s32[7,2,128]{2,1,0:T(2,128)S(1)}, s32[7,2,128]{2,1,0:T(2,128)}, u32[]{:S(2)}) copy-start(s32[7,2,128]{2,1,0:T(2,128)} %idx_ref.3) | copy-start | bytes 21508
  2.1 14.7 %copy-start.3 = (bf16[64,64]{1,0:T(8,128)(2,1)S(1)}, bf16[64,64]{1,0:T(8,128)(2,1)}, u32[]{:S(2)}) copy-start(bf16[64,64]{1,0:T(8,128)(2,1)} %refs_2_.3) | copy-start | bytes 24580
  2.1 14.7 %copy-start.4 = (bf16[64,64]{1,0:T(8,128)(2,1)S(1)}, bf16[64,64]{1,0:T(8,128)(2,1)}, u32[]{:S(2)}) copy-start(bf16[64,64]{1,0:T(8,128)(2,1)} %refs_3_.3) | copy-start | bytes 24580
  2.1 14.7 %copy-start.5 = (bf16[64,128]{1,0:T(8,128)(2,1)S(1)}, bf16[64,128]{1,0:T(8,128)(2,1)}, u32[]{:S(2)}) copy-start(bf16[64,128]{1,0:T(8,128)(2,1)} %refs_4_.3) | copy-start | bytes 49156
  2.2 14.7 %copy-start.6 = (bf16[128,64]{0,1:T(8,128)(2,1)S(1)}, bf16[128,64]{0,1:T(8,128)(2,1)}, u32[]{:S(2)}) copy-start(bf16[128,64]{0,1:T(8,128)(2,1)} %param.37) | copy-start | bytes 49156
  16.9 1.3 %collective-permute-start = (f32[136,128]{1,0:T(8,128)S(1)}, f32[136,128]{1,0:T(8,128)S(1)}, u32[]{:S(2)}, u32[]{:S(2)}) collective-permute-start(f32[136,128]{1,0:T(8,128)S(1)} %get-tuple-element.58), channel_id=1, source_target_pairs={{0,8},{8,0},{16,24},{24,16},{1,9},{9,1},{17,25},{25,17},{2,10},{10... | collective-permute-start | bytes 208904 | tf_op jit(solution)/shard_map/ppermute | solution.py:626
  39.1 3.7 %collective-permute-start.3 = (bf16[136,128]{1,0:T(8,128)(2,1)S(1)}, bf16[136,128]{1,0:T(8,128)(2,1)S(1)}, u32[]{:S(2)}, u32[]{:S(2)}) collective-permute-start(bf16[136,128]{1,0:T(8,128)(2,1)S(1)} %shard_map.335.refs_0_), channel_id=1, source_target_pairs={{0,24},{8,16},{16,8},{24,0},{1,25},{9,17},{17,9},{25,1},{2,26},{10... | collective-permute-start | bytes 104456 | tf_op jit(solution)/shard_map/ppermute | solution.py:638
  39.1 4.1 %collective-permute-start.2 = (bf16[136,128]{1,0:T(8,128)(2,1)S(1)}, bf16[136,128]{1,0:T(8,128)(2,1)S(1)}, u32[]{:S(2)}, u32[]{:S(2)}) collective-permute-start(bf16[136,128]{1,0:T(8,128)(2,1)S(1)} %shard_map.335.refs_0_), channel_id=1, source_target_pairs={{0,16},{8,24},{16,0},{24,8},{1,17},{9,25},{17,1},{25,9},{2,18},{10... | collective-permute-start | bytes 104456 | tf_op jit(solution)/shard_map/ppermute | solution.py:638
  40.7 2.5 %collective-permute-start.1 = (bf16[136,128]{1,0:T(8,128)(2,1)S(1)}, bf16[136,128]{1,0:T(8,128)(2,1)S(1)}, u32[]{:S(2)}, u32[]{:S(2)}) collective-permute-start(bf16[136,128]{1,0:T(8,128)(2,1)S(1)} %shard_map.335.refs_0_), channel_id=1, source_target_pairs={{0,8},{8,0},{16,24},{24,16},{1,9},{9,1},{17,25},{25,17},{2,10},{10... | collective-permute-start | bytes 104456 | tf_op jit(solution)/shard_map/ppermute | solution.py:638

commit v7 on v6

--- a/solution.py
+++ b/solution.py
@@ -79,6 +79,11 @@
     n = wide.shape[1] // 2
     both = mm(a_pair, wide)
     return both[:, :n] + both[:, n:]
+
+
+def both_parts_left(a, wide):
+    n = wide.shape[1] // 2
+    return wide_mm(a, wide[:n])
 
 
 def norm_stats(values):
@@ -297,12 +302,20 @@
             top * mm(mark_ones[h], seen)
             + mm_nt(mark_ones[h], along)[:, :1] * mm(along, seen)[:1]
         )
-    mixed_m = (jnp.concatenate(now, 1) * out_scale).T.astype(bf16)
+    mixed = [mm_wide(summed_t[h], inverse_wide[h]) for h in hs]
+    blank_h = jnp.zeros((size, marks), f32)
+    mixed_m = jnp.concatenate(
+        [jnp.concatenate([mixed[h] if g == h else blank_h for g in hs], 1) for h in hs], 0
+    ).T.astype(bf16)
+    d_att = mm(wo, d_branch).astype(bf16)
     q_tok = q_t.astype(f32).T.astype(bf16)
     k_tok = k_t.astype(f32).T.astype(bf16)
     ones_tok = jnp.ones((tokens, width), bf16)
     d_start = [mm_wide(back[h], inverse_wide[h]) for h in hs]
-    d_summed = [both_parts(mm, wo_of[h], d_start[h]) for h in hs]
+    d_att_early = mm(wo, d_branch).astype(bf16)
+    d_mixed = mm(d_att_early, near_q_tok) * out_scale
+    d_mixed = [d_mixed[rows_of[h], at[h]].astype(bf16) for h in hs]
+    d_summed = [both_parts_left(d_mixed[h], inverse_wide[h]) for h in hs]
     none = jnp.zeros((size, marks), f32)
     d_summed_t = jnp.concatenate(
         [jnp.concatenate([d_summed[h] if g == h else none for g in hs], 1) for h in hs], 0
@@ -316,10 +329,12 @@
 
     def pull_some(i):
         now_at = chunks[i]
-        pulls_q.append(mm(mixed_m, d_branch[:, now_at]).astype(bf16) * near_q[:, now_at])
+        pull = (mm(mixed_m, d_att[:, now_at]) * out_scale).astype(bf16)
+        pulls_q.append((pull.astype(f32) * near_q[:, now_at].astype(f32)).astype(bf16))
 
     def pull_rest():
-        pulls_q.append(mm(d_summed_m, v_t).astype(bf16) * near_k)
+        pull = mm(d_summed_m, v_t).astype(bf16)
+        pulls_q.append((pull.astype(f32) * near_k.astype(f32)).astype(bf16))
 
     def add_tok(pull, tok):
         toks.append(mm(pull, pair(tok, ones_tok)))
@@ -375,7 +390,9 @@
             both16 = [
                 jnp.concatenate([d_rest[h].astype(bf16), back[h].astype(bf16)], 0) for h in hs
             ]
-            turned = [wide_mm(both16[h], wides[step][h][:marks]) for h in hs]
+            turned = [
+                mm_wide(jnp.concatenate([d_rest[h], back[h]], 0), wides[step][h]) for h in hs
+            ]
             back = [back[h] + turned[h][marks:] for h in hs]
             d_rest = [turned[h][:marks] + mm(beside_rest[step][h], both16[h]) for h in hs]
         for work in beside[last - step]:

time: 44.3 us -> 44.3 us (level)
  no operation moved by 1% of the time
where the time goes in v7:
time: 44.3 us; the launch traced here: 44.1 us
  blocking collectives  35.4 us (80%)
  waiting for transfers between devices  2.66 us (6%)
  starting transfers between devices  1.99 us (4%)
  Pallas kernels  1.74 us (4%)
  other arithmetic  1.17 us (3%)
  between operations  0.98 us (2%)
    all_to_all x1, blocking collectives, shards(): got = lax.all_to_all(back, 'tok', 0, 0, tiled=True)  20.8 us
    all_to_all x1, blocking collectives, shards(): got = lax.all_to_all(sent, 'tok', 0, 0, tiled=True)  14.6 us
    ppermute x3, starting transfers between devices, from_xor(): return lax.ppermute(array, 'rows', [(i, i ^ m) for i in range(n_rows)])  1.92 us
    pallas_call x6, Pallas kernels, call(): pl.pallas_call(kernel, out_shape=outs, in_specs=[vmem] * len(args), out_s...  1.74 us
    ppermute x3, waiting for transfers between devices, from_xor(): return lax.ppermute(array, 'rows', [(i, i ^ m) for i in range(n_rows)])  1.46 us
    ppermute x1, waiting for transfers between devices, shards(): send = lax.ppermute(send, 'rows', [(i, i ^ 1) for i in range(n_rows)])  1.2 us
    concatenate x1, other arithmetic, shards(): jnp.concatenate([tokens_in, grad_out], 2)  1.12 us
  transfers between devices with their start and end apart: 4, of which 3 were waited for; matrix products, arithmetic and copies ran while one was open for 0% of the time, Pallas kernels for 2%

profile of v7, /device:TPU:0, one launch (start us, length us, event | category | flops | bytes accessed | tf_op | source)
XLA Modules:
  0.0 44.1 jit_solution(7880565948273250770)
XLA Ops:
  0.7 0.0 copy-start.17
  0.7 0.0 copy-start.16
  0.7 0.0 copy-start.15
  0.7 0.0 copy-start.14
  0.7 0.0 copy-start.13
  0.7 0.0 copy-start.12
  0.7 0.0 copy-start.11
  0.7 0.0 copy-start.10
  0.7 0.0 copy-start.9
  0.8 0.0 copy-start.8
  0.8 0.0 copy-start.7
  0.8 1.1 %pad_maximum_fusion.1.xg_ref = bf16[7,64,128]{2,1,0:T(8,128)(2,1)S(1)} fusion(bf16[7,64,64]{2,1,0:T(8,128)(2,1)} %param.39, bf16[7,64,64]{2,1,0:T(8,128)(2,1)} %param.20), kind=kLoop, calls=%fused_computation.1 | loop fusion | flops 229376 | bytes 229376 | tf_op jit(solution)/shard_map/concatenate | solution.py:620
  1.9 0.0 copy-done.17
  1.9 0.0 copy-done.16
  1.9 0.0 copy-done.15
  1.9 0.0 copy-done.14
  1.9 0.0 copy-done.13
  1.9 0.0 copy-done.12
  2.0 0.0 copy-done.11
  2.0 0.0 copy-done.10
  2.0 0.0 copy-done.9
  2.0 0.0 copy-done.8
  2.0 0.0 copy-done.7
  2.0 0.1 shard_map.331
  2.1 0.0 copy-start.2
  2.1 0.0 copy-start.3
  2.1 0.0 copy-start.4
  2.1 0.0 copy-start.5
  2.2 0.0 copy-start.6
  2.2 14.6 %all_to_all.10.blk_ref = bf16[8,72,128]{2,1,0:T(8,128)(2,1)S(1)} all-to-all(bf16[8,72,128]{2,1,0:T(8,128)(2,1)S(1)} %get-tuple-element.49), channel_id=1, replica_groups=mesh['rows'=4,'tok'=8] {'tok'}, dimensions={0} | all-to-all | bytes 294912 | tf_op jit(solution)/shard_map/all_to_all | solution.py:625
  16.8 0.0 copy-done
  16.8 0.0 copy-done.1
  16.8 0.0 copy-done.2
  16.8 0.0 copy-done.3
  16.8 0.0 copy-done.4
  16.8 0.0 copy-done.5
  16.8 0.0 copy-done.6
  16.9 0.1 collective-permute-start
  17.0 1.2 %collective-permute-done = f32[136,128]{1,0:T(8,128)S(1)} collective-permute-done((f32[136,128]{1,0:T(8,128)S(1)}, f32[136,128]{1,0:T(8,128)S(1)}, u32[]{:S(2)}, u32[]{:S(2)}) %collective-permute-start) | collective-permute-done | bytes 69664 | tf_op jit(solution)/shard_map/ppermute | solution.py:643
  18.3 20.8 %all_to_all.11.got_ref = bf16[8,200,128]{2,1,0:T(8,128)(2,1)S(1)} all-to-all(bf16[8,200,128]{2,1,0:T(8,128)(2,1)S(1)} %pad_maximum_fusion), channel_id=1, replica_groups=mesh['rows'=4,'tok'=8] {'tok'}, dimensions={0} | all-to-all | bytes 819200 | tf_op jit(solution)/shard_map/all_to_all | solution.py:659
  39.1 0.1 collective-permute-start.3
  39.2 1.6 %collective-permute-start.2 = (bf16[136,128]{1,0:T(8,128)(2,1)S(1)}, bf16[136,128]{1,0:T(8,128)(2,1)S(1)}, u32[]{:S(2)}, u32[]{:S(2)}) collective-permute-start(bf16[136,128]{1,0:T(8,128)(2,1)S(1)} %shard_map.335.refs_0_), channel_id=1, source_target_pairs={{0,16},{8,24},{16,0},{24,8},{1,17},{9,25},{17,1},{25,9},{2,18},{10... | collective-permute-start | bytes 104456 | tf_op jit(solution)/shard_map/ppermute | solution.py:655
  40.8 0.3 collective-permute-start.1
  41.1 0.8 %shard_map.334 = (bf16[7,64,64]{2,1,0:T(8,128)(2,1)}, f32[7,64,64]{2,1,0:T(8,128)}) custom-call(bf16[8,200,128]{2,1,0:T(8,128)(2,1)S(1)} %all_to_all.11.got_ref), custom_call_target="tpu_custom_call" | custom-call | tf_op jit(solution)/shard_map/pallas_call | solution.py:602
  41.9 1.0 %collective-permute-done.3.refs_3_ = bf16[136,128]{1,0:T(8,128)(2,1)S(1)} collective-permute-done((bf16[136,128]{1,0:T(8,128)(2,1)S(1)}, bf16[136,128]{1,0:T(8,128)(2,1)S(1)}, u32[]{:S(2)}, u32[]{:S(2)}) %collective-permute-start.3) | collective-permute-done | bytes 34848 | tf_op jit(solution)/shard_map/ppermute | solution.py:655
  42.9 0.4 %collective-permute-done.2.refs_2_ = bf16[136,128]{1,0:T(8,128)(2,1)S(1)} collective-permute-done((bf16[136,128]{1,0:T(8,128)(2,1)S(1)}, bf16[136,128]{1,0:T(8,128)(2,1)S(1)}, u32[]{:S(2)}, u32[]{:S(2)}) %collective-permute-start.2) | collective-permute-done | bytes 34848 | tf_op jit(solution)/shard_map/ppermute | solution.py:655
  43.3 0.0 collective-permute-done.1.refs_1_
  43.3 0.8 %shard_map.336 = (f32[64]{0:T(128)}, f32[64]{0:T(128)}, f32[64,64]{1,0:T(8,128)}, f32[64]{0:T(128)}, f32[64,64]{1,0:T(8,128)}, /*index=5*/f32[64]{0:T(128)}, f32...) custom-call(bf16[136,128]{1,0:T(8,128)(2,1)S(1)} %shard_map.335.refs, ...), custom_call_target="tpu_custom_call" | custom-call | tf_op jit(solution)/shard_map/pallas_call | solution.py:602
  (8 shorter events, 0.2 us)
Async XLA Ops:
  0.7 1.2 %copy-start.17 = (bf16[64]{0:T(256)(128)(2,1)S(1)}, bf16[64]{0:T(256)(128)(2,1)}, u32[]{:S(2)}) copy-start(bf16[64]{0:T(256)(128)(2,1)} %refs_9_.1) | copy-start | bytes 388
  0.7 1.2 %copy-start.16 = (bf16[128]{0:T(256)(128)(2,1)S(1)}, bf16[128]{0:T(256)(128)(2,1)}, u32[]{:S(2)}) copy-start(bf16[128]{0:T(256)(128)(2,1)} %refs_8_.1) | copy-start | bytes 772
  0.7 1.2 %copy-start.15 = (bf16[64]{0:T(256)(128)(2,1)S(1)}, bf16[64]{0:T(256)(128)(2,1)}, u32[]{:S(2)}) copy-start(bf16[64]{0:T(256)(128)(2,1)} %refs_7_.1) | copy-start | bytes 388
  0.7 1.2 %copy-start.14 = (bf16[64]{0:T(256)(128)(2,1)S(1)}, bf16[64]{0:T(256)(128)(2,1)}, u32[]{:S(2)}) copy-start(bf16[64]{0:T(256)(128)(2,1)} %refs_6_.1) | copy-start | bytes 388
  0.7 1.2 %copy-start.13 = (bf16[64]{0:T(256)(128)(2,1)S(1)}, bf16[64]{0:T(256)(128)(2,1)}, u32[]{:S(2)}) copy-start(bf16[64]{0:T(256)(128)(2,1)} %refs_5_.1) | copy-start | bytes 388
  0.7 1.2 %copy-start.12 = (bf16[64]{0:T(256)(128)(2,1)S(1)}, bf16[64]{0:T(256)(128)(2,1)}, u32[]{:S(2)}) copy-start(bf16[64]{0:T(256)(128)(2,1)} %refs_4_.2) | copy-start | bytes 388
  0.7 1.2 %copy-start.11 = (bf16[64]{0:T(256)(128)(2,1)S(1)}, bf16[64]{0:T(256)(128)(2,1)}, u32[]{:S(2)}) copy-start(bf16[64]{0:T(256)(128)(2,1)} %refs_3_.2) | copy-start | bytes 388
  0.7 1.2 %copy-start.10 = (bf16[64]{0:T(256)(128)(2,1)S(1)}, bf16[64]{0:T(256)(128)(2,1)}, u32[]{:S(2)}) copy-start(bf16[64]{0:T(256)(128)(2,1)} %refs_2_.2) | copy-start | bytes 388
  0.7 1.2 %copy-start.9 = (bf16[64]{0:T(256)(128)(2,1)S(1)}, bf16[64]{0:T(256)(128)(2,1)}, u32[]{:S(2)}) copy-start(bf16[64]{0:T(256)(128)(2,1)} %refs_1_.2) | copy-start | bytes 388
  0.8 1.2 %copy-start.8 = (bf16[64]{0:T(256)(128)(2,1)S(1)}, bf16[64]{0:T(256)(128)(2,1)}, u32[]{:S(2)}) copy-start(bf16[64]{0:T(256)(128)(2,1)} %refs_0_.2) | copy-start | bytes 388
  0.8 1.2 %copy-start.7 = (s32[7,64]{1,0:T(8,128)S(1)}, s32[7,64]{1,0:T(8,128)}, u32[]{:S(2)}) copy-start(s32[7,64]{1,0:T(8,128)} %s_ref.1) | copy-start | bytes 5380
  2.1 14.7 %copy-start = (bf16[64,64]{1,0:T(8,128)(2,1)S(1)}, bf16[64,64]{1,0:T(8,128)(2,1)}, u32[]{:S(2)}) copy-start(bf16[64,64]{1,0:T(8,128)(2,1)} %wq_ref.1) | copy-start | bytes 24580
  2.1 14.7 %copy-start.1 = (bf16[64,64]{1,0:T(8,128)(2,1)S(1)}, bf16[64,64]{1,0:T(8,128)(2,1)}, u32[]{:S(2)}) copy-start(bf16[64,64]{1,0:T(8,128)(2,1)} %wk_ref.1) | copy-start | bytes 24580
  2.1 14.7 %copy-start.2 = (s32[7,2,128]{2,1,0:T(2,128)S(1)}, s32[7,2,128]{2,1,0:T(2,128)}, u32[]{:S(2)}) copy-start(s32[7,2,128]{2,1,0:T(2,128)} %idx_ref.3) | copy-start | bytes 21508
  2.1 14.7 %copy-start.3 = (bf16[64,64]{1,0:T(8,128)(2,1)S(1)}, bf16[64,64]{1,0:T(8,128)(2,1)}, u32[]{:S(2)}) copy-start(bf16[64,64]{1,0:T(8,128)(2,1)} %refs_2_.3) | copy-start | bytes 24580
  2.1 14.7 %copy-start.4 = (bf16[64,64]{1,0:T(8,128)(2,1)S(1)}, bf16[64,64]{1,0:T(8,128)(2,1)}, u32[]{:S(2)}) copy-start(bf16[64,64]{1,0:T(8,128)(2,1)} %refs_3_.3) | copy-start | bytes 24580
  2.1 14.7 %copy-start.5 = (bf16[64,128]{1,0:T(8,128)(2,1)S(1)}, bf16[64,128]{1,0:T(8,128)(2,1)}, u32[]{:S(2)}) copy-start(bf16[64,128]{1,0:T(8,128)(2,1)} %refs_4_.3) | copy-start | bytes 49156
  2.2 14.7 %copy-start.6 = (bf16[128,64]{0,1:T(8,128)(2,1)S(1)}, bf16[128,64]{0,1:T(8,128)(2,1)}, u32[]{:S(2)}) copy-start(bf16[128,64]{0,1:T(8,128)(2,1)} %param.37) | copy-start | bytes 49156
  16.9 1.3 %collective-permute-start = (f32[136,128]{1,0:T(8,128)S(1)}, f32[136,128]{1,0:T(8,128)S(1)}, u32[]{:S(2)}, u32[]{:S(2)}) collective-permute-start(f32[136,128]{1,0:T(8,128)S(1)} %get-tuple-element.58), channel_id=1, source_target_pairs={{0,8},{8,0},{16,24},{24,16},{1,9},{9,1},{17,25},{25,17},{2,10},{10... | collective-permute-start | bytes 208904 | tf_op jit(solution)/shard_map/ppermute | solution.py:643
  39.1 3.7 %collective-permute-start.3 = (bf16[136,128]{1,0:T(8,128)(2,1)S(1)}, bf16[136,128]{1,0:T(8,128)(2,1)S(1)}, u32[]{:S(2)}, u32[]{:S(2)}) collective-permute-start(bf16[136,128]{1,0:T(8,128)(2,1)S(1)} %shard_map.335.refs_0_), channel_id=1, source_target_pairs={{0,24},{8,16},{16,8},{24,0},{1,25},{9,17},{17,9},{25,1},{2,26},{10... | collective-permute-start | bytes 104456 | tf_op jit(solution)/shard_map/ppermute | solution.py:655
  39.2 4.1 %collective-permute-start.2 = (bf16[136,128]{1,0:T(8,128)(2,1)S(1)}, bf16[136,128]{1,0:T(8,128)(2,1)S(1)}, u32[]{:S(2)}, u32[]{:S(2)}) collective-permute-start(bf16[136,128]{1,0:T(8,128)(2,1)S(1)} %shard_map.335.refs_0_), channel_id=1, source_target_pairs={{0,16},{8,24},{16,0},{24,8},{1,17},{9,25},{17,1},{25,9},{2,18},{10... | collective-permute-start | bytes 104456 | tf_op jit(solution)/shard_map/ppermute | solution.py:655
  40.8 2.5 %collective-permute-start.1 = (bf16[136,128]{1,0:T(8,128)(2,1)S(1)}, bf16[136,128]{1,0:T(8,128)(2,1)S(1)}, u32[]{:S(2)}, u32[]{:S(2)}) collective-permute-start(bf16[136,128]{1,0:T(8,128)(2,1)S(1)} %shard_map.335.refs_0_), channel_id=1, source_target_pairs={{0,8},{8,0},{16,24},{24,16},{1,9},{9,1},{17,25},{25,17},{2,10},{10... | collective-permute-start | bytes 104456 | tf_op jit(solution)/shard_map/ppermute | solution.py:655

commit v8 on v7

--- a/solution.py
+++ b/solution.py
@@ -12,7 +12,7 @@
 EPS = 1e-05
 RIDGE = 0.1
 FAR = 640.0
-SEG_ROWS = 8
+SEG_ROWS = 16
 FIRST = 1
 GRAD_ROWS = 272
 NORM_ROW = 131

time: 44.3 us -> 44.7 us (level)
  no operation moved by 1% of the time
where the time goes in v8:
time: 44.7 us; the launch traced here: 44.4 us
  blocking collectives  35.8 us (80%)
  waiting for transfers between devices  2.66 us (6%)
  starting transfers between devices  1.99 us (4%)
  Pallas kernels  1.74 us (4%)
  other arithmetic  1.17 us (3%)
  between operations  0.98 us (2%)
    all_to_all x1, blocking collectives, shards(): got = lax.all_to_all(back, 'tok', 0, 0, tiled=True)  21 us
    all_to_all x1, blocking collectives, shards(): got = lax.all_to_all(sent, 'tok', 0, 0, tiled=True)  14.7 us
    ppermute x3, starting transfers between devices, from_xor(): return lax.ppermute(array, 'rows', [(i, i ^ m) for i in range(n_rows)])  1.92 us
    pallas_call x6, Pallas kernels, call(): pl.pallas_call(kernel, out_shape=outs, in_specs=[vmem] * len(args), out_s...  1.74 us
    ppermute x3, waiting for transfers between devices, from_xor(): return lax.ppermute(array, 'rows', [(i, i ^ m) for i in range(n_rows)])  1.46 us
    ppermute x1, waiting for transfers between devices, shards(): send = lax.ppermute(send, 'rows', [(i, i ^ 1) for i in range(n_rows)])  1.2 us
    concatenate x1, other arithmetic, shards(): jnp.concatenate([tokens_in, grad_out], 2)  1.12 us
  transfers between devices with their start and end apart: 4, of which 3 were waited for; matrix products, arithmetic and copies ran while one was open for 0% of the time, Pallas kernels for 2%

profile of v8, /device:TPU:0, one launch (start us, length us, event | category | flops | bytes accessed | tf_op | source)
XLA Modules:
  0.0 44.4 jit_solution(2232215899479798586)
XLA Ops:
  0.7 0.0 copy-start.17
  0.7 0.0 copy-start.16
  0.7 0.0 copy-start.15
  0.7 0.0 copy-start.14
  0.7 0.0 copy-start.13
  0.7 0.0 copy-start.12
  0.7 0.0 copy-start.11
  0.7 0.0 copy-start.10
  0.7 0.0 copy-start.9
  0.8 0.0 copy-start.8
  0.8 0.0 copy-start.7
  0.8 1.1 %pad_maximum_fusion.1.xg_ref = bf16[7,64,128]{2,1,0:T(8,128)(2,1)S(1)} fusion(bf16[7,64,64]{2,1,0:T(8,128)(2,1)} %param.39, bf16[7,64,64]{2,1,0:T(8,128)(2,1)} %param.20), kind=kLoop, calls=%fused_computation.1 | loop fusion | flops 229376 | bytes 229376 | tf_op jit(solution)/shard_map/concatenate | solution.py:620
  1.9 0.0 copy-done.17
  1.9 0.0 copy-done.16
  1.9 0.0 copy-done.15
  1.9 0.0 copy-done.14
  1.9 0.0 copy-done.13
  1.9 0.0 copy-done.12
  2.0 0.0 copy-done.11
  2.0 0.0 copy-done.10
  2.0 0.0 copy-done.9
  2.0 0.0 copy-done.8
  2.0 0.0 copy-done.7
  2.0 0.1 shard_map.331
  2.1 0.0 copy-start.1
  2.1 0.0 copy-start.2
  2.1 0.0 copy-start.3
  2.1 0.0 copy-start.4
  2.1 0.0 copy-start.5
  2.2 0.0 copy-start.6
  2.2 14.7 %all_to_all.10.blk_ref = bf16[8,80,128]{2,1,0:T(8,128)(2,1)S(1)} all-to-all(bf16[8,80,128]{2,1,0:T(8,128)(2,1)S(1)} %get-tuple-element.49), channel_id=1, replica_groups=mesh['rows'=4,'tok'=8] {'tok'}, dimensions={0} | all-to-all | bytes 327680 | tf_op jit(solution)/shard_map/all_to_all | solution.py:625
  16.9 0.0 copy-done
  16.9 0.0 copy-done.1
  16.9 0.0 copy-done.2
  16.9 0.0 copy-done.3
  16.9 0.0 copy-done.4
  16.9 0.0 copy-done.5
  17.0 0.1 collective-permute-start
  17.1 1.2 %collective-permute-done = f32[136,128]{1,0:T(8,128)S(1)} collective-permute-done((f32[136,128]{1,0:T(8,128)S(1)}, f32[136,128]{1,0:T(8,128)S(1)}, u32[]{:S(2)}, u32[]{:S(2)}) %collective-permute-start) | collective-permute-done | bytes 69664 | tf_op jit(solution)/shard_map/ppermute | solution.py:643
  18.4 21.0 %all_to_all.11.got_ref = bf16[8,200,128]{2,1,0:T(8,128)(2,1)S(1)} all-to-all(bf16[8,200,128]{2,1,0:T(8,128)(2,1)S(1)} %pad_maximum_fusion), channel_id=1, replica_groups=mesh['rows'=4,'tok'=8] {'tok'}, dimensions={0} | all-to-all | bytes 819200 | tf_op jit(solution)/shard_map/all_to_all | solution.py:659
  39.5 0.1 collective-permute-start.3
  39.6 1.6 %collective-permute-start.2 = (bf16[136,128]{1,0:T(8,128)(2,1)S(1)}, bf16[136,128]{1,0:T(8,128)(2,1)S(1)}, u32[]{:S(2)}, u32[]{:S(2)}) collective-permute-start(bf16[136,128]{1,0:T(8,128)(2,1)S(1)} %shard_map.335.refs_0_), channel_id=1, source_target_pairs={{0,16},{8,24},{16,0},{24,8},{1,17},{9,25},{17,1},{25,9},{2,18},{10... | collective-permute-start | bytes 104456 | tf_op jit(solution)/shard_map/ppermute | solution.py:655
  41.2 0.3 collective-permute-start.1
  41.4 0.8 %shard_map.334 = (bf16[7,64,64]{2,1,0:T(8,128)(2,1)}, f32[7,64,64]{2,1,0:T(8,128)}) custom-call(bf16[8,200,128]{2,1,0:T(8,128)(2,1)S(1)} %all_to_all.11.got_ref), custom_call_target="tpu_custom_call" | custom-call | tf_op jit(solution)/shard_map/pallas_call | solution.py:602
  42.2 1.0 %collective-permute-done.3.refs_3_ = bf16[136,128]{1,0:T(8,128)(2,1)S(1)} collective-permute-done((bf16[136,128]{1,0:T(8,128)(2,1)S(1)}, bf16[136,128]{1,0:T(8,128)(2,1)S(1)}, u32[]{:S(2)}, u32[]{:S(2)}) %collective-permute-start.3) | collective-permute-done | bytes 34848 | tf_op jit(solution)/shard_map/ppermute | solution.py:655
  43.2 0.4 %collective-permute-done.2.refs_2_ = bf16[136,128]{1,0:T(8,128)(2,1)S(1)} collective-permute-done((bf16[136,128]{1,0:T(8,128)(2,1)S(1)}, bf16[136,128]{1,0:T(8,128)(2,1)S(1)}, u32[]{:S(2)}, u32[]{:S(2)}) %collective-permute-start.2) | collective-permute-done | bytes 34848 | tf_op jit(solution)/shard_map/ppermute | solution.py:655
  43.7 0.0 collective-permute-done.1.refs_1_
  43.7 0.8 %shard_map.336 = (f32[64]{0:T(128)}, f32[64]{0:T(128)}, f32[64,64]{1,0:T(8,128)}, f32[64]{0:T(128)}, f32[64,64]{1,0:T(8,128)}, /*index=5*/f32[64]{0:T(128)}, f32...) custom-call(bf16[136,128]{1,0:T(8,128)(2,1)S(1)} %shard_map.335.refs, ...), custom_call_target="tpu_custom_call" | custom-call | tf_op jit(solution)/shard_map/pallas_call | solution.py:602
  (8 shorter events, 0.2 us)
Async XLA Ops:
  0.7 1.2 %copy-start.17 = (bf16[64]{0:T(256)(128)(2,1)S(1)}, bf16[64]{0:T(256)(128)(2,1)}, u32[]{:S(2)}) copy-start(bf16[64]{0:T(256)(128)(2,1)} %refs_9_.1) | copy-start | bytes 388
  0.7 1.2 %copy-start.16 = (bf16[128]{0:T(256)(128)(2,1)S(1)}, bf16[128]{0:T(256)(128)(2,1)}, u32[]{:S(2)}) copy-start(bf16[128]{0:T(256)(128)(2,1)} %refs_8_.1) | copy-start | bytes 772
  0.7 1.2 %copy-start.15 = (bf16[64]{0:T(256)(128)(2,1)S(1)}, bf16[64]{0:T(256)(128)(2,1)}, u32[]{:S(2)}) copy-start(bf16[64]{0:T(256)(128)(2,1)} %refs_7_.1) | copy-start | bytes 388
  0.7 1.2 %copy-start.14 = (bf16[64]{0:T(256)(128)(2,1)S(1)}, bf16[64]{0:T(256)(128)(2,1)}, u32[]{:S(2)}) copy-start(bf16[64]{0:T(256)(128)(2,1)} %refs_6_.1) | copy-start | bytes 388
  0.7 1.2 %copy-start.13 = (bf16[64]{0:T(256)(128)(2,1)S(1)}, bf16[64]{0:T(256)(128)(2,1)}, u32[]{:S(2)}) copy-start(bf16[64]{0:T(256)(128)(2,1)} %refs_5_.1) | copy-start | bytes 388
  0.7 1.2 %copy-start.12 = (bf16[64]{0:T(256)(128)(2,1)S(1)}, bf16[64]{0:T(256)(128)(2,1)}, u32[]{:S(2)}) copy-start(bf16[64]{0:T(256)(128)(2,1)} %refs_4_.2) | copy-start | bytes 388
  0.7 1.2 %copy-start.11 = (bf16[64]{0:T(256)(128)(2,1)S(1)}, bf16[64]{0:T(256)(128)(2,1)}, u32[]{:S(2)}) copy-start(bf16[64]{0:T(256)(128)(2,1)} %refs_3_.2) | copy-start | bytes 388
  0.7 1.2 %copy-start.10 = (bf16[64]{0:T(256)(128)(2,1)S(1)}, bf16[64]{0:T(256)(128)(2,1)}, u32[]{:S(2)}) copy-start(bf16[64]{0:T(256)(128)(2,1)} %refs_2_.2) | copy-start | bytes 388
  0.7 1.2 %copy-start.9 = (bf16[64]{0:T(256)(128)(2,1)S(1)}, bf16[64]{0:T(256)(128)(2,1)}, u32[]{:S(2)}) copy-start(bf16[64]{0:T(256)(128)(2,1)} %refs_1_.2) | copy-start | bytes 388
  0.8 1.2 %copy-start.8 = (bf16[64]{0:T(256)(128)(2,1)S(1)}, bf16[64]{0:T(256)(128)(2,1)}, u32[]{:S(2)}) copy-start(bf16[64]{0:T(256)(128)(2,1)} %refs_0_.2) | copy-start | bytes 388
  0.8 1.2 %copy-start.7 = (s32[7,64]{1,0:T(8,128)S(1)}, s32[7,64]{1,0:T(8,128)}, u32[]{:S(2)}) copy-start(s32[7,64]{1,0:T(8,128)} %s_ref.1) | copy-start | bytes 5380
  2.1 14.8 %copy-start = (bf16[64,64]{1,0:T(8,128)(2,1)S(1)}, bf16[64,64]{1,0:T(8,128)(2,1)}, u32[]{:S(2)}) copy-start(bf16[64,64]{1,0:T(8,128)(2,1)} %wq_ref.1) | copy-start | bytes 24580
  2.1 14.8 %copy-start.1 = (bf16[64,64]{1,0:T(8,128)(2,1)S(1)}, bf16[64,64]{1,0:T(8,128)(2,1)}, u32[]{:S(2)}) copy-start(bf16[64,64]{1,0:T(8,128)(2,1)} %wk_ref.1) | copy-start | bytes 24580
  2.1 14.8 %copy-start.2 = (s32[7,2,128]{2,1,0:T(2,128)S(1)}, s32[7,2,128]{2,1,0:T(2,128)}, u32[]{:S(2)}) copy-start(s32[7,2,128]{2,1,0:T(2,128)} %idx_ref.3) | copy-start | bytes 21508
  2.1 14.8 %copy-start.3 = (bf16[64,64]{1,0:T(8,128)(2,1)S(1)}, bf16[64,64]{1,0:T(8,128)(2,1)}, u32[]{:S(2)}) copy-start(bf16[64,64]{1,0:T(8,128)(2,1)} %refs_2_.3) | copy-start | bytes 24580
  2.1 14.8 %copy-start.4 = (bf16[64,64]{1,0:T(8,128)(2,1)S(1)}, bf16[64,64]{1,0:T(8,128)(2,1)}, u32[]{:S(2)}) copy-start(bf16[64,64]{1,0:T(8,128)(2,1)} %refs_3_.3) | copy-start | bytes 24580
  2.1 14.8 %copy-start.5 = (bf16[64,128]{1,0:T(8,128)(2,1)S(1)}, bf16[64,128]{1,0:T(8,128)(2,1)}, u32[]{:S(2)}) copy-start(bf16[64,128]{1,0:T(8,128)(2,1)} %refs_4_.3) | copy-start | bytes 49156
  2.2 14.8 %copy-start.6 = (bf16[128,64]{0,1:T(8,128)(2,1)S(1)}, bf16[128,64]{0,1:T(8,128)(2,1)}, u32[]{:S(2)}) copy-start(bf16[128,64]{0,1:T(8,128)(2,1)} %param.37) | copy-start | bytes 49156
  17.0 1.3 %collective-permute-start = (f32[136,128]{1,0:T(8,128)S(1)}, f32[136,128]{1,0:T(8,128)S(1)}, u32[]{:S(2)}, u32[]{:S(2)}) collective-permute-start(f32[136,128]{1,0:T(8,128)S(1)} %get-tuple-element.58), channel_id=1, source_target_pairs={{0,8},{8,0},{16,24},{24,16},{1,9},{9,1},{17,25},{25,17},{2,10},{10... | collective-permute-start | bytes 208904 | tf_op jit(solution)/shard_map/ppermute | solution.py:643
  39.5 3.7 %collective-permute-start.3 = (bf16[136,128]{1,0:T(8,128)(2,1)S(1)}, bf16[136,128]{1,0:T(8,128)(2,1)S(1)}, u32[]{:S(2)}, u32[]{:S(2)}) collective-permute-start(bf16[136,128]{1,0:T(8,128)(2,1)S(1)} %shard_map.335.refs_0_), channel_id=1, source_target_pairs={{0,24},{8,16},{16,8},{24,0},{1,25},{9,17},{17,9},{25,1},{2,26},{10... | collective-permute-start | bytes 104456 | tf_op jit(solution)/shard_map/ppermute | solution.py:655
  39.6 4.1 %collective-permute-start.2 = (bf16[136,128]{1,0:T(8,128)(2,1)S(1)}, bf16[136,128]{1,0:T(8,128)(2,1)S(1)}, u32[]{:S(2)}, u32[]{:S(2)}) collective-permute-start(bf16[136,128]{1,0:T(8,128)(2,1)S(1)} %shard_map.335.refs_0_), channel_id=1, source_target_pairs={{0,16},{8,24},{16,0},{24,8},{1,17},{9,25},{17,1},{25,9},{2,18},{10... | collective-permute-start | bytes 104456 | tf_op jit(solution)/shard_map/ppermute | solution.py:655
  41.2 2.5 %collective-permute-start.1 = (bf16[136,128]{1,0:T(8,128)(2,1)S(1)}, bf16[136,128]{1,0:T(8,128)(2,1)S(1)}, u32[]{:S(2)}, u32[]{:S(2)}) collective-permute-start(bf16[136,128]{1,0:T(8,128)(2,1)S(1)} %shard_map.335.refs_0_), channel_id=1, source_target_pairs={{0,8},{8,0},{16,24},{24,16},{1,9},{9,1},{17,25},{25,17},{2,10},{10... | collective-permute-start | bytes 104456 | tf_op jit(solution)/shard_map/ppermute | solution.py:655

commit v9 on v7

--- a/solution.py
+++ b/solution.py
@@ -284,24 +284,7 @@
     d_sent_t = mm(d_branch, near_q_tok) * out_scale
     back = [d_sent_t[:, at[h]] for h in hs]
 
-    beside_gram = [pair(sent_t[h].T, -gram[h]).astype(bf16) for h in hs]
-    kernel_inv = [kernel[h] * inv2[h] for h in hs]
-    widest_a = [(2.0 / widest[h]) * (eye - rests[0][h]) for h in hs]
-    widest_b = [(2.0 / widest[h]) * grown[0][h] for h in hs]
     mark_both = jnp.concatenate([mark16, own.astype(bf16)], 0)
-    mark_ones = [
-        jnp.concatenate([mark16[:, at[h]], jnp.ones((16, marks), bf16)], 0) for h in hs
-    ]
-    top_part = []
-    for h in hs:
-        top = (sums[h] == widest[h]).astype(f32)
-        top = top * (1.0 / row_sum(top))
-        seen = kernel[h].astype(bf16)
-        along = jnp.broadcast_to(top, (16, marks)).astype(bf16)
-        top_part.append(
-            top * mm(mark_ones[h], seen)
-            + mm_nt(mark_ones[h], along)[:, :1] * mm(along, seen)[:1]
-        )
     mixed = [mm_wide(summed_t[h], inverse_wide[h]) for h in hs]
     blank_h = jnp.zeros((size, marks), f32)
     mixed_m = jnp.concatenate(
@@ -311,16 +294,6 @@
     q_tok = q_t.astype(f32).T.astype(bf16)
     k_tok = k_t.astype(f32).T.astype(bf16)
     ones_tok = jnp.ones((tokens, width), bf16)
-    d_start = [mm_wide(back[h], inverse_wide[h]) for h in hs]
-    d_att_early = mm(wo, d_branch).astype(bf16)
-    d_mixed = mm(d_att_early, near_q_tok) * out_scale
-    d_mixed = [d_mixed[rows_of[h], at[h]].astype(bf16) for h in hs]
-    d_summed = [both_parts_left(d_mixed[h], inverse_wide[h]) for h in hs]
-    none = jnp.zeros((size, marks), f32)
-    d_summed_t = jnp.concatenate(
-        [jnp.concatenate([d_summed[h] if g == h else none for g in hs], 1) for h in hs], 0
-    )
-    d_summed_m = d_summed_t.T.astype(bf16)
     def stays(pull, p_t):
         both = mm(mark_both, pull)
         return sharp * (both[:width] - both[width:] * p_t.astype(f32))
@@ -333,7 +306,7 @@
         pulls_q.append((pull.astype(f32) * near_q[:, now_at].astype(f32)).astype(bf16))
 
     def pull_rest():
-        pull = mm(d_summed_m, v_t).astype(bf16)
+        pull = mm(early["d_summed_m"], v_t).astype(bf16)
         pulls_q.append((pull.astype(f32) * near_k.astype(f32)).astype(bf16))
 
     def add_tok(pull, tok):
@@ -347,6 +320,52 @@
         add_tok(pulls_q[1], k_tok)
 
     early = {}
+    first_back = back
+
+    def add_end():
+        beside_gram = [pair(sent_t[h].T, -gram[h]).astype(bf16) for h in hs]
+        kernel_inv = [kernel[h] * inv2[h] for h in hs]
+        widest_a = [(2.0 / widest[h]) * (eye - rests[0][h]) for h in hs]
+        widest_b = [(2.0 / widest[h]) * grown[0][h] for h in hs]
+        mark_ones = [
+            jnp.concatenate([mark16[:, at[h]], jnp.ones((16, marks), bf16)], 0) for h in hs
+        ]
+        top_part = []
+        for h in hs:
+            top = (sums[h] == widest[h]).astype(f32)
+            top = top * (1.0 / row_sum(top))
+            seen = kernel[h].astype(bf16)
+            along = jnp.broadcast_to(top, (16, marks)).astype(bf16)
+            top_part.append(
+                top * mm(mark_ones[h], seen)
+                + mm_nt(mark_ones[h], along)[:, :1] * mm(along, seen)[:1]
+            )
+        early.update(
+            beside_gram=beside_gram,
+            kernel_inv=kernel_inv,
+            widest_a=widest_a,
+            widest_b=widest_b,
+            mark_ones=mark_ones,
+            top_part=top_part,
+        )
+
+    def add_summed():
+        d_start = [mm_wide(first_back[h], inverse_wide[h]) for h in hs]
+        d_att_early = mm(wo, d_branch).astype(bf16)
+        d_mixed = mm(d_att_early, near_q_tok) * out_scale
+        d_mixed = [d_mixed[rows_of[h], at[h]].astype(bf16) for h in hs]
+        d_summed = [both_parts_left(d_mixed[h], inverse_wide[h]) for h in hs]
+        none = jnp.zeros((size, marks), f32)
+        d_summed_t = jnp.concatenate(
+            [jnp.concatenate([d_summed[h] if g == h else none for g in hs], 1) for h in hs], 0
+        )
+        d_summed_m = d_summed_t.T.astype(bf16)
+        early.update(
+            d_start=d_start,
+            d_summed_t=d_summed_t,
+            d_summed_m=d_summed_m,
+        )
+
 
     def add_down():
         early["down"] = mm_nt(g16_t, act)
@@ -359,12 +378,12 @@
 
     def add_wo():
         early["wo"] = jnp.concatenate(
-            [mm_nt(summed_t[h].astype(bf16), d_start[h].astype(bf16)) for h in hs], 0
+            [mm_nt(summed_t[h].astype(bf16), early["d_start"][h].astype(bf16)) for h in hs], 0
         )
 
     def add_stay():
         stay_q, stay_k = stays(pulls_q[0], q_t), stays(pulls_q[1], k_t)
-        dv = mm(d_summed_t.astype(bf16), near_k)
+        dv = mm(early["d_summed_t"].astype(bf16), near_k)
         early["stay"] = jnp.concatenate([stay_q, stay_k, dv], 0).astype(bf16)
 
     def add_qkv():
@@ -374,11 +393,11 @@
         early["normed"] = mm(wqkv, early["stay"])
 
     beside = [
-        [partial(pull_some, 0), partial(pull_some, 1), partial(pull_some, 2), partial(pull_some, 3)],
-        [add_tok_q, pull_rest],
-        [add_tok_k],
+        [add_summed, partial(pull_some, 0), partial(pull_some, 1)],
+        [partial(pull_some, 2), partial(pull_some, 3), pull_rest],
+        [add_tok_q, add_tok_k],
         [add_stay],
-        [add_up, add_down],
+        [add_up, add_down, add_end],
         [add_qkv, add_normed, add_bias, add_wo],
     ]
     b16 = [back[h].astype(bf16) for h in hs]
@@ -399,7 +418,7 @@
             work()
     d16 = [d_rest[h].astype(bf16) for h in hs]
     d_gram = [
-        mm(beside_gram[h], jnp.concatenate([back[h].astype(bf16), d16[h]], 0))
+        mm(early["beside_gram"][h], jnp.concatenate([back[h].astype(bf16), d16[h]], 0))
         - wide_mm(d16[h], gram_wide[h][:marks])
         for h in hs
     ]
@@ -408,9 +427,9 @@
     stay, d_normed_tok = early["stay"], early["normed"]
     gram_part = []
     for h in hs:
-        d_widest = total_of(d_rest[h] * widest_a[h]) - total_of(back[h] * widest_b[h])
-        weighted = ((d_gram[h] + d_gram[h].T) * kernel_inv[h]).astype(bf16)
-        gram_part.append(mm(mark_ones[h], weighted) + d_widest * top_part[h])
+        d_widest = total_of(d_rest[h] * early["widest_a"][h]) - total_of(back[h] * early["widest_b"][h])
+        weighted = ((d_gram[h] + d_gram[h].T) * early["kernel_inv"][h]).astype(bf16)
+        gram_part.append(mm(early["mark_ones"][h], weighted) + d_widest * early["top_part"][h])
     gram_part = jnp.concatenate(gram_part, 1)
     d_mark_t = (
         (tok_t + gram_part[:width] - mark_t * (tok_sum + gram_part[width : width + 1])) * own

time: 44.3 us -> 44.4 us (level)
  no operation moved by 1% of the time
where the time goes in v9:
time: 44.4 us; the launch traced here: 44.1 us
  blocking collectives  35.5 us (80%)
  waiting for transfers between devices  2.66 us (6%)
  starting transfers between devices  1.99 us (4%)
  Pallas kernels  1.74 us (4%)
  other arithmetic  1.17 us (3%)
  between operations  0.98 us (2%)
    all_to_all x1, blocking collectives, shards(): got = lax.all_to_all(back, 'tok', 0, 0, tiled=True)  20.8 us
    all_to_all x1, blocking collectives, shards(): got = lax.all_to_all(sent, 'tok', 0, 0, tiled=True)  14.6 us
    ppermute x3, starting transfers between devices, from_xor(): return lax.ppermute(array, 'rows', [(i, i ^ m) for i in range(n_rows)])  1.92 us
    pallas_call x6, Pallas kernels, call(): pl.pallas_call(kernel, out_shape=outs, in_specs=[vmem] * len(args), out_s...  1.74 us
    ppermute x3, waiting for transfers between devices, from_xor(): return lax.ppermute(array, 'rows', [(i, i ^ m) for i in range(n_rows)])  1.46 us
    ppermute x1, waiting for transfers between devices, shards(): send = lax.ppermute(send, 'rows', [(i, i ^ 1) for i in range(n_rows)])  1.2 us
    concatenate x1, other arithmetic, shards(): jnp.concatenate([tokens_in, grad_out], 2)  1.12 us
  transfers between devices with their start and end apart: 4, of which 3 were waited for; matrix products, arithmetic and copies ran while one was open for 0% of the time, Pallas kernels for 2%

profile of v9, /device:TPU:0, one launch (start us, length us, event | category | flops | bytes accessed | tf_op | source)
XLA Modules:
  0.0 44.1 jit_solution(5885596921006602064)
XLA Ops:
  0.7 0.0 copy-start.17
  0.7 0.0 copy-start.16
  0.7 0.0 copy-start.15
  0.7 0.0 copy-start.14
  0.7 0.0 copy-start.13
  0.7 0.0 copy-start.12
  0.7 0.0 copy-start.11
  0.7 0.0 copy-start.10
  0.7 0.0 copy-start.9
  0.8 0.0 copy-start.8
  0.8 0.0 copy-start.7
  0.8 1.1 %pad_maximum_fusion.1.xg_ref = bf16[7,64,128]{2,1,0:T(8,128)(2,1)S(1)} fusion(bf16[7,64,64]{2,1,0:T(8,128)(2,1)} %param.39, bf16[7,64,64]{2,1,0:T(8,128)(2,1)} %param.20), kind=kLoop, calls=%fused_computation.1 | loop fusion | flops 229376 | bytes 229376 | tf_op jit(solution)/shard_map/concatenate | solution.py:639
  1.9 0.0 copy-done.17
  1.9 0.0 copy-done.16
  1.9 0.0 copy-done.15
  1.9 0.0 copy-done.14
  1.9 0.0 copy-done.13
  1.9 0.0 copy-done.12
  2.0 0.0 copy-done.11
  2.0 0.0 copy-done.10
  2.0 0.0 copy-done.9
  2.0 0.0 copy-done.8
  2.0 0.0 copy-done.7
  2.0 0.1 shard_map.331
  2.1 0.0 copy-start.2
  2.1 0.0 copy-start.3
  2.1 0.0 copy-start.4
  2.1 0.0 copy-start.5
  2.2 0.0 copy-start.6
  2.2 14.6 %all_to_all.10.blk_ref = bf16[8,72,128]{2,1,0:T(8,128)(2,1)S(1)} all-to-all(bf16[8,72,128]{2,1,0:T(8,128)(2,1)S(1)} %get-tuple-element.49), channel_id=1, replica_groups=mesh['rows'=4,'tok'=8] {'tok'}, dimensions={0} | all-to-all | bytes 294912 | tf_op jit(solution)/shard_map/all_to_all | solution.py:644
  16.8 0.0 copy-done
  16.8 0.0 copy-done.1
  16.8 0.0 copy-done.2
  16.8 0.0 copy-done.3
  16.8 0.0 copy-done.4
  16.8 0.0 copy-done.5
  16.8 0.0 copy-done.6
  16.9 0.1 collective-permute-start
  17.0 1.2 %collective-permute-done = f32[136,128]{1,0:T(8,128)S(1)} collective-permute-done((f32[136,128]{1,0:T(8,128)S(1)}, f32[136,128]{1,0:T(8,128)S(1)}, u32[]{:S(2)}, u32[]{:S(2)}) %collective-permute-start) | collective-permute-done | bytes 69664 | tf_op jit(solution)/shard_map/ppermute | solution.py:662
  18.3 20.8 %all_to_all.11.got_ref = bf16[8,200,128]{2,1,0:T(8,128)(2,1)S(1)} all-to-all(bf16[8,200,128]{2,1,0:T(8,128)(2,1)S(1)} %pad_maximum_fusion), channel_id=1, replica_groups=mesh['rows'=4,'tok'=8] {'tok'}, dimensions={0} | all-to-all | bytes 819200 | tf_op jit(solution)/shard_map/all_to_all | solution.py:678
  39.2 0.1 collective-permute-start.3
  39.3 1.6 %collective-permute-start.2 = (bf16[136,128]{1,0:T(8,128)(2,1)S(1)}, bf16[136,128]{1,0:T(8,128)(2,1)S(1)}, u32[]{:S(2)}, u32[]{:S(2)}) collective-permute-start(bf16[136,128]{1,0:T(8,128)(2,1)S(1)} %shard_map.335.refs_0_), channel_id=1, source_target_pairs={{0,16},{8,24},{16,0},{24,8},{1,17},{9,25},{17,1},{25,9},{2,18},{10... | collective-permute-start | bytes 104456 | tf_op jit(solution)/shard_map/ppermute | solution.py:674
  40.8 0.3 collective-permute-start.1
  41.1 0.8 %shard_map.334 = (bf16[7,64,64]{2,1,0:T(8,128)(2,1)}, f32[7,64,64]{2,1,0:T(8,128)}) custom-call(bf16[8,200,128]{2,1,0:T(8,128)(2,1)S(1)} %all_to_all.11.got_ref), custom_call_target="tpu_custom_call" | custom-call | tf_op jit(solution)/shard_map/pallas_call | solution.py:621
  41.9 1.0 %collective-permute-done.3.refs_3_ = bf16[136,128]{1,0:T(8,128)(2,1)S(1)} collective-permute-done((bf16[136,128]{1,0:T(8,128)(2,1)S(1)}, bf16[136,128]{1,0:T(8,128)(2,1)S(1)}, u32[]{:S(2)}, u32[]{:S(2)}) %collective-permute-start.3) | collective-permute-done | bytes 34848 | tf_op jit(solution)/shard_map/ppermute | solution.py:674
  42.9 0.4 %collective-permute-done.2.refs_2_ = bf16[136,128]{1,0:T(8,128)(2,1)S(1)} collective-permute-done((bf16[136,128]{1,0:T(8,128)(2,1)S(1)}, bf16[136,128]{1,0:T(8,128)(2,1)S(1)}, u32[]{:S(2)}, u32[]{:S(2)}) %collective-permute-start.2) | collective-permute-done | bytes 34848 | tf_op jit(solution)/shard_map/ppermute | solution.py:674
  43.4 0.0 collective-permute-done.1.refs_1_
  43.4 0.8 %shard_map.336 = (f32[64]{0:T(128)}, f32[64]{0:T(128)}, f32[64,64]{1,0:T(8,128)}, f32[64]{0:T(128)}, f32[64,64]{1,0:T(8,128)}, /*index=5*/f32[64]{0:T(128)}, f32...) custom-call(bf16[136,128]{1,0:T(8,128)(2,1)S(1)} %shard_map.335.refs, ...), custom_call_target="tpu_custom_call" | custom-call | tf_op jit(solution)/shard_map/pallas_call | solution.py:621
  (8 shorter events, 0.2 us)
Async XLA Ops:
  0.7 1.2 %copy-start.17 = (bf16[64]{0:T(256)(128)(2,1)S(1)}, bf16[64]{0:T(256)(128)(2,1)}, u32[]{:S(2)}) copy-start(bf16[64]{0:T(256)(128)(2,1)} %refs_9_.1) | copy-start | bytes 388
  0.7 1.2 %copy-start.16 = (bf16[128]{0:T(256)(128)(2,1)S(1)}, bf16[128]{0:T(256)(128)(2,1)}, u32[]{:S(2)}) copy-start(bf16[128]{0:T(256)(128)(2,1)} %refs_8_.1) | copy-start | bytes 772
  0.7 1.2 %copy-start.15 = (bf16[64]{0:T(256)(128)(2,1)S(1)}, bf16[64]{0:T(256)(128)(2,1)}, u32[]{:S(2)}) copy-start(bf16[64]{0:T(256)(128)(2,1)} %refs_7_.1) | copy-start | bytes 388
  0.7 1.2 %copy-start.14 = (bf16[64]{0:T(256)(128)(2,1)S(1)}, bf16[64]{0:T(256)(128)(2,1)}, u32[]{:S(2)}) copy-start(bf16[64]{0:T(256)(128)(2,1)} %refs_6_.1) | copy-start | bytes 388
  0.7 1.2 %copy-start.13 = (bf16[64]{0:T(256)(128)(2,1)S(1)}, bf16[64]{0:T(256)(128)(2,1)}, u32[]{:S(2)}) copy-start(bf16[64]{0:T(256)(128)(2,1)} %refs_5_.1) | copy-start | bytes 388
  0.7 1.2 %copy-start.12 = (bf16[64]{0:T(256)(128)(2,1)S(1)}, bf16[64]{0:T(256)(128)(2,1)}, u32[]{:S(2)}) copy-start(bf16[64]{0:T(256)(128)(2,1)} %refs_4_.2) | copy-start | bytes 388
  0.7 1.2 %copy-start.11 = (bf16[64]{0:T(256)(128)(2,1)S(1)}, bf16[64]{0:T(256)(128)(2,1)}, u32[]{:S(2)}) copy-start(bf16[64]{0:T(256)(128)(2,1)} %refs_3_.2) | copy-start | bytes 388
  0.7 1.2 %copy-start.10 = (bf16[64]{0:T(256)(128)(2,1)S(1)}, bf16[64]{0:T(256)(128)(2,1)}, u32[]{:S(2)}) copy-start(bf16[64]{0:T(256)(128)(2,1)} %refs_2_.2) | copy-start | bytes 388
  0.7 1.2 %copy-start.9 = (bf16[64]{0:T(256)(128)(2,1)S(1)}, bf16[64]{0:T(256)(128)(2,1)}, u32[]{:S(2)}) copy-start(bf16[64]{0:T(256)(128)(2,1)} %refs_1_.2) | copy-start | bytes 388
  0.8 1.2 %copy-start.8 = (bf16[64]{0:T(256)(128)(2,1)S(1)}, bf16[64]{0:T(256)(128)(2,1)}, u32[]{:S(2)}) copy-start(bf16[64]{0:T(256)(128)(2,1)} %refs_0_.2) | copy-start | bytes 388
  0.8 1.2 %copy-start.7 = (s32[7,64]{1,0:T(8,128)S(1)}, s32[7,64]{1,0:T(8,128)}, u32[]{:S(2)}) copy-start(s32[7,64]{1,0:T(8,128)} %s_ref.1) | copy-start | bytes 5380
  2.1 14.7 %copy-start = (bf16[64,64]{1,0:T(8,128)(2,1)S(1)}, bf16[64,64]{1,0:T(8,128)(2,1)}, u32[]{:S(2)}) copy-start(bf16[64,64]{1,0:T(8,128)(2,1)} %wq_ref.1) | copy-start | bytes 24580
  2.1 14.7 %copy-start.1 = (bf16[64,64]{1,0:T(8,128)(2,1)S(1)}, bf16[64,64]{1,0:T(8,128)(2,1)}, u32[]{:S(2)}) copy-start(bf16[64,64]{1,0:T(8,128)(2,1)} %wk_ref.1) | copy-start | bytes 24580
  2.1 14.7 %copy-start.2 = (s32[7,2,128]{2,1,0:T(2,128)S(1)}, s32[7,2,128]{2,1,0:T(2,128)}, u32[]{:S(2)}) copy-start(s32[7,2,128]{2,1,0:T(2,128)} %idx_ref.3) | copy-start | bytes 21508
  2.1 14.7 %copy-start.3 = (bf16[64,64]{1,0:T(8,128)(2,1)S(1)}, bf16[64,64]{1,0:T(8,128)(2,1)}, u32[]{:S(2)}) copy-start(bf16[64,64]{1,0:T(8,128)(2,1)} %refs_2_.3) | copy-start | bytes 24580
  2.1 14.7 %copy-start.4 = (bf16[64,64]{1,0:T(8,128)(2,1)S(1)}, bf16[64,64]{1,0:T(8,128)(2,1)}, u32[]{:S(2)}) copy-start(bf16[64,64]{1,0:T(8,128)(2,1)} %refs_3_.3) | copy-start | bytes 24580
  2.1 14.7 %copy-start.5 = (bf16[64,128]{1,0:T(8,128)(2,1)S(1)}, bf16[64,128]{1,0:T(8,128)(2,1)}, u32[]{:S(2)}) copy-start(bf16[64,128]{1,0:T(8,128)(2,1)} %refs_4_.3) | copy-start | bytes 49156
  2.2 14.7 %copy-start.6 = (bf16[128,64]{0,1:T(8,128)(2,1)S(1)}, bf16[128,64]{0,1:T(8,128)(2,1)}, u32[]{:S(2)}) copy-start(bf16[128,64]{0,1:T(8,128)(2,1)} %param.37) | copy-start | bytes 49156
  16.9 1.3 %collective-permute-start = (f32[136,128]{1,0:T(8,128)S(1)}, f32[136,128]{1,0:T(8,128)S(1)}, u32[]{:S(2)}, u32[]{:S(2)}) collective-permute-start(f32[136,128]{1,0:T(8,128)S(1)} %get-tuple-element.58), channel_id=1, source_target_pairs={{0,8},{8,0},{16,24},{24,16},{1,9},{9,1},{17,25},{25,17},{2,10},{10... | collective-permute-start | bytes 208904 | tf_op jit(solution)/shard_map/ppermute | solution.py:662
  39.2 3.7 %collective-permute-start.3 = (bf16[136,128]{1,0:T(8,128)(2,1)S(1)}, bf16[136,128]{1,0:T(8,128)(2,1)S(1)}, u32[]{:S(2)}, u32[]{:S(2)}) collective-permute-start(bf16[136,128]{1,0:T(8,128)(2,1)S(1)} %shard_map.335.refs_0_), channel_id=1, source_target_pairs={{0,24},{8,16},{16,8},{24,0},{1,25},{9,17},{17,9},{25,1},{2,26},{10... | collective-permute-start | bytes 104456 | tf_op jit(solution)/shard_map/ppermute | solution.py:674
  39.3 4.1 %collective-permute-start.2 = (bf16[136,128]{1,0:T(8,128)(2,1)S(1)}, bf16[136,128]{1,0:T(8,128)(2,1)S(1)}, u32[]{:S(2)}, u32[]{:S(2)}) collective-permute-start(bf16[136,128]{1,0:T(8,128)(2,1)S(1)} %shard_map.335.refs_0_), channel_id=1, source_target_pairs={{0,16},{8,24},{16,0},{24,8},{1,17},{9,25},{17,1},{25,9},{2,18},{10... | collective-permute-start | bytes 104456 | tf_op jit(solution)/shard_map/ppermute | solution.py:674
  40.8 2.5 %collective-permute-start.1 = (bf16[136,128]{1,0:T(8,128)(2,1)S(1)}, bf16[136,128]{1,0:T(8,128)(2,1)S(1)}, u32[]{:S(2)}, u32[]{:S(2)}) collective-permute-start(bf16[136,128]{1,0:T(8,128)(2,1)S(1)} %shard_map.335.refs_0_), channel_id=1, source_target_pairs={{0,8},{8,0},{16,24},{24,16},{1,9},{9,1},{17,25},{25,17},{2,10},{10... | collective-permute-start | bytes 104456 | tf_op jit(solution)/shard_map/ppermute | solution.py:674

commit v10 on v9

--- a/solution.py
+++ b/solution.py
@@ -677,7 +677,7 @@
     back = jnp.concatenate([out, jnp.broadcast_to(total, (n_tok, h, 128))], 1)
     got = lax.all_to_all(back, "tok", 0, 0, tiled=True)
     mine = call(partial(sum_kernel, tok), sds((h, 128), bf16), got)
-    parts = [mine] + [from_xor(mine, m) for m in range(1, n_rows)]
+    parts = [mine] + [from_xor(mine, m) for m in reversed(range(1, n_rows))][::-1]
     layer_out, grad_input = call(
         rows_kernel, (sds((rows, tok, width), bf16), sds((rows, tok, width), f32)), got
     )

time: 44.4 us -> 44.4 us (level)
  no operation moved by 1% of the time
where the time goes in v10:
time: 44.4 us; the launch traced here: 44.1 us
  blocking collectives  35.5 us (80%)
  waiting for transfers between devices  2.66 us (6%)
  starting transfers between devices  1.99 us (4%)
  Pallas kernels  1.74 us (4%)
  other arithmetic  1.17 us (3%)
  between operations  0.98 us (2%)
    all_to_all x1, blocking collectives, shards(): got = lax.all_to_all(back, 'tok', 0, 0, tiled=True)  20.8 us
    all_to_all x1, blocking collectives, shards(): got = lax.all_to_all(sent, 'tok', 0, 0, tiled=True)  14.6 us
    ppermute x3, starting transfers between devices, from_xor(): return lax.ppermute(array, 'rows', [(i, i ^ m) for i in range(n_rows)])  1.92 us
    pallas_call x6, Pallas kernels, call(): pl.pallas_call(kernel, out_shape=outs, in_specs=[vmem] * len(args), out_s...  1.74 us
    ppermute x3, waiting for transfers between devices, from_xor(): return lax.ppermute(array, 'rows', [(i, i ^ m) for i in range(n_rows)])  1.46 us
    ppermute x1, waiting for transfers between devices, shards(): send = lax.ppermute(send, 'rows', [(i, i ^ 1) for i in range(n_rows)])  1.2 us
    concatenate x1, other arithmetic, shards(): jnp.concatenate([tokens_in, grad_out], 2)  1.12 us
  transfers between devices with their start and end apart: 4, of which 3 were waited for; matrix products, arithmetic and copies ran while one was open for 0% of the time, Pallas kernels for 2%

profile of v10, /device:TPU:0, one launch (start us, length us, event | category | flops | bytes accessed | tf_op | source)
XLA Modules:
  0.0 44.1 jit_solution(5885596921006602064)
XLA Ops:
  0.7 0.0 copy-start.17
  0.7 0.0 copy-start.16
  0.7 0.0 copy-start.15
  0.7 0.0 copy-start.14
  0.7 0.0 copy-start.13
  0.7 0.0 copy-start.12
  0.7 0.0 copy-start.11
  0.7 0.0 copy-start.10
  0.7 0.0 copy-start.9
  0.8 0.0 copy-start.8
  0.8 0.0 copy-start.7
  0.8 1.1 %pad_maximum_fusion.1.xg_ref = bf16[7,64,128]{2,1,0:T(8,128)(2,1)S(1)} fusion(bf16[7,64,64]{2,1,0:T(8,128)(2,1)} %param.39, bf16[7,64,64]{2,1,0:T(8,128)(2,1)} %param.20), kind=kLoop, calls=%fused_computation.1 | loop fusion | flops 229376 | bytes 229376 | tf_op jit(solution)/shard_map/concatenate | solution.py:639
  1.9 0.0 copy-done.17
  1.9 0.0 copy-done.16
  1.9 0.0 copy-done.15
  1.9 0.0 copy-done.14
  1.9 0.0 copy-done.13
  1.9 0.0 copy-done.12
  2.0 0.0 copy-done.11
  2.0 0.0 copy-done.10
  2.0 0.0 copy-done.9
  2.0 0.0 copy-done.8
  2.0 0.0 copy-done.7
  2.0 0.1 shard_map.331
  2.1 0.0 copy-start.2
  2.1 0.0 copy-start.3
  2.1 0.0 copy-start.4
  2.1 0.0 copy-start.5
  2.2 0.0 copy-start.6
  2.2 14.6 %all_to_all.10.blk_ref = bf16[8,72,128]{2,1,0:T(8,128)(2,1)S(1)} all-to-all(bf16[8,72,128]{2,1,0:T(8,128)(2,1)S(1)} %get-tuple-element.49), channel_id=1, replica_groups=mesh['rows'=4,'tok'=8] {'tok'}, dimensions={0} | all-to-all | bytes 294912 | tf_op jit(solution)/shard_map/all_to_all | solution.py:644
  16.8 0.0 copy-done
  16.8 0.0 copy-done.1
  16.8 0.0 copy-done.2
  16.8 0.0 copy-done.3
  16.8 0.0 copy-done.4
  16.8 0.0 copy-done.5
  16.8 0.0 copy-done.6
  16.9 0.1 collective-permute-start
  17.0 1.2 %collective-permute-done = f32[136,128]{1,0:T(8,128)S(1)} collective-permute-done((f32[136,128]{1,0:T(8,128)S(1)}, f32[136,128]{1,0:T(8,128)S(1)}, u32[]{:S(2)}, u32[]{:S(2)}) %collective-permute-start) | collective-permute-done | bytes 69664 | tf_op jit(solution)/shard_map/ppermute | solution.py:662
  18.3 20.8 %all_to_all.11.got_ref = bf16[8,200,128]{2,1,0:T(8,128)(2,1)S(1)} all-to-all(bf16[8,200,128]{2,1,0:T(8,128)(2,1)S(1)} %pad_maximum_fusion), channel_id=1, replica_groups=mesh['rows'=4,'tok'=8] {'tok'}, dimensions={0} | all-to-all | bytes 819200 | tf_op jit(solution)/shard_map/all_to_all | solution.py:678
  39.2 0.1 collective-permute-start.3
  39.3 1.6 %collective-permute-start.2 = (bf16[136,128]{1,0:T(8,128)(2,1)S(1)}, bf16[136,128]{1,0:T(8,128)(2,1)S(1)}, u32[]{:S(2)}, u32[]{:S(2)}) collective-permute-start(bf16[136,128]{1,0:T(8,128)(2,1)S(1)} %shard_map.335.refs_0_), channel_id=1, source_target_pairs={{0,16},{8,24},{16,0},{24,8},{1,17},{9,25},{17,1},{25,9},{2,18},{10... | collective-permute-start | bytes 104456 | tf_op jit(solution)/shard_map/ppermute | solution.py:674
  40.8 0.3 collective-permute-start.1
  41.1 0.8 %shard_map.334 = (bf16[7,64,64]{2,1,0:T(8,128)(2,1)}, f32[7,64,64]{2,1,0:T(8,128)}) custom-call(bf16[8,200,128]{2,1,0:T(8,128)(2,1)S(1)} %all_to_all.11.got_ref), custom_call_target="tpu_custom_call" | custom-call | tf_op jit(solution)/shard_map/pallas_call | solution.py:621
  41.9 1.0 %collective-permute-done.3.refs_3_ = bf16[136,128]{1,0:T(8,128)(2,1)S(1)} collective-permute-done((bf16[136,128]{1,0:T(8,128)(2,1)S(1)}, bf16[136,128]{1,0:T(8,128)(2,1)S(1)}, u32[]{:S(2)}, u32[]{:S(2)}) %collective-permute-start.3) | collective-permute-done | bytes 34848 | tf_op jit(solution)/shard_map/ppermute | solution.py:674
  42.9 0.4 %collective-permute-done.2.refs_2_ = bf16[136,128]{1,0:T(8,128)(2,1)S(1)} collective-permute-done((bf16[136,128]{1,0:T(8,128)(2,1)S(1)}, bf16[136,128]{1,0:T(8,128)(2,1)S(1)}, u32[]{:S(2)}, u32[]{:S(2)}) %collective-permute-start.2) | collective-permute-done | bytes 34848 | tf_op jit(solution)/shard_map/ppermute | solution.py:674
  43.4 0.0 collective-permute-done.1.refs_1_
  43.4 0.8 %shard_map.336 = (f32[64]{0:T(128)}, f32[64]{0:T(128)}, f32[64,64]{1,0:T(8,128)}, f32[64]{0:T(128)}, f32[64,64]{1,0:T(8,128)}, /*index=5*/f32[64]{0:T(128)}, f32...) custom-call(bf16[136,128]{1,0:T(8,128)(2,1)S(1)} %shard_map.335.refs, ...), custom_call_target="tpu_custom_call" | custom-call | tf_op jit(solution)/shard_map/pallas_call | solution.py:621
  (8 shorter events, 0.2 us)
Async XLA Ops:
  0.7 1.2 %copy-start.17 = (bf16[64]{0:T(256)(128)(2,1)S(1)}, bf16[64]{0:T(256)(128)(2,1)}, u32[]{:S(2)}) copy-start(bf16[64]{0:T(256)(128)(2,1)} %refs_9_.1) | copy-start | bytes 388
  0.7 1.2 %copy-start.16 = (bf16[128]{0:T(256)(128)(2,1)S(1)}, bf16[128]{0:T(256)(128)(2,1)}, u32[]{:S(2)}) copy-start(bf16[128]{0:T(256)(128)(2,1)} %refs_8_.1) | copy-start | bytes 772
  0.7 1.2 %copy-start.15 = (bf16[64]{0:T(256)(128)(2,1)S(1)}, bf16[64]{0:T(256)(128)(2,1)}, u32[]{:S(2)}) copy-start(bf16[64]{0:T(256)(128)(2,1)} %refs_7_.1) | copy-start | bytes 388
  0.7 1.2 %copy-start.14 = (bf16[64]{0:T(256)(128)(2,1)S(1)}, bf16[64]{0:T(256)(128)(2,1)}, u32[]{:S(2)}) copy-start(bf16[64]{0:T(256)(128)(2,1)} %refs_6_.1) | copy-start | bytes 388
  0.7 1.2 %copy-start.13 = (bf16[64]{0:T(256)(128)(2,1)S(1)}, bf16[64]{0:T(256)(128)(2,1)}, u32[]{:S(2)}) copy-start(bf16[64]{0:T(256)(128)(2,1)} %refs_5_.1) | copy-start | bytes 388
  0.7 1.2 %copy-start.12 = (bf16[64]{0:T(256)(128)(2,1)S(1)}, bf16[64]{0:T(256)(128)(2,1)}, u32[]{:S(2)}) copy-start(bf16[64]{0:T(256)(128)(2,1)} %refs_4_.2) | copy-start | bytes 388
  0.7 1.2 %copy-start.11 = (bf16[64]{0:T(256)(128)(2,1)S(1)}, bf16[64]{0:T(256)(128)(2,1)}, u32[]{:S(2)}) copy-start(bf16[64]{0:T(256)(128)(2,1)} %refs_3_.2) | copy-start | bytes 388
  0.7 1.2 %copy-start.10 = (bf16[64]{0:T(256)(128)(2,1)S(1)}, bf16[64]{0:T(256)(128)(2,1)}, u32[]{:S(2)}) copy-start(bf16[64]{0:T(256)(128)(2,1)} %refs_2_.2) | copy-start | bytes 388
  0.7 1.2 %copy-start.9 = (bf16[64]{0:T(256)(128)(2,1)S(1)}, bf16[64]{0:T(256)(128)(2,1)}, u32[]{:S(2)}) copy-start(bf16[64]{0:T(256)(128)(2,1)} %refs_1_.2) | copy-start | bytes 388
  0.8 1.2 %copy-start.8 = (bf16[64]{0:T(256)(128)(2,1)S(1)}, bf16[64]{0:T(256)(128)(2,1)}, u32[]{:S(2)}) copy-start(bf16[64]{0:T(256)(128)(2,1)} %refs_0_.2) | copy-start | bytes 388
  0.8 1.2 %copy-start.7 = (s32[7,64]{1,0:T(8,128)S(1)}, s32[7,64]{1,0:T(8,128)}, u32[]{:S(2)}) copy-start(s32[7,64]{1,0:T(8,128)} %s_ref.1) | copy-start | bytes 5380
  2.1 14.7 %copy-start = (bf16[64,64]{1,0:T(8,128)(2,1)S(1)}, bf16[64,64]{1,0:T(8,128)(2,1)}, u32[]{:S(2)}) copy-start(bf16[64,64]{1,0:T(8,128)(2,1)} %wq_ref.1) | copy-start | bytes 24580
  2.1 14.7 %copy-start.1 = (bf16[64,64]{1,0:T(8,128)(2,1)S(1)}, bf16[64,64]{1,0:T(8,128)(2,1)}, u32[]{:S(2)}) copy-start(bf16[64,64]{1,0:T(8,128)(2,1)} %wk_ref.1) | copy-start | bytes 24580
  2.1 14.7 %copy-start.2 = (s32[7,2,128]{2,1,0:T(2,128)S(1)}, s32[7,2,128]{2,1,0:T(2,128)}, u32[]{:S(2)}) copy-start(s32[7,2,128]{2,1,0:T(2,128)} %idx_ref.3) | copy-start | bytes 21508
  2.1 14.7 %copy-start.3 = (bf16[64,64]{1,0:T(8,128)(2,1)S(1)}, bf16[64,64]{1,0:T(8,128)(2,1)}, u32[]{:S(2)}) copy-start(bf16[64,64]{1,0:T(8,128)(2,1)} %refs_2_.3) | copy-start | bytes 24580
  2.1 14.7 %copy-start.4 = (bf16[64,64]{1,0:T(8,128)(2,1)S(1)}, bf16[64,64]{1,0:T(8,128)(2,1)}, u32[]{:S(2)}) copy-start(bf16[64,64]{1,0:T(8,128)(2,1)} %refs_3_.3) | copy-start | bytes 24580
  2.1 14.7 %copy-start.5 = (bf16[64,128]{1,0:T(8,128)(2,1)S(1)}, bf16[64,128]{1,0:T(8,128)(2,1)}, u32[]{:S(2)}) copy-start(bf16[64,128]{1,0:T(8,128)(2,1)} %refs_4_.3) | copy-start | bytes 49156
  2.2 14.7 %copy-start.6 = (bf16[128,64]{0,1:T(8,128)(2,1)S(1)}, bf16[128,64]{0,1:T(8,128)(2,1)}, u32[]{:S(2)}) copy-start(bf16[128,64]{0,1:T(8,128)(2,1)} %param.37) | copy-start | bytes 49156
  16.9 1.3 %collective-permute-start = (f32[136,128]{1,0:T(8,128)S(1)}, f32[136,128]{1,0:T(8,128)S(1)}, u32[]{:S(2)}, u32[]{:S(2)}) collective-permute-start(f32[136,128]{1,0:T(8,128)S(1)} %get-tuple-element.58), channel_id=1, source_target_pairs={{0,8},{8,0},{16,24},{24,16},{1,9},{9,1},{17,25},{25,17},{2,10},{10... | collective-permute-start | bytes 208904 | tf_op jit(solution)/shard_map/ppermute | solution.py:662
  39.2 3.7 %collective-permute-start.3 = (bf16[136,128]{1,0:T(8,128)(2,1)S(1)}, bf16[136,128]{1,0:T(8,128)(2,1)S(1)}, u32[]{:S(2)}, u32[]{:S(2)}) collective-permute-start(bf16[136,128]{1,0:T(8,128)(2,1)S(1)} %shard_map.335.refs_0_), channel_id=1, source_target_pairs={{0,24},{8,16},{16,8},{24,0},{1,25},{9,17},{17,9},{25,1},{2,26},{10... | collective-permute-start | bytes 104456 | tf_op jit(solution)/shard_map/ppermute | solution.py:674
  39.3 4.1 %collective-permute-start.2 = (bf16[136,128]{1,0:T(8,128)(2,1)S(1)}, bf16[136,128]{1,0:T(8,128)(2,1)S(1)}, u32[]{:S(2)}, u32[]{:S(2)}) collective-permute-start(bf16[136,128]{1,0:T(8,128)(2,1)S(1)} %shard_map.335.refs_0_), channel_id=1, source_target_pairs={{0,16},{8,24},{16,0},{24,8},{1,17},{9,25},{17,1},{25,9},{2,18},{10... | collective-permute-start | bytes 104456 | tf_op jit(solution)/shard_map/ppermute | solution.py:674
  40.8 2.5 %collective-permute-start.1 = (bf16[136,128]{1,0:T(8,128)(2,1)S(1)}, bf16[136,128]{1,0:T(8,128)(2,1)S(1)}, u32[]{:S(2)}, u32[]{:S(2)}) collective-permute-start(bf16[136,128]{1,0:T(8,128)(2,1)S(1)} %shard_map.335.refs_0_), channel_id=1, source_target_pairs={{0,8},{8,0},{16,24},{24,16},{1,9},{9,1},{17,25},{25,17},{2,10},{10... | collective-permute-start | bytes 104456 | tf_op jit(solution)/shard_map/ppermute | solution.py:674
